TPU v7x, 128 devices: a whole 4x4x4 slice. The times are simulated.
128 devices in a mesh: pipe: 8 (over y, core), cross: 16 (over x, z).
Axes of the slice: x: 4, y: 4, z: 4, core: 2. Of those that a mesh axis runs over, the one named last changes fastest.
Arguments:
- pops_first: float32 [19, 128, 128, 128], P(None, 'pipe', 'cross'), may hold values from 0.02 to 0.1
- pops_second: float32 [19, 128, 128, 128], P(None, 'pipe', 'cross'), may hold values from 0.02 to 0.1
- phase_first: float32 [128, 128, 128], P('pipe', 'cross'), may hold values from -1 to 1
- phase_second: float32 [128, 128, 128], P('pipe', 'cross'), may hold values from -1 to 1
- adjoint_last: float32 [19, 128, 128, 128], P(None, 'pipe', 'cross'), may hold values from -6 to 6
- wettability: float32 [4096], replicated, may hold values from -0.8 to 0.8
- fluid: int32 [128, 128, 128], P('pipe', 'cross'), may hold values from 0 to 1, as said below
- wall: int32 [128, 128, 128], P('pipe', 'cross'), may hold values from 0 to 1, as said below
- patch: int32 [128, 128, 128], P('pipe', 'cross'), may hold values from 0 to 4095, as said below
Outputs:
- adjoint_first: float32 [19, 128, 128, 128], P(None, 'pipe', 'cross')
- wettability_gradient: float32 [4096], replicated
Inputs may be any that keep to these rules, and one draw needn't show every extreme that they name: 1 marks fluid nodes; every node with the first or last index along the second or the third dimension is solid. `wall`: 1 exactly on solid nodes that have a fluid node at one of the 18 lattice offsets, indices modulo the grid. `patch`: read only where wall is 1.
All inputs are finite; a program needn't handle non-finite values.
Results may differ from a plain program's by a relative error of at most 0.0001.
Values sent between devices are 32-bit elements; how exact they have to be, the bound alone decides.
No kernel may reach another device: no remote copies, remote signals or barrier semaphores. Data moves between devices by JAX's collectives and lax.ppermute only.
A program may use at most 64 MiB of HBM per device.

v0:
```python
import jax
import jax.numpy as jnp
from jax import lax
from jax.sharding import PartitionSpec as P

lattice_vel = (
    (0, 0, 0),
    (1, 0, 0),
    (-1, 0, 0),
    (0, 1, 0),
    (0, -1, 0),
    (0, 0, 1),
    (0, 0, -1),
    (1, 1, 0),
    (-1, -1, 0),
    (1, -1, 0),
    (-1, 1, 0),
    (1, 0, 1),
    (-1, 0, -1),
    (1, 0, -1),
    (-1, 0, 1),
    (0, 1, 1),
    (0, -1, -1),
    (0, 1, -1),
    (0, -1, 1),
)
lattice_wts = (1.0 / 3.0,) + (1.0 / 18.0,) * 6 + (1.0 / 36.0,) * 12
opposite = (0, 2, 1, 4, 3, 6, 5, 8, 7, 10, 9, 12, 11, 14, 13, 16, 15, 18, 17)
strength = 2.0
relax_heavy = 1.0
relax_light = 0.7


def with_halo(block, sides, width):
    for axis, dim in sides:
        count = lax.axis_size(axis)
        forward = [(i, i + 1) for i in range(count - 1)]
        forward.append((count - 1, 0))
        backward = [(target, source) for source, target in forward]
        low = lax.ppermute(
            lax.slice_in_dim(block, block.shape[dim] - width, None, axis=dim), axis, forward
        )
        high = lax.ppermute(lax.slice_in_dim(block, 0, width, axis=dim), axis, backward)
        block = jnp.concatenate([low, block, high], axis=dim)
    return block


def collide(pops, grad, omega):
    vel = jnp.asarray(lattice_vel, dtype=jnp.float32)
    wts = jnp.asarray(lattice_wts, dtype=jnp.float32).reshape(19, 1, 1, 1)
    density = jnp.sum(pops, axis=0)
    momentum = jnp.einsum("id,ixyz->dxyz", vel, pops, precision=lax.Precision.HIGHEST)
    speed = momentum / density
    along = jnp.einsum("id,dxyz->ixyz", vel, speed, precision=lax.Precision.HIGHEST)
    usq = jnp.sum(speed * speed, axis=0)
    equil = wts * density * (1.0 + 3.0 * along + 4.5 * along * along - 1.5 * usq)
    normal = jnp.einsum("id,dxyz->ixyz", vel, grad, precision=lax.Precision.HIGHEST)
    nsq = jnp.sum(grad * grad, axis=0)
    extra = strength * wts * (normal * normal - nsq / 3.0) / jnp.sqrt(1.0 + nsq)
    return pops - omega * (pops - equil) + extra


def offset_view(padded, move):
    cx_len = padded.shape[-3] - 2
    cy_len = padded.shape[-2] - 2
    piece = padded[..., 1 + move[0] : 1 + move[0] + cx_len, 1 + move[1] : 1 + move[1] + cy_len, :]
    return jnp.roll(piece, -move[2], axis=-1)


def color_gradient(padded):
    inner = padded[1:-1, 1:-1, :]
    total = [jnp.zeros_like(inner), jnp.zeros_like(inner), jnp.zeros_like(inner)]
    for i in range(1, 19):
        moved = offset_view(padded, lattice_vel[i])
        for d in range(3):
            if lattice_vel[i][d] != 0:
                total[d] = total[d] + 3.0 * lattice_wts[i] * lattice_vel[i][d] * moved
    return jnp.stack(total)


def gradient_back(padded_dn):
    result = jnp.zeros_like(padded_dn[0, 1:-1, 1:-1, :])
    for i in range(1, 19):
        move = lattice_vel[i]
        proj = move[0] * padded_dn[0] + move[1] * padded_dn[1] + move[2] * padded_dn[2]
        result = result + 3.0 * lattice_wts[i] * offset_view(proj, (-move[0], -move[1], -move[2]))
    return result


def full_view(adjoint):
    padded = with_halo(adjoint, (("pipe", 1), ("cross", 2)), 1)
    return [offset_view(padded[i], lattice_vel[i]) for i in range(19)]


def propagate_back(adjoint, viewed, fluid_w, fluid_pad):
    rows = []
    for i in range(19):
        ahead = offset_view(fluid_pad, lattice_vel[i])
        rows.append(fluid_w * (ahead * viewed[i] + (1.0 - ahead) * adjoint[opposite[i]]))
    return jnp.stack(rows)


def local_patches(dphi, wall_w, patch, count):
    return jax.ops.segment_sum((dphi * wall_w).reshape(-1), patch.reshape(-1), num_segments=count)


def step_terms(dgrad, wall_w, patch, count):
    padded_dn = with_halo(dgrad, (("pipe", 1), ("cross", 2)), 1)
    local = local_patches(gradient_back(padded_dn), wall_w, patch, count)
    return lax.psum(local, ("pipe", "cross"))


def shards(
    pops_first,
    pops_second,
    phase_first,
    phase_second,
    adjoint_last,
    wettability,
    fluid,
    wall,
    patch,
):
    count = wettability.shape[0]
    fluid_w = fluid.astype(jnp.float32)
    wall_w = wall.astype(jnp.float32)
    contact = wall_w * wettability[patch]
    fields = jnp.stack([fluid_w * phase_second + contact, fluid_w * phase_first + contact, fluid_w])
    padded = with_halo(fields, (("pipe", 1), ("cross", 2)), 1)
    fluid_pad = padded[2]
    adjoint = adjoint_last
    total = jnp.zeros((count,), jnp.float32)
    for pops, phase, level in ((pops_second, phase_second, 0), (pops_first, phase_first, 1)):
        grad = color_gradient(padded[level])
        omega = 1.0 / (relax_heavy * (1.0 + phase) * 0.5 + relax_light * (1.0 - phase) * 0.5)
        viewed = full_view(adjoint)
        post = propagate_back(adjoint, viewed, fluid_w, fluid_pad)
        _, pull = jax.vjp(lambda a, b: collide(a, b, omega), pops, grad)
        adjoint, dgrad = pull(post)
        total = total + step_terms(dgrad, wall_w, patch, count)
    return (adjoint, total)


def solution(mesh):
    return jax.shard_map(
        shards,
        mesh=mesh,
        in_specs=(
            P(None, "pipe", "cross", None),
            P(None, "pipe", "cross", None),
            P("pipe", "cross", None),
            P("pipe", "cross", None),
            P(None, "pipe", "cross", None),
            P(),
            P("pipe", "cross", None),
            P("pipe", "cross", None),
            P("pipe", "cross", None),
        ),
        out_specs=(P(None, "pipe", "cross", None), P()),
        check_vma=False,
    )
```

profile of v0, /device:TPU:1, one launch (start us, length us, event | category | flops | bytes accessed | tf_op | source)
XLA Modules:
  0.0 470.2 jit_solution(2119148171750985404)
XLA Ops:
  2.2 2.7 collective-permute-start.4
  6.7 90.5 %gather_fusion = f32[16384]{0:T(1024)S(1)} fusion(f32[4096]{0:T(1024)S(1)} %copy-done, s32[16384]{0:T(1024)S(1)} %fusion.51), kind=kCustom, calls=%fused_computation | custom fusion | bytes 196608 | tf_op jit(solution)/shard_map/gather | solution.py:127
  97.4 1.7 collective-permute-start.1
  99.9 3.0 multiply_reduce_fusion.3
  103.0 1.7 multiply_reduce_fusion.5
  104.7 2.6 fusion.305
  109.5 6.0 %collective-permute-start.3 = (f32[3,18,1,128]{3,2,1,0:T(1,128)S(1)}, f32[3,18,1,128]{3,2,1,0:T(1,128)S(1)}, u32[]{:S(2)}, u32[]{:S(2)}) collective-permute-start(f32[3,18,1,128]{3,2,1,0:T(1,128)S(1)} %get-tuple-element.124), channel_id=1, source_target_pairs={{1,0},{2,1},{3,2},{4,3},{5,4},{6,5},{7,6},{8,7},{9,8},{10,9},{11,1... | collective-permute-start | bytes 82952 | tf_op jit(solution)/shard_map/ppermute | solution.py:43
  116.7 5.4 %collective-permute-done.2 = f32[3,18,1,128]{3,2,1,0:T(1,128)S(1)} collective-permute-done((f32[3,18,1,128]{3,2,1,0:T(1,128)S(1)}, f32[3,18,1,128]{3,2,1,0:T(1,128)S(1)}, u32[]{:S(2)}, u32[]{:S(2)}) %collective-permute-start.2) | collective-permute-done | bytes 27680 | tf_op jit(solution)/shard_map/ppermute | solution.py:40
  142.9 2.6 fusion.44
  157.4 2.7 fusion.42
  164.6 2.6 collective-permute-done.7
  167.3 3.6 collective-permute-done.6
  177.6 1.8 multiply_reduce_fusion.4
  180.9 1.6 fusion.2
  182.6 3.1 collective-permute-start.13
  189.9 4.2 collective-permute-start.9
  196.9 3.0 collective-permute-start.11
  201.1 86.0 %scatter_custom_fusion = f32[4096]{0:T(1024)S(1)} fusion(s32[16384]{0:T(1024)} %bitcast.770, f32[16384]{0:T(1024)} %fusion.107, f32[]{:T(128)} %constant.9.clone.1), kind=kCustom, calls=%fused_computation.667 | custom fusion | flops 16384 | bytes 16896 | tf_op jit(solution)/shard_map/scatter-add | solution.py:104
  294.6 1.8 multiply_reduce_fusion.2
  299.7 4.0 collective-permute-start.17
  304.9 4.9 %collective-permute-start.19 = (f32[3,18,1,128]{3,2,1,0:T(1,128)S(1)}, f32[3,18,1,128]{3,2,1,0:T(1,128)S(1)}, u32[]{:S(2)}, u32[]{:S(2)}) collective-permute-start(f32[3,18,1,128]{3,2,1,0:T(1,128)S(1)} %get-tuple-element.120), channel_id=1, source_target_pairs={{1,0},{2,1},{3,2},{4,3},{5,4},{6,5},{7,6},{8,7},{9,8},{10,9},{11,1... | collective-permute-start | bytes 82952 | tf_op jit(solution)/shard_map/ppermute | solution.py:43
  311.5 4.7 collective-permute-done.18
  317.8 86.0 %scatter_custom_fusion.1 = f32[4096]{0:T(1024)S(1)} fusion(s32[16384]{0:T(1024)} %bitcast.771, f32[16384]{0:T(1024)S(1)} %fusion.63, f32[]{:T(128)} %constant.9.clone.1), kind=kCustom, calls=%fused_computation.665 | custom fusion | flops 16384 | bytes 16896 | tf_op jit(solution)/shard_map/scatter-add | solution.py:104
  403.9 66.1 %psum.16 = f32[4096]{0:T(1024)} all-reduce(f32[4096]{0:T(1024)S(1)} %add.945), channel_id=1, replica_groups=mesh['pipe'=8,'cross'=16] {'pipe','cross'}, use_global_device_ids=true, to_apply=%region_14.15 | all-reduce | flops 4096 | bytes 32768 | tf_op jit(solution)/shard_map/psum | solution.py:110
  (489 shorter events, 74.5 us)
Async XLA Ops:
  2.2 158.5 %collective-permute-start.4 = (f32[19,1,8,128]{3,2,1,0:T(8,128)}, f32[19,1,8,128]{3,2,1,0:T(8,128)}, u32[]{:S(2)}, u32[]{:S(2)}) collective-permute-start(f32[19,1,8,128]{3,2,1,0:T(8,128)} %get-tuple-element.83), channel_id=1, source_target_pairs={{0,16},{16,32},{32,48},{48,64},{64,80},{80,96},{96,112},{112,0},{1... | collective-permute-start | bytes 233480 | tf_op jit(solution)/shard_map/ppermute | solution.py:40
  4.9 156.8 %collective-permute-start.5 = (f32[19,1,8,128]{3,2,1,0:T(8,128)}, f32[19,1,8,128]{3,2,1,0:T(8,128)}, u32[]{:S(2)}, u32[]{:S(2)}) collective-permute-start(f32[19,1,8,128]{3,2,1,0:T(8,128)} %get-tuple-element.82), channel_id=1, source_target_pairs={{16,0},{32,16},{48,32},{64,48},{80,64},{96,80},{112,96},{0,112},{1... | collective-permute-start | bytes 233480 | tf_op jit(solution)/shard_map/ppermute | solution.py:43
  6.7 90.6 %copy-start.1 = (s32[16,8,128]{2,1,0:T(8,128)S(1)}, s32[16,8,128]{2,1,0:T(8,128)}, u32[]{:S(2)}) copy-start(s32[16,8,128]{2,1,0:T(8,128)} %param.19) | copy-start | bytes 196612
  6.7 90.6 %copy-start.8 = (s32[16,8,128]{2,1,0:T(8,128)S(1)}, s32[16,8,128]{2,1,0:T(8,128)}, u32[]{:S(2)}) copy-start(s32[16,8,128]{2,1,0:T(8,128)} %param.20) | copy-start | bytes 196612
  6.7 90.6 %copy-start.109 = (f32[16,8,128]{2,1,0:T(8,128)S(1)}, f32[16,8,128]{2,1,0:T(8,128)}, u32[]{:S(2)}) copy-start(f32[16,8,128]{2,1,0:T(8,128)} %param.16) | copy-start | bytes 196612
  6.7 92.5 %copy-start.6 = (f32[19,16,8,128]{3,2,1,0:T(8,128)S(1)}, f32[19,16,8,128]{3,2,1,0:T(8,128)}, u32[]{:S(2)}) copy-start(f32[19,16,8,128]{3,2,1,0:T(8,128)} %param.13) | copy-start | bytes 3735556
  97.4 12.1 %collective-permute-start.1 = (f32[3,1,8,128]{3,2,1,0:T(8,128)S(1)}, f32[3,1,8,128]{3,2,1,0:T(8,128)S(1)}, u32[]{:S(2)}, u32[]{:S(2)}) collective-permute-start(f32[3,1,8,128]{3,2,1,0:T(8,128)S(1)} %get-tuple-element.134), channel_id=1, source_target_pairs={{16,0},{32,16},{48,32},{64,48},{80,64},{96,80},{112,96},{0,112},{1... | collective-permute-start | bytes 36872 | tf_op jit(solution)/shard_map/ppermute | solution.py:43
  99.1 10.4 %collective-permute-start = (f32[3,1,8,128]{3,2,1,0:T(8,128)S(1)}, f32[3,1,8,128]{3,2,1,0:T(8,128)S(1)}, u32[]{:S(2)}, u32[]{:S(2)}) collective-permute-start(f32[3,1,8,128]{3,2,1,0:T(8,128)S(1)} %get-tuple-element.133), channel_id=1, source_target_pairs={{0,16},{16,32},{32,48},{48,64},{64,80},{80,96},{96,112},{112,0},{1... | collective-permute-start | bytes 36872 | tf_op jit(solution)/shard_map/ppermute | solution.py:40
  109.5 7.2 %collective-permute-start.3 = (f32[3,18,1,128]{3,2,1,0:T(1,128)S(1)}, f32[3,18,1,128]{3,2,1,0:T(1,128)S(1)}, u32[]{:S(2)}, u32[]{:S(2)}) collective-permute-start(f32[3,18,1,128]{3,2,1,0:T(1,128)S(1)} %get-tuple-element.124), channel_id=1, source_target_pairs={{1,0},{2,1},{3,2},{4,3},{5,4},{6,5},{7,6},{8,7},{9,8},{10,9},{11,1... | collective-permute-start | bytes 82952 | tf_op jit(solution)/shard_map/ppermute | solution.py:43
  115.5 6.5 %collective-permute-start.2 = (f32[3,18,1,128]{3,2,1,0:T(1,128)S(1)}, f32[3,18,1,128]{3,2,1,0:T(1,128)S(1)}, u32[]{:S(2)}, u32[]{:S(2)}) collective-permute-start(f32[3,18,1,128]{3,2,1,0:T(1,128)S(1)} %get-tuple-element.123), channel_id=1, source_target_pairs={{0,1},{1,2},{2,3},{3,4},{4,5},{5,6},{6,7},{7,8},{8,9},{9,10},{10,1... | collective-permute-start | bytes 82952 | tf_op jit(solution)/shard_map/ppermute | solution.py:40
  162.9 4.4 collective-permute-start.7
  163.0 7.9 %collective-permute-start.6 = (f32[19,18,1,128]{3,2,1,0:T(1,128)S(1)}, f32[19,18,1,128]{3,2,1,0:T(1,128)S(1)}, u32[]{:S(2)}, u32[]{:S(2)}) collective-permute-start(f32[19,18,1,128]{3,2,1,0:T(1,128)S(1)} %get-tuple-element.78), channel_id=1, source_target_pairs={{0,1},{1,2},{2,3},{3,4},{4,5},{5,6},{6,7},{7,8},{8,9},{9,10},{10,1... | collective-permute-start | bytes 525320 | tf_op jit(solution)/shard_map/ppermute | solution.py:40
  182.6 5.7 %collective-permute-start.13 = (f32[3,1,8,128]{3,2,1,0:T(8,128)S(1)}, f32[3,1,8,128]{3,2,1,0:T(8,128)S(1)}, u32[]{:S(2)}, u32[]{:S(2)}) collective-permute-start(f32[3,1,8,128]{3,2,1,0:T(8,128)S(1)} %get-tuple-element.128), channel_id=1, source_target_pairs={{16,0},{32,16},{48,32},{64,48},{80,64},{96,80},{112,96},{0,112},{1... | collective-permute-start | bytes 36872 | tf_op jit(solution)/shard_map/ppermute | solution.py:43
  185.7 2.6 collective-permute-start.12
  188.3 5.8 %collective-permute-start.15 = (f32[3,18,1,128]{3,2,1,0:T(1,128)S(1)}, f32[3,18,1,128]{3,2,1,0:T(1,128)S(1)}, u32[]{:S(2)}, u32[]{:S(2)}) collective-permute-start(f32[3,18,1,128]{3,2,1,0:T(1,128)S(1)} %get-tuple-element.122), channel_id=1, source_target_pairs={{1,0},{2,1},{3,2},{4,3},{5,4},{6,5},{7,6},{8,7},{9,8},{10,9},{11,1... | collective-permute-start | bytes 82952 | tf_op jit(solution)/shard_map/ppermute | solution.py:43
  188.4 6.1 %collective-permute-start.14 = (f32[3,18,1,128]{3,2,1,0:T(1,128)S(1)}, f32[3,18,1,128]{3,2,1,0:T(1,128)S(1)}, u32[]{:S(2)}, u32[]{:S(2)}) collective-permute-start(f32[3,18,1,128]{3,2,1,0:T(1,128)S(1)} %get-tuple-element.121), channel_id=1, source_target_pairs={{0,1},{1,2},{2,3},{3,4},{4,5},{5,6},{6,7},{7,8},{8,9},{9,10},{10,1... | collective-permute-start | bytes 82952 | tf_op jit(solution)/shard_map/ppermute | solution.py:40
  189.9 6.0 %collective-permute-start.9 = (f32[19,1,8,128]{3,2,1,0:T(8,128)S(1)}, f32[19,1,8,128]{3,2,1,0:T(8,128)S(1)}, u32[]{:S(2)}, u32[]{:S(2)}) collective-permute-start(f32[19,1,8,128]{3,2,1,0:T(8,128)S(1)} %get-tuple-element.81), channel_id=1, source_target_pairs={{16,0},{32,16},{48,32},{64,48},{80,64},{96,80},{112,96},{0,112},{1... | collective-permute-start | bytes 233480 | tf_op jit(solution)/shard_map/ppermute | solution.py:43
  194.1 1.8 collective-permute-start.8
  196.9 90.2 %collective-permute-start.11 = (f32[19,18,1,128]{3,2,1,0:T(1,128)}, f32[19,18,1,128]{3,2,1,0:T(1,128)}, u32[]{:S(2)}, u32[]{:S(2)}) collective-permute-start(f32[19,18,1,128]{3,2,1,0:T(1,128)} %get-tuple-element.77), channel_id=1, source_target_pairs={{1,0},{2,1},{3,2},{4,3},{5,4},{6,5},{7,6},{8,7},{9,8},{10,9},{11,1... | collective-permute-start | bytes 525320 | tf_op jit(solution)/shard_map/ppermute | solution.py:43
  199.9 87.2 %collective-permute-start.10 = (f32[19,18,1,128]{3,2,1,0:T(1,128)}, f32[19,18,1,128]{3,2,1,0:T(1,128)}, u32[]{:S(2)}, u32[]{:S(2)}) collective-permute-start(f32[19,18,1,128]{3,2,1,0:T(1,128)} %get-tuple-element.76), channel_id=1, source_target_pairs={{0,1},{1,2},{2,3},{3,4},{4,5},{5,6},{6,7},{7,8},{8,9},{9,10},{10,1... | collective-permute-start | bytes 525320 | tf_op jit(solution)/shard_map/ppermute | solution.py:40
  299.7 4.8 %collective-permute-start.17 = (f32[3,1,8,128]{3,2,1,0:T(8,128)S(1)}, f32[3,1,8,128]{3,2,1,0:T(8,128)S(1)}, u32[]{:S(2)}, u32[]{:S(2)}) collective-permute-start(f32[3,1,8,128]{3,2,1,0:T(8,128)S(1)} %get-tuple-element.126), channel_id=1, source_target_pairs={{16,0},{32,16},{48,32},{64,48},{80,64},{96,80},{112,96},{0,112},{1... | collective-permute-start | bytes 36872 | tf_op jit(solution)/shard_map/ppermute | solution.py:43
  303.7 1.2 collective-permute-start.16
  304.9 6.6 %collective-permute-start.19 = (f32[3,18,1,128]{3,2,1,0:T(1,128)S(1)}, f32[3,18,1,128]{3,2,1,0:T(1,128)S(1)}, u32[]{:S(2)}, u32[]{:S(2)}) collective-permute-start(f32[3,18,1,128]{3,2,1,0:T(1,128)S(1)} %get-tuple-element.120), channel_id=1, source_target_pairs={{1,0},{2,1},{3,2},{4,3},{5,4},{6,5},{7,6},{8,7},{9,8},{10,9},{11,1... | collective-permute-start | bytes 82952 | tf_op jit(solution)/shard_map/ppermute | solution.py:43
  309.9 6.3 %collective-permute-start.18 = (f32[3,18,1,128]{3,2,1,0:T(1,128)S(1)}, f32[3,18,1,128]{3,2,1,0:T(1,128)S(1)}, u32[]{:S(2)}, u32[]{:S(2)}) collective-permute-start(f32[3,18,1,128]{3,2,1,0:T(1,128)S(1)} %get-tuple-element.119), channel_id=1, source_target_pairs={{0,1},{1,2},{2,3},{3,4},{4,5},{5,6},{6,7},{7,8},{8,9},{9,10},{10,1... | collective-permute-start | bytes 82952 | tf_op jit(solution)/shard_map/ppermute | solution.py:40
  (112 other events, 341.1 us)
where the time goes:
time: 477 us; the launch traced here: 470 us
  other arithmetic  195 us (41%)
  local copies, waits for them, and re-layouts  128 us (27%)
  blocking collectives  66.1 us (14%)
  starting transfers between devices  35.1 us (7%)
  matrix products  23.9 us (5%)
  waiting for transfers between devices  18.9 us (4%)
    scatter-add x2, other arithmetic, local_patches(): jax.ops.segment_sum((dphi * wall_w).reshape(-1), patch.reshape(-1), num_s...  172 us
    gather x1, local copies, waits for them, and re-layouts, shards(): contact = wall_w * wettability[patch]  90.5 us
    psum x1, blocking collectives, step_terms(): return lax.psum(local, ('pipe', 'cross'))  66.1 us
    ppermute x10, starting transfers between devices, with_halo(): lax.ppermute(lax.slice_in_dim(block, 0, width, axis=dim), axis, backward)  27.2 us
    concatenate x20, local copies, waits for them, and re-layouts, offset_view(): return jnp.roll(piece, -move[2], axis=-1)  15.2 us
    ppermute x10, waiting for transfers between devices, with_halo(): lax.ppermute(lax.slice_in_dim(block, block.shape[dim] - width, None, axis...  14.4 us
    slice x106, local copies, waits for them, and re-layouts, offset_view(): return jnp.roll(piece, -move[2], axis=-1)  14.3 us
  transfers between devices with their start and end apart: 20, of which 8 were waited for; matrix products, arithmetic and copies ran while one was open for 49% of the time, Pallas kernels for 0%

commit v1 on v0

v1 whole, which is shorter than its diff:
```python
import functools

import jax
import jax.numpy as jnp
from jax import lax
from jax.experimental import pallas as pl
from jax.experimental.pallas import tpu as pltpu
from jax.sharding import PartitionSpec as P

lattice_vel = (
    (0, 0, 0),
    (1, 0, 0),
    (-1, 0, 0),
    (0, 1, 0),
    (0, -1, 0),
    (0, 0, 1),
    (0, 0, -1),
    (1, 1, 0),
    (-1, -1, 0),
    (1, -1, 0),
    (-1, 1, 0),
    (1, 0, 1),
    (-1, 0, -1),
    (1, 0, -1),
    (-1, 0, 1),
    (0, 1, 1),
    (0, -1, -1),
    (0, 1, -1),
    (0, -1, 1),
)
opposite = (0, 2, 1, 4, 3, 6, 5, 8, 7, 10, 9, 12, 11, 14, 13, 16, 15, 18, 17)
relax_heavy = 1.0
relax_light = 0.7

x_plus = (1, 7, 9, 11, 13)
x_minus = (2, 8, 10, 12, 14)
y_plus = (3, 7, 10, 15, 17)
y_minus = (4, 8, 9, 16, 18)

NX = 16
NY = 8
NZ = 128
WX = NX + 2
LOW = 8
ROWS = 24
FIELDS = 5
f32 = jnp.float32


def tile(ref, lead, x, move):
    index = lead + (x + 1 + move[0], pl.ds(LOW + move[1], NY), slice(None))
    value = ref[index]
    if move[2]:
        value = pltpu.roll(value, (-move[2]) % NZ, 1)
    return value


def look_up(table, index):
    high = lax.shift_right_logical(index, 7)
    low = index & 127
    result = jnp.zeros(index.shape, f32)
    for r in range(32):
        row = jnp.broadcast_to(table[pl.ds(r, 1), :], index.shape)
        picked = jnp.take_along_axis(row, low, axis=1, mode="promise_in_bounds")
        result = jnp.where(high == r, picked, result)
    return result


def roll_z(value, step):
    return pltpu.roll(value, (-step) % NZ, 1)


def gradient(view):
    sixth, twelfth = 1.0 / 6.0, 1.0 / 12.0
    east, west, north, south = view(1, 0), view(-1, 0), view(0, 1), view(0, -1)
    dx, dy = east - west, north - south
    xy = view(1, 1) - view(-1, -1)
    xmy = view(1, -1) - view(-1, 1)
    along = sixth * view(0, 0) + twelfth * (east + west + north + south)
    gx = sixth * dx + twelfth * (xy + xmy + roll_z(dx, 1) + roll_z(dx, -1))
    gy = sixth * dy + twelfth * (xy - xmy + roll_z(dy, 1) + roll_z(dy, -1))
    return gx, gy, roll_z(along, 1) - roll_z(along, -1)


def moments(q):
    a, b = 1.0 / 18.0, 1.0 / 36.0

    def pair(i):
        return q[i] + q[i + 1], q[i] - q[i + 1]

    (sx, dx), (sy, dy), (sz, dz) = pair(1), pair(3), pair(5)
    (s7, d7), (s9, d9), (s11, d11) = pair(7), pair(9), pair(11)
    (s13, d13), (s15, d15), (s17, d17) = pair(13), pair(15), pair(17)
    xy, xz, yz = s7 + s9, s11 + s13, s15 + s17
    m0 = (1.0 / 3.0) * q[0] + a * (sx + sy + sz) + b * (xy + xz + yz)
    mx = a * dx + b * (d7 + d9 + d11 + d13)
    my = a * dy + b * (d7 - d9 + d15 + d17)
    mz = a * dz + b * (d11 - d13 + d15 - d17)
    mxx = a * sx + b * (xy + xz)
    myy = a * sy + b * (xy + yz)
    mzz = a * sz + b * (xz + yz)
    return m0, (mx, my, mz), (mxx, myy, mzz, b * (s7 - s9), b * (s11 - s13), b * (s15 - s17))


def velocity(f):
    density = f[0]
    for i in range(1, 19):
        density = density + f[i]
    d = {i: f[i] - f[i + 1] for i in range(1, 19, 2)}
    inv = 1.0 / density
    ux = (d[1] + d[7] + d[9] + d[11] + d[13]) * inv
    uy = (d[3] + d[7] - d[9] + d[15] + d[17]) * inv
    uz = (d[5] + d[11] - d[13] + d[15] - d[17]) * inv
    return ux, uy, uz


def apply_second(second, v):
    mxx, myy, mzz, mxy, mxz, myz = second
    x, y, z = v
    return (
        mxx * x + mxy * y + mxz * z,
        mxy * x + myy * y + myz * z,
        mxz * x + myz * y + mzz * z,
    )


def dot3(a, b):
    return a[0] * b[0] + a[1] * b[1] + a[2] * b[2]


def collide_back(post, q, f, phase, store):
    q0, q1, q2 = q
    u = velocity(f)
    omega = 1.0 / (relax_heavy * (1.0 + phase) * 0.5 + relax_light * (1.0 - phase) * 0.5)
    q2u = apply_second(q2, u)
    along = q0 - 4.5 * dot3(u, q2u) + 1.5 * dot3(u, u) * q0
    base = omega * along
    bx, by, bz = [omega * (3.0 * q1[d] + 9.0 * q2u[d] - 3.0 * u[d] * q0) for d in range(3)]
    keep = 1.0 - omega
    store(0, keep * post[0] + base)
    slopes = (bx, by, bz, bx + by, bx - by, bx + bz, bx - bz, by + bz, by - bz)
    for k, slope in enumerate(slopes):
        i = 1 + 2 * k
        store(i, keep * post[i] + (base + slope))
        store(i + 1, keep * post[i + 1] + (base - slope))


def gradient_back(q0, q2, n):
    nsq = dot3(n, n)
    root = 1.0 / jnp.sqrt(1.0 + nsq)
    q2n = apply_second(q2, n)
    energy = dot3(n, q2n) - (1.0 / 3.0) * nsq * q0
    third = (4.0 / 3.0) * q0
    tail = 2.0 * energy * root * root * root
    return [root * (4.0 * q2n[d] - third * n[d]) - tail * n[d] for d in range(3)]


def gradient_adjoint(view):
    sixth, twelfth = 1.0 / 6.0, 1.0 / 12.0
    xe, xw, yn, ys = view(0, 1, 0), view(0, -1, 0), view(1, 0, 1), view(1, 0, -1)
    zc = sixth * view(2, 0, 0)
    around = view(2, 1, 0) + view(2, -1, 0) + view(2, 0, 1) + view(2, 0, -1)
    across = xe - xw + yn - ys
    flat = sixth * across + twelfth * (
        view(0, 1, 1) + view(1, 1, 1) - view(0, -1, -1) - view(1, -1, -1)
        + view(0, 1, -1) - view(1, 1, -1) - view(0, -1, 1) + view(1, -1, 1)
    )
    ahead = zc + twelfth * (across + around)
    behind = twelfth * (across - around) - zc
    return -(flat + roll_z(ahead, 1) + roll_z(behind, -1))


def side_adjoint(rows, sign):
    sixth, twelfth = 1.0 / 6.0, 1.0 / 12.0
    gx, gy, gz = [lambda move, d=d: rows[d, pl.ds(1 + move, WX), :] for d in range(3)]
    flat = sixth * sign * gy(0) + twelfth * (sign * (gy(1) + gy(-1)) + gx(1) - gx(-1))
    return -(flat + twelfth * (roll_z(sign * gy(0) + gz(0), 1) + roll_z(sign * gy(0) - gz(0), -1)))


def whole_call(kernel, name, out_shape, args, scratch=(), aliases=None, in_hbm=False):
    options = {}
    if in_hbm:
        options["in_specs"] = [pl.BlockSpec(memory_space=pl.ANY)] * len(args)
    else:
        options["compiler_params"] = pltpu.CompilerParams(vmem_limit_bytes=24 * 1024 * 1024)
    return pl.pallas_call(
        kernel,
        out_shape=[jax.ShapeDtypeStruct(shape, kind) for shape, kind in out_shape],
        scratch_shapes=scratch,
        input_output_aliases=aliases or {},
        name=name,
        **options,
    )(*args)


def take_rows(out, slot, flat, start):
    out[pl.ds(slot * NX, NX), :] = flat[pl.ds(start, NX, stride=NY), :].astype(f32)


def pack_kernel(adj_hbm, *refs):
    hbm, (x_up, x_down, y_up, y_down), (adj, *fields) = refs[:FIELDS], refs[FIELDS : FIELDS + 4], refs[FIELDS + 4 : -1]
    sem = refs[-1]
    copies = [pltpu.make_async_copy(adj_hbm, adj, sem.at[0])]
    for k in range(FIELDS):
        copies.append(pltpu.make_async_copy(hbm[k], fields[k], sem.at[k + 1]))
    for copy in copies:
        copy.start()
    for copy in copies:
        copy.wait()
    flat = adj.reshape(19 * NX * NY, NZ)
    for k in range(5):
        x_up[k] = adj[x_plus[k], 0]
        x_down[k] = adj[x_minus[k], NX - 1]
        take_rows(y_up, k, flat, y_plus[k] * NX * NY)
        take_rows(y_down, k, flat, y_minus[k] * NX * NY + NY - 1)
    for k in range(FIELDS):
        x_up[5 + k] = fields[k][0].astype(f32)
        x_down[5 + k] = fields[k][NX - 1].astype(f32)
        rows = fields[k].reshape(NX * NY, NZ)
        take_rows(y_up, 5 + k, rows, 0)
        take_rows(y_down, 5 + k, rows, NY - 1)


def pack(adjoint, fields):
    face, side = ((5 + FIELDS, NY, NZ), f32), (((5 + FIELDS) * NX, NZ), f32)
    scratch = [pltpu.VMEM((19, NX, NY, NZ), f32)]
    scratch += [pltpu.VMEM((NX, NY, NZ), field.dtype) for field in fields]
    scratch.append(pltpu.SemaphoreType.DMA((1 + FIELDS,)))
    return whole_call(pack_kernel, "pack", [face, face, side, side], (adjoint, *fields), scratch, in_hbm=True)


edge_up = (10, 7)
edge_down = (8, 9)


def pack_edges_kernel(count, low, high, _, up, down):
    for out, pops, row in ((up, edge_up, 0), (down, edge_down, NY - 1)):
        out[pl.ds(0, 1), :] = low[x_minus.index(pops[0]), pl.ds(row, 1), :]
        out[pl.ds(1, 1), :] = high[x_plus.index(pops[1]), pl.ds(row, 1), :]
        for k in range(count):
            out[pl.ds(2 + k, 1), :] = low[5 + k, pl.ds(row, 1), :]
            out[pl.ds(2 + count + k, 1), :] = high[5 + k, pl.ds(row, 1), :]
        used = 2 + 2 * count
        size = out.shape[0]
        out[pl.ds(used, size - used), :] = jnp.zeros((size - used, NZ), f32)


def pack_edges(low, high, count, after):
    out = ((16 if count else 8, NZ), f32)
    kernel = functools.partial(pack_edges_kernel, count)
    return whole_call(kernel, "pack_edges", [out, out], (low, high, after))


def fill_sides(pad, lead, y_low, low_slot, y_high, high_slot):
    for x in range(NX):
        pad[lead + (x + 1, pl.ds(LOW - 1, 1), slice(None))] = y_low[pl.ds(low_slot * NX + x, 1), :]
        pad[lead + (x + 1, pl.ds(LOW + NY, 1), slice(None))] = y_high[pl.ds(high_slot * NX + x, 1), :]


def fill_pops(pad, adj, planes, y_low, y_high):
    for p in range(19):
        for x in planes:
            pad[p, x + 1, pl.ds(LOW, NY), :] = adj[p, x]
    for k in range(5):
        for x in planes:
            pad[y_minus[k], x + 1, pl.ds(LOW - 1, 1), :] = y_low[pl.ds(k * NX + x, 1), :]
            pad[y_plus[k], x + 1, pl.ds(LOW + NY, 1), :] = y_high[pl.ds(k * NX + x, 1), :]


def fill_pops_outer(pad, x_low, x_high, e_low, e_high):
    for k in range(5):
        pad[x_minus[k], 0, pl.ds(LOW, NY), :] = x_low[k]
        pad[x_plus[k], WX - 1, pl.ds(LOW, NY), :] = x_high[k]
    for row, pops, edge in ((LOW + NY, edge_up, e_high), (LOW - 1, edge_down, e_low)):
        pad[pops[0], 0, pl.ds(row, 1), :] = edge[pl.ds(0, 1), :]
        pad[pops[1], WX - 1, pl.ds(row, 1), :] = edge[pl.ds(1, 1), :]


def fill_field(pad, lead, own, slot, y_low, y_high):
    for x in range(NX):
        pad[lead + (x + 1, pl.ds(LOW, NY), slice(None))] = own[x].astype(f32)
    fill_sides(pad, lead, y_low, 5 + slot, y_high, 5 + slot)


def fill_field_outer(pad, lead, slot, x_low, x_high, e_low, e_high):
    pad[lead + (0, pl.ds(LOW, NY), slice(None))] = x_low[5 + slot]
    pad[lead + (WX - 1, pl.ds(LOW, NY), slice(None))] = x_high[5 + slot]
    for row, edge in ((LOW + NY, e_high), (LOW - 1, e_low)):
        pad[lead + (0, pl.ds(row, 1), slice(None))] = edge[pl.ds(2 + slot, 1), :]
        pad[lead + (WX - 1, pl.ds(row, 1), slice(None))] = edge[pl.ds(2 + FIELDS + slot, 1), :]


def propagate_back(adj_pad, fluid_pad, x):
    here = tile(fluid_pad, (), x, (0, 0, 0))
    post = [here * adj_pad[0, x + 1, pl.ds(LOW, NY), :]]
    for i in range(1, 19):
        ahead = tile(fluid_pad, (), x, lattice_vel[i])
        moved = tile(adj_pad, (i,), x, lattice_vel[i])
        back = adj_pad[opposite[i], x + 1, pl.ds(LOW, NY), :]
        post.append(here * jnp.where(ahead != 0.0, moved, back))
    return post


def step_plane(x, adj_pad, fluid_pad, pops, phase, adj_out, mom_out):
    post = propagate_back(adj_pad, fluid_pad, x)
    q = moments(post)

    def store(i, value):
        adj_out[i, x] = value

    collide_back(post, q, [pops[i, x] for i in range(19)], phase[x], store)
    if mom_out is not None:
        mom_out[0, x] = q[0]
        for k in range(6):
            mom_out[1 + k, x] = q[2][k]


inner = range(1, NX - 1)


def second_inner_kernel(pops, phase, adj, fluid, y_low, y_high, adj_out, mom_out, adj_pad, fluid_pad):
    fill_field(fluid_pad, (), fluid, 2, y_low, y_high)
    fill_pops(adj_pad, adj, range(NX), y_low, y_high)

    def plane(x, carry):
        step_plane(x, adj_pad, fluid_pad, pops, phase, adj_out, mom_out)
        return carry

    lax.fori_loop(1, NX - 1, plane, 0)


block = ((19, NX, NY, NZ), f32)
seven = ((7, NX, NY, NZ), f32)
vector = ((3, NX, NY, NZ), f32)


def pad_scratch():
    return [pltpu.VMEM((19, WX, ROWS, NZ), f32), pltpu.VMEM((WX, ROWS, NZ), f32)]


def second_outer_kernel(
    pops, phase, adj, fluid, y_low, y_high, x_low, x_high, e_low, e_high, adj_in, mom_in,
    adj_out, mom_out, x_up, x_down, y_up, y_down, adj_pad, fluid_pad,
):
    fill_field(fluid_pad, (), fluid, 2, y_low, y_high)
    fill_field_outer(fluid_pad, (), 2, x_low, x_high, e_low, e_high)
    fill_pops(adj_pad, adj, (0, 1, NX - 2, NX - 1), y_low, y_high)
    fill_pops_outer(adj_pad, x_low, x_high, e_low, e_high)
    for x in (0, NX - 1):
        step_plane(x, adj_pad, fluid_pad, pops, phase, adj_out, mom_out)
    flat = adj_out.reshape(19 * NX * NY, NZ)
    for k in range(5):
        x_up[k] = adj_out[x_plus[k], 0]
        x_down[k] = adj_out[x_minus[k], NX - 1]
        take_rows(y_up, k, flat, y_plus[k] * NX * NY)
        take_rows(y_down, k, flat, y_minus[k] * NX * NY + NY - 1)


def one_hots(index, row, hit_out, right_out, at):
    row_iota = lax.broadcasted_iota(jnp.int32, (64, NZ), 0)
    key = (lax.shift_right_logical(index, 6) & 1) * 32 + lax.shift_right_logical(index, 7)
    low = index & 63
    hit = jnp.where(row_iota == key[row : row + 1, :], 1.0, 0.0)
    hit_out[:, pl.ds(at, NZ)] = hit.astype(jnp.bfloat16)
    right = jnp.where(row_iota == low[row : row + 1, :], 1.0, 0.0)
    right_out[:, pl.ds(at, NZ)] = right.astype(jnp.bfloat16)


OWN = NX * NY * NZ
SIDE = WX * NZ
HALO = 2 * NY * NZ + 2 * SIDE


def own_kernel(table, phase_a, phase_b, fluid, wall, patch, phi_out, hit_out, right_out):
    def plane(x, carry):
        index = patch[x] & 4095
        contact = wall[x].astype(f32) * look_up(table, index)
        wet = fluid[x].astype(f32)
        phi_out[0, x] = wet * phase_a[x] + contact
        phi_out[1, x] = wet * phase_b[x] + contact
        for r in range(NY):
            one_hots(index, r, hit_out, right_out, pl.multiple_of((x * NY + r) * NZ, NZ))
        return carry

    lax.fori_loop(0, NX, plane, 0)


def middle_kernel(
    phi, table, fluid, wall, mom, y_low, y_high, x_low, x_high, e_low, e_high,
    dgrad_out, grad_out, fluid_out, wall_own, wall_face, wall_side, hit_out, right_out,
    phi_pad,
):
    fill_field(fluid_out, (), fluid, 2, y_low, y_high)
    fill_field_outer(fluid_out, (), 2, x_low, x_high, e_low, e_high)

    def copy(x, carry):
        for t in range(2):
            phi_pad[t, x + 1, pl.ds(LOW, NY), :] = phi[t, x]
        wall_own[x] = wall[x].astype(f32)
        return carry

    lax.fori_loop(0, NX, copy, 0)

    def imposed(slot):
        index = slot(4).astype(jnp.int32) & 4095
        contact = slot(3) * look_up(table, index)
        return index, [slot(2) * slot(t) + contact for t in range(2)]

    for side, (face, x) in enumerate(((x_low, 0), (x_high, WX - 1))):
        index, values = imposed(lambda k: face[5 + k])
        wall_face[side] = face[8]
        for t in range(2):
            phi_pad[t, x, pl.ds(LOW, NY), :] = values[t]
        for r in range(NY):
            one_hots(index, r, hit_out, right_out, (side * NY + r) * NZ)
    base = 2 * NY * NZ
    for side, (rows, edge, y) in enumerate(((y_low, e_low, LOW - 1), (y_high, e_high, LOW + NY))):
        index, values = imposed(lambda k: rows[pl.ds((5 + k) * NX, NX), :])
        wall_side[side, pl.ds(1, NX), :] = rows[pl.ds(8 * NX, NX), :]
        for x in range(NX):
            for t in range(2):
                phi_pad[t, x + 1, pl.ds(y, 1), :] = values[t][x : x + 1, :]
            one_hots(index, x, hit_out, right_out, base + side * SIDE + (x + 1) * NZ)
    corners = [(edge, first) for edge in (e_low, e_high) for first in (2, 2 + FIELDS)]

    def corner_rows(k):
        rows = [edge[pl.ds(first + k, 1), :] for edge, first in corners]
        return jnp.concatenate(rows + rows, axis=0)

    index, values = imposed(corner_rows)
    on_wall = corner_rows(3)
    for r in range(4):
        side, x, y = r // 2, (WX - 1) * (r % 2), (LOW - 1, LOW + NY)[r // 2]
        wall_side[side, pl.ds(x, 1), :] = on_wall[r : r + 1, :]
        for t in range(2):
            phi_pad[t, x, pl.ds(y, 1), :] = values[t][r : r + 1, :]
        one_hots(index, r, hit_out, right_out, base + side * SIDE + x * NZ)

    def plane(x, carry):
        def view(t):
            return lambda a, b: tile(phi_pad, (t,), x, (a, b, 0))

        first, n = gradient(view(0)), gradient(view(1))
        for d in range(3):
            grad_out[d, x] = first[d]
        dgrad = gradient_back(mom[0, x], [mom[1 + k, x] for k in range(6)], n)
        for d in range(3):
            dgrad_out[d, x] = dgrad[d]
        return carry

    lax.fori_loop(0, NX, plane, 0)


def own_terms(*args):
    hots = ((64, OWN), jnp.bfloat16)
    return whole_call(own_kernel, "own_terms", [((2, NX, NY, NZ), f32), hots, hots], args)


def middle(*args):
    shapes = [vector, vector, ((WX, ROWS, NZ), f32), ((NX, NY, NZ), f32), ((2, NY, NZ), f32), ((2, WX, NZ), f32)]
    shapes += [((64, HALO), jnp.bfloat16)] * 2
    return whole_call(middle_kernel, "middle", shapes, args, [pltpu.VMEM((2, WX, ROWS, NZ), f32)])


def weighted(hit, values):
    bigs, smalls = [], []
    for value in values:
        big = value.astype(jnp.bfloat16).astype(f32)
        for r in range(value.shape[0]):
            for rows, source in ((bigs, big), (smalls, value - big)):
                row = jnp.broadcast_to(source[r : r + 1, :], (16, NZ)).astype(jnp.bfloat16)
                rows.append(jnp.concatenate([row] * 4, axis=0))
    return jnp.concatenate(
        [hit * jnp.concatenate(bigs, axis=1), hit * jnp.concatenate(smalls, axis=1)], axis=0
    )


def table_sum(left, right):
    return lax.dot_general(left, right, (((1,), (1,)), ((), ())), preferred_element_type=f32)


def gradient_plane(x, adj_pad, fluid_pad, grad, dgrad_in, out):
    q0, _, q2 = moments(propagate_back(adj_pad, fluid_pad, x))
    dgrad = gradient_back(q0, q2, [grad[d, x] for d in range(3)])
    for d in range(3):
        out(d, x, dgrad[d] + dgrad_in[d, x])


def plane_adjoint(pad, x):
    return gradient_adjoint(lambda d, a, b: pad[d, x + 1 + a, pl.ds(LOW + b, NY), :])


GROUP = 4


def own_group(start, dgrad_pad, wall, hits, rights):
    values = [plane_adjoint(dgrad_pad, start + k + 1) * wall[start + k] for k in range(GROUP)]
    nodes = pl.ds(pl.multiple_of(start * NY * NZ, NY * NZ), GROUP * NY * NZ)
    return table_sum(weighted(hits[:, nodes], values), rights[:, nodes])


def first_inner_kernel(
    adj, fluid_pad, grad, dgrad_in, y_low, y_high, wall, hits, rights,
    dgrad_out, acc_out,
    adj_pad, dgrad_pad,
):
    fill_pops(adj_pad, adj, range(NX), y_low, y_high)
    dgrad_pad[...] = jnp.zeros_like(dgrad_pad)

    def out(d, x, value):
        dgrad_out[d, x] = value
        dgrad_pad[d, x + 2, pl.ds(LOW, NY), :] = value

    def plane(x, carry):
        gradient_plane(x, adj_pad, fluid_pad, grad, dgrad_in, out)
        return carry

    lax.fori_loop(1, NX - 1, plane, 0)
    acc_out[...] = jnp.zeros_like(acc_out)

    def group(g, carry):
        acc_out[...] += own_group(2 + g * GROUP, dgrad_pad, wall, hits, rights)
        return carry

    lax.fori_loop(0, (NX - 4) // GROUP, group, 0)


def first_outer_kernel(
    adj, fluid_pad, grad, dgrad_in, y_low, y_high, x_low, x_high, e_low, e_high, dgrad_inner, acc_in,
    wall, hits, rights, wall_face, wall_side, halo_hits, halo_rights,
    total_out,
    adj_pad, dgrad_pad, rows,
):
    fill_pops(adj_pad, adj, (0, 1, NX - 2, NX - 1), y_low, y_high)
    fill_pops_outer(adj_pad, x_low, x_high, e_low, e_high)
    for d in range(3):
        for x in (0, 1, 2, 3, NX, NX + 1, NX + 2, NX + 3):
            dgrad_pad[d, x] = jnp.zeros((ROWS, NZ), f32)

    def out(d, x, value):
        dgrad_pad[d, x + 2, pl.ds(LOW, NY), :] = value

    for x in (0, NX - 1):
        gradient_plane(x, adj_pad, fluid_pad, grad, dgrad_in, out)
    for x in inner:
        for d in range(3):
            out(d, x, dgrad_inner[d, x])
    values = [plane_adjoint(dgrad_pad, x + 1) * wall[x] for x in (0, 1, NX - 2, NX - 1)]
    total = acc_in[...]
    for k, start in enumerate((0, NX - 2)):
        nodes = pl.ds(start * NY * NZ, 2 * NY * NZ)
        total = total + table_sum(weighted(hits[:, nodes], values[2 * k : 2 * k + 2]), rights[:, nodes])
    values = [plane_adjoint(dgrad_pad, x) * wall_face[k] for k, x in enumerate((0, WX - 1))]
    flat = dgrad_pad.reshape(3 * (WX + 2) * ROWS, NZ)
    for side, (row, sign) in enumerate(((LOW, 1.0), (LOW + NY - 1, -1.0))):
        for d in range(3):
            rows[d] = flat[pl.ds(d * (WX + 2) * ROWS + row, WX + 2, stride=ROWS), :]
        values.append(side_adjoint(rows, sign) * wall_side[side])
    total = total + table_sum(weighted(halo_hits[...], values), halo_rights[...])
    both = total[:64] + total[64:]
    total_out[...] = jnp.concatenate([both[:32], both[32:]], axis=1)


def first_adjoint_kernel(
    pops, phase, adj, fluid_pad, y_low, y_high, x_low, x_high, e_low, e_high, adj_out, adj_pad
):
    fill_pops(adj_pad, adj, range(NX), y_low, y_high)
    fill_pops_outer(adj_pad, x_low, x_high, e_low, e_high)

    def plane(x, carry):
        step_plane(x, adj_pad, fluid_pad, pops, phase, adj_out, None)
        return carry

    lax.fori_loop(0, NX, plane, 0)


def ring(axis, value, step):
    count = lax.axis_size(axis)
    return lax.ppermute(value, axis, [(i, (i + step) % count) for i in range(count)])


def group_sum(value, axis, stride, size):
    count = lax.axis_size(axis)
    got = []
    for s in range(1, size):
        pairs = []
        for i in range(count):
            digit = (i // stride) % size
            pairs.append((i, i + ((digit + s) % size - digit) * stride))
        got.append(lax.ppermute(value, axis, pairs))
    for part in got:
        value = value + part
    return value


def shards(
    pops_first,
    pops_second,
    phase_first,
    phase_second,
    adjoint_last,
    wettability,
    fluid,
    wall,
    patch,
):
    table = wettability.reshape(32, NZ)
    fields = (phase_first, phase_second, fluid, wall, patch)
    x_up, x_down, y_up, y_down = pack(adjoint_last, fields)
    x_high, x_low = ring("pipe", x_up, -1), ring("pipe", x_down, 1)
    y_high, y_low = ring("cross", y_up, -1), ring("cross", y_down, 1)
    phi, hits, rights = own_terms(table, *fields)
    e_up, e_down = pack_edges(x_low, x_high, FIELDS, phi)
    e_high, e_low = ring("cross", e_up, -1), ring("cross", e_down, 1)
    given = (pops_second, phase_second, adjoint_last, fluid, y_low, y_high)
    adjoint, mom = whole_call(
        second_inner_kernel, "second_inner", [block, seven], given, pad_scratch()
    )
    outer = (x_low, x_high, e_low, e_high)
    face, side = ((5, NY, NZ), f32), ((5 * NX, NZ), f32)
    adjoint, mom, x_up, x_down, y_up, y_down = whole_call(
        second_outer_kernel,
        "second_outer",
        [block, seven, face, face, side, side],
        given + outer + (adjoint, mom),
        pad_scratch(),
        {10: 0, 11: 1},
    )
    x_high2, x_low2 = ring("pipe", x_up, -1), ring("pipe", x_down, 1)
    y_high2, y_low2 = ring("cross", y_up, -1), ring("cross", y_down, 1)
    dgrad, grad, fluid_pad, wall_own, wall_face, wall_side, halo_hits, halo_rights = middle(
        phi, table, fluid, wall, mom, y_low, y_high, *outer
    )
    e_up, e_down = pack_edges(x_low2, x_high2, 0, wall_side)
    e_high2, e_low2 = ring("cross", e_up, -1), ring("cross", e_down, 1)
    given = (adjoint, fluid_pad, grad, dgrad, y_low2, y_high2)
    nodes = (wall_own, hits, rights)
    adj_scratch = pad_scratch()[:1]
    dgrad_scratch = adj_scratch + [pltpu.VMEM((3, WX + 2, ROWS, NZ), f32)]
    dgrad_inner, acc = whole_call(
        first_inner_kernel, "first_inner", [vector, ((128, 64), f32)], given + nodes, dgrad_scratch
    )
    outer = (x_low2, x_high2, e_low2, e_high2)
    (total,) = whole_call(
        first_outer_kernel,
        "first_outer",
        [((32, NZ), f32)],
        given + outer + (dgrad_inner, acc) + nodes + (wall_face, wall_side, halo_hits, halo_rights),
        dgrad_scratch + [pltpu.VMEM((3, WX + 2, NZ), f32)],
    )
    (adjoint,) = whole_call(
        first_adjoint_kernel,
        "first_adjoint",
        [block],
        (pops_first, phase_first, adjoint, fluid_pad, y_low2, y_high2, *outer),
        adj_scratch,
    )
    total = group_sum(total, "pipe", 1, 2)
    total = group_sum(total, "pipe", 2, 4)
    total = group_sum(total, "cross", 1, 4)
    total = group_sum(total, "cross", 4, 4)
    return adjoint, total.reshape(wettability.shape)


def solution(mesh):
    return jax.shard_map(
        shards,
        mesh=mesh,
        in_specs=(
            P(None, "pipe", "cross", None),
            P(None, "pipe", "cross", None),
            P("pipe", "cross", None),
            P("pipe", "cross", None),
            P(None, "pipe", "cross", None),
            P(),
            P("pipe", "cross", None),
            P("pipe", "cross", None),
            P("pipe", "cross", None),
        ),
        out_specs=(P(None, "pipe", "cross", None), P()),
        check_vma=False,
    )
```

time: 477 us -> 67.5 us (0.14)
  the two profiles are of different devices: /device:TPU:1 before, /device:TPU:0 now
where the time goes in v1:
time: 67.5 us; the launch traced here: 67.3 us
  starting transfers between devices  36.9 us (55%)
  Pallas kernels  15.7 us (23%)
  waiting for transfers between devices  11.2 us (17%)
  local copies, waits for them, and re-layouts  2.03 us (3%)
  between operations  0.91 us (1%)
    ppermute x12, starting transfers between devices, ring(): lax.ppermute(value, axis, [(i, (i + step) % count) for i in range(count)])  28.6 us
    pallas_call x10, Pallas kernels, whole_call(): pl.pallas_call(kernel, out_shape=[jax.ShapeDtypeStruct(shape, kind) for s...  15.7 us
    ppermute x10, waiting for transfers between devices, group_sum(): got.append(lax.ppermute(value, axis, pairs))  11.1 us
    ppermute x10, starting transfers between devices, group_sum(): got.append(lax.ppermute(value, axis, pairs))  8.27 us
    unnamed x18, local copies, waits for them, and re-layouts  2.03 us
  transfers between devices with their start and end apart: 22, of which 7 were waited for; matrix products, arithmetic and copies ran while one was open for 0% of the time, Pallas kernels for 18%

profile of v1, /device:TPU:0, one launch (start us, length us, event | category | flops | bytes accessed | tf_op | source)
XLA Modules:
  0.0 67.3 jit_solution(11427004304470452625)
XLA Ops:
  0.7 2.2 %pack.1 = (f32[10,8,128]{2,1,0:T(8,128)}, f32[10,8,128]{2,1,0:T(8,128)}, f32[160,128]{1,0:T(8,128)}, f32[160,128]{1,0:T(8,128)}) custom-call(f32[19,16,8,128]{3,2,1,0:T(8,128)} %adj.3, f32[16,8,128]{2,1,0:T(8,128)} %phase.5, f32[16,8,128]{2,1,0:T(8,128)} %phase.4, s32[16,8,128]{2,1,0:T(8,128)} %fluid.7, s32[16,8,128]{2,1,0:T(8,128)} %wall.3, s32[16,8,128]{2,1,0:T(8,128)} %patch.1), custom_call_target="tpu_custom_call" | custom-call | tf_op jit(solution)/shard_map/pack/pallas_call | solution.py:186
  2.9 2.1 %collective-permute-start = (f32[160,128]{1,0:T(8,128)}, f32[160,128]{1,0:T(8,128)S(1)}, u32[]{:S(2)}, u32[]{:S(2)}) collective-permute-start(f32[160,128]{1,0:T(8,128)} %get-tuple-element.31), channel_id=1, source_target_pairs={{0,1},{1,2},{2,3},{3,4},{4,5},{5,6},{6,7},{7,8},{8,9},{9,10},{10,1... | collective-permute-start | bytes 245768 | tf_op jit(solution)/shard_map/ppermute | solution.py:579
  4.9 4.4 %collective-permute-start.1 = (f32[160,128]{1,0:T(8,128)}, f32[160,128]{1,0:T(8,128)S(1)}, u32[]{:S(2)}, u32[]{:S(2)}) collective-permute-start(f32[160,128]{1,0:T(8,128)} %get-tuple-element.32), channel_id=1, source_target_pairs={{0,15},{1,0},{2,1},{3,2},{4,3},{5,4},{6,5},{7,6},{8,7},{9,8},{10,9... | collective-permute-start | bytes 245768 | tf_op jit(solution)/shard_map/ppermute | solution.py:579
  9.3 3.0 %collective-permute-start.3 = (f32[10,8,128]{2,1,0:T(8,128)}, f32[10,8,128]{2,1,0:T(8,128)S(1)}, u32[]{:S(2)}, u32[]{:S(2)}) collective-permute-start(f32[10,8,128]{2,1,0:T(8,128)} %get-tuple-element.34), channel_id=1, source_target_pairs={{0,112},{16,0},{32,16},{48,32},{64,48},{80,64},{96,80},{112,96},{1... | collective-permute-start | bytes 122888 | tf_op jit(solution)/shard_map/ppermute | solution.py:579
  13.0 1.8 %own_terms.1 = (f32[2,16,8,128]{3,2,1,0:T(8,128)S(1)}, bf16[64,16384]{1,0:T(8,128)(2,1)S(1)}, bf16[64,16384]{1,0:T(8,128)(2,1)S(1)}) custom-call(f32[32,128]{1,0:T(8,128)S(1)} %bitcast.3, f32[16,8,128]{2,1,0:T(8,128)S(1)} %copy-done.5, f32[16,8,128]{2,1,0:T(8,128)S(1)} %copy-done.4, s32[16,8,128]{2,1,0:T(8,128)S(1)} %copy-done.2, ...), custom_call_target="tpu_custom_call" | custom-call | tf_op jit(solution)/shard_map/own_terms/pallas_call | solution.py:186
  15.0 5.3 %collective-permute-start.5 = (f32[16,128]{1,0:T(8,128)S(1)}, f32[16,128]{1,0:T(8,128)S(1)}, u32[]{:S(2)}, u32[]{:S(2)}) collective-permute-start(f32[16,128]{1,0:T(8,128)S(1)} %get-tuple-element.37), channel_id=1, source_target_pairs={{0,15},{1,0},{2,1},{3,2},{4,3},{5,4},{6,5},{7,6},{8,7},{9,8},{10,9... | collective-permute-start | bytes 24584 | tf_op jit(solution)/shard_map/ppermute | solution.py:579
  20.4 1.3 %copy-done.1 = f32[19,16,8,128]{3,2,1,0:T(8,128)S(1)} copy-done((f32[19,16,8,128]{3,2,1,0:T(8,128)S(1)}, f32[19,16,8,128]{3,2,1,0:T(8,128)}, u32[]{:S(2)}) %copy-start.1) | copy-done | bytes 1245208
  21.7 1.8 %second_inner.1 = (f32[19,16,8,128]{3,2,1,0:T(8,128)S(1)}, f32[7,16,8,128]{3,2,1,0:T(8,128)S(1)}) custom-call(f32[19,16,8,128]{3,2,1,0:T(8,128)S(1)} %copy-done.1, f32[16,8,128]{2,1,0:T(8,128)S(1)} %copy-done.4, f32[19,16,8,128]{3,2,1,0:T(8,128)S(1)} %copy-done, s32[16,8,128]{2,1,0:T(8,128)S(1)} %copy-done.2, f32[160,128]{1,0:T(8,128)S(1)} %collective-permute-done.y_low, ...), custom_call_target="tpu_custom_call" | custom-call | tf_op jit(solution)/shard_map/second_inner/pallas_call | solution.py:186
  23.7 5.3 %collective-permute-start.7 = (f32[80,128]{1,0:T(8,128)S(1)}, f32[80,128]{1,0:T(8,128)S(1)}, u32[]{:S(2)}, u32[]{:S(2)}) collective-permute-start(f32[80,128]{1,0:T(8,128)S(1)} %get-tuple-element.44), channel_id=1, source_target_pairs={{0,15},{1,0},{2,1},{3,2},{4,3},{5,4},{6,5},{7,6},{8,7},{9,8},{10,9... | collective-permute-start | bytes 122888 | tf_op jit(solution)/shard_map/ppermute | solution.py:579
  29.0 3.0 %collective-permute-start.9 = (f32[5,8,128]{2,1,0:T(8,128)S(1)}, f32[5,8,128]{2,1,0:T(8,128)S(1)}, u32[]{:S(2)}, u32[]{:S(2)}) collective-permute-start(f32[5,8,128]{2,1,0:T(8,128)S(1)} %get-tuple-element.46), channel_id=1, source_target_pairs={{0,112},{16,0},{32,16},{48,32},{64,48},{80,64},{96,80},{112,96},{1... | collective-permute-start | bytes 61448 | tf_op jit(solution)/shard_map/ppermute | solution.py:579
  32.0 2.3 %middle.1 = (f32[3,16,8,128]{3,2,1,0:T(8,128)S(1)}, f32[3,16,8,128]{3,2,1,0:T(8,128)S(1)}, f32[18,24,128]{2,1,0:T(8,128)S(1)}, f32[16,8,128]{2,1,0:T(8,128)S(1)}...) custom-call(f32[2,16,8,128]{3,2,1,0:T(8,128)S(1)} %get-tuple-element, ...), custom_call_target="tpu_custom_call" | custom-call | tf_op jit(solution)/shard_map/middle/pallas_call | solution.py:186
  34.5 5.3 %collective-permute-start.11 = (f32[8,128]{1,0:T(8,128)S(1)}, f32[8,128]{1,0:T(8,128)S(1)}, u32[]{:S(2)}, u32[]{:S(2)}) collective-permute-start(f32[8,128]{1,0:T(8,128)S(1)} %get-tuple-element.49), channel_id=1, source_target_pairs={{0,15},{1,0},{2,1},{3,2},{4,3},{5,4},{6,5},{7,6},{8,7},{9,8},{10,9... | collective-permute-start | bytes 12296 | tf_op jit(solution)/shard_map/ppermute | solution.py:579
  39.8 3.2 %first_inner.1 = (f32[3,16,8,128]{3,2,1,0:T(8,128)S(1)}, f32[128,64]{1,0:T(8,128)S(1)}) custom-call(f32[19,16,8,128]{3,2,1,0:T(8,128)S(1)} %get-tuple-element.40.adj, f32[18,24,128]{2,1,0:T(8,128)S(1)} %get-tuple-element.42.fluid_pad, f32[3,16,8,128]{3,2,1,0:T(8,128)S(1)} %get-tuple-element.50.grad, f32[3,16,8,128]{3,2,1,0:T(8,128)S(1)} %get-tuple-element.51.dgrad_in, ...), custom_call_target="tpu_custom_call" | custom-call | tf_op jit(solution)/shard_map/first_inner/pallas_call | solution.py:186
  43.0 1.1 %first_outer.1 = f32[32,128]{1,0:T(8,128)S(1)} custom-call(f32[19,16,8,128]{3,2,1,0:T(8,128)S(1)} %get-tuple-element.40.adj, f32[18,24,128]{2,1,0:T(8,128)S(1)} %get-tuple-element.42.fluid_pad, f32[3,16,8,128]{3,2,1,0:T(8,128)S(1)} %get-tuple-element.50.grad, f32[3,16,8,128]{3,2,1,0:T(8,128)S(1)} %get-tuple-element.51.dgrad_in, ...), custom_call_target="tpu_custom_call" | custom-call | tf_op jit(solution)/shard_map/first_outer/pallas_call | solution.py:186
  44.2 1.2 %collective-permute-done.12 = f32[32,128]{1,0:T(8,128)S(1)} collective-permute-done((f32[32,128]{1,0:T(8,128)S(1)}, f32[32,128]{1,0:T(8,128)S(1)}, u32[]{:S(2)}, u32[]{:S(2)}) %collective-permute-start.12) | collective-permute-done | bytes 16416 | tf_op jit(solution)/shard_map/ppermute | solution.py:590
  45.4 1.5 %collective-permute-start.15 = (f32[32,128]{1,0:T(8,128)S(1)}, f32[32,128]{1,0:T(8,128)S(1)}, u32[]{:S(2)}, u32[]{:S(2)}) collective-permute-start(f32[32,128]{1,0:T(8,128)S(1)} %add.30), channel_id=1, source_target_pairs={{0,96},{16,112},{32,0},{48,16},{64,32},{80,48},{96,64},{112,80},{1... | collective-permute-start | bytes 49160 | tf_op jit(solution)/shard_map/ppermute | solution.py:590
  47.8 1.4 %collective-permute-done.15 = f32[32,128]{1,0:T(8,128)S(1)} collective-permute-done((f32[32,128]{1,0:T(8,128)S(1)}, f32[32,128]{1,0:T(8,128)S(1)}, u32[]{:S(2)}, u32[]{:S(2)}) %collective-permute-start.15) | collective-permute-done | bytes 16416 | tf_op jit(solution)/shard_map/ppermute | solution.py:590
  49.1 3.0 %collective-permute-done.14 = f32[32,128]{1,0:T(8,128)S(1)} collective-permute-done((f32[32,128]{1,0:T(8,128)S(1)}, f32[32,128]{1,0:T(8,128)S(1)}, u32[]{:S(2)}, u32[]{:S(2)}) %collective-permute-start.14) | collective-permute-done | bytes 16416 | tf_op jit(solution)/shard_map/ppermute | solution.py:590
  52.3 1.9 %collective-permute-start.16 = (f32[32,128]{1,0:T(8,128)S(1)}, f32[32,128]{1,0:T(8,128)S(1)}, u32[]{:S(2)}, u32[]{:S(2)}) collective-permute-start(f32[32,128]{1,0:T(8,128)S(1)} %add_add_fusion.1), channel_id=1, source_target_pairs={{0,1},{1,2},{2,3},{3,0},{4,5},{5,6},{6,7},{7,4},{8,9},{9,10},{10,1... | collective-permute-start | bytes 49160 | tf_op jit(solution)/shard_map/ppermute | solution.py:590
  54.2 1.7 %collective-permute-done.18 = f32[32,128]{1,0:T(8,128)S(1)} collective-permute-done((f32[32,128]{1,0:T(8,128)S(1)}, f32[32,128]{1,0:T(8,128)S(1)}, u32[]{:S(2)}, u32[]{:S(2)}) %collective-permute-start.18) | collective-permute-done | bytes 16416 | tf_op jit(solution)/shard_map/ppermute | solution.py:590
  55.9 1.7 %collective-permute-done.17 = f32[32,128]{1,0:T(8,128)S(1)} collective-permute-done((f32[32,128]{1,0:T(8,128)S(1)}, f32[32,128]{1,0:T(8,128)S(1)}, u32[]{:S(2)}, u32[]{:S(2)}) %collective-permute-start.17) | collective-permute-done | bytes 16416 | tf_op jit(solution)/shard_map/ppermute | solution.py:590
  58.6 2.8 %collective-permute-start.21 = (f32[32,128]{1,0:T(8,128)S(1)}, f32[32,128]{1,0:T(8,128)S(1)}, u32[]{:S(2)}, u32[]{:S(2)}) collective-permute-start(f32[32,128]{1,0:T(8,128)S(1)} %add_add_fusion), channel_id=1, source_target_pairs={{0,12},{1,13},{2,14},{3,15},{4,0},{5,1},{6,2},{7,3},{8,4},{9,5},{1... | collective-permute-start | bytes 49160 | tf_op jit(solution)/shard_map/ppermute | solution.py:590
  62.4 3.0 %first_adjoint.1 = f32[19,16,8,128]{3,2,1,0:T(8,128)} custom-call(f32[19,16,8,128]{3,2,1,0:T(8,128)S(1)} %copy-done.3, f32[16,8,128]{2,1,0:T(8,128)S(1)} %copy-done.5, f32[19,16,8,128]{3,2,1,0:T(8,128)S(1)} %get-tuple-element.40.adj, f32[18,24,128]{2,1,0:T(8,128)S(1)} %get-tuple-element.42.fluid_pad, f32[80,128]{1,0:T(8,128)S(1)} %collective-permute-done.6.y_low, ...), custom_call_target="tpu_custom_call" | custom-call | tf_op jit(solution)/shard_map/first_adjoint/pallas_call | solution.py:186
  65.4 1.3 %collective-permute-done.20 = f32[32,128]{1,0:T(8,128)S(1)} collective-permute-done((f32[32,128]{1,0:T(8,128)S(1)}, f32[32,128]{1,0:T(8,128)S(1)}, u32[]{:S(2)}, u32[]{:S(2)}) %collective-permute-start.20) | collective-permute-done | bytes 16416 | tf_op jit(solution)/shard_map/ppermute | solution.py:590
  (52 shorter events, 4.9 us)
Async XLA Ops:
  0.7 19.7 %copy-start = (f32[19,16,8,128]{3,2,1,0:T(8,128)S(1)}, f32[19,16,8,128]{3,2,1,0:T(8,128)}, u32[]{:S(2)}) copy-start(f32[19,16,8,128]{3,2,1,0:T(8,128)} %adj.3) | copy-start | bytes 3735556
  2.9 17.5 %collective-permute-start = (f32[160,128]{1,0:T(8,128)}, f32[160,128]{1,0:T(8,128)S(1)}, u32[]{:S(2)}, u32[]{:S(2)}) collective-permute-start(f32[160,128]{1,0:T(8,128)} %get-tuple-element.31), channel_id=1, source_target_pairs={{0,1},{1,2},{2,3},{3,4},{4,5},{5,6},{6,7},{7,8},{8,9},{9,10},{10,1... | collective-permute-start | bytes 245768 | tf_op jit(solution)/shard_map/ppermute | solution.py:579
  4.9 15.4 %collective-permute-start.1 = (f32[160,128]{1,0:T(8,128)}, f32[160,128]{1,0:T(8,128)S(1)}, u32[]{:S(2)}, u32[]{:S(2)}) collective-permute-start(f32[160,128]{1,0:T(8,128)} %get-tuple-element.32), channel_id=1, source_target_pairs={{0,15},{1,0},{2,1},{3,2},{4,3},{5,4},{6,5},{7,6},{8,7},{9,8},{10,9... | collective-permute-start | bytes 245768 | tf_op jit(solution)/shard_map/ppermute | solution.py:579
  9.3 5.6 %collective-permute-start.2 = (f32[10,8,128]{2,1,0:T(8,128)}, f32[10,8,128]{2,1,0:T(8,128)S(1)}, u32[]{:S(2)}, u32[]{:S(2)}) collective-permute-start(f32[10,8,128]{2,1,0:T(8,128)} %get-tuple-element.33), channel_id=1, source_target_pairs={{0,16},{16,32},{32,48},{48,64},{64,80},{80,96},{96,112},{112,0},{1... | collective-permute-start | bytes 122888 | tf_op jit(solution)/shard_map/ppermute | solution.py:579
  9.3 5.6 %collective-permute-start.3 = (f32[10,8,128]{2,1,0:T(8,128)}, f32[10,8,128]{2,1,0:T(8,128)S(1)}, u32[]{:S(2)}, u32[]{:S(2)}) collective-permute-start(f32[10,8,128]{2,1,0:T(8,128)} %get-tuple-element.34), channel_id=1, source_target_pairs={{0,112},{16,0},{32,16},{48,32},{64,48},{80,64},{96,80},{112,96},{1... | collective-permute-start | bytes 122888 | tf_op jit(solution)/shard_map/ppermute | solution.py:579
  14.9 8.5 %collective-permute-start.4 = (f32[16,128]{1,0:T(8,128)S(1)}, f32[16,128]{1,0:T(8,128)S(1)}, u32[]{:S(2)}, u32[]{:S(2)}) collective-permute-start(f32[16,128]{1,0:T(8,128)S(1)} %get-tuple-element.36), channel_id=1, source_target_pairs={{0,1},{1,2},{2,3},{3,4},{4,5},{5,6},{6,7},{7,8},{8,9},{9,10},{10,1... | collective-permute-start | bytes 24584 | tf_op jit(solution)/shard_map/ppermute | solution.py:579
  15.0 8.4 %collective-permute-start.5 = (f32[16,128]{1,0:T(8,128)S(1)}, f32[16,128]{1,0:T(8,128)S(1)}, u32[]{:S(2)}, u32[]{:S(2)}) collective-permute-start(f32[16,128]{1,0:T(8,128)S(1)} %get-tuple-element.37), channel_id=1, source_target_pairs={{0,15},{1,0},{2,1},{3,2},{4,3},{5,4},{6,5},{7,6},{8,7},{9,8},{10,9... | collective-permute-start | bytes 24584 | tf_op jit(solution)/shard_map/ppermute | solution.py:579
  23.6 16.2 %collective-permute-start.6 = (f32[80,128]{1,0:T(8,128)S(1)}, f32[80,128]{1,0:T(8,128)S(1)}, u32[]{:S(2)}, u32[]{:S(2)}) collective-permute-start(f32[80,128]{1,0:T(8,128)S(1)} %get-tuple-element.43), channel_id=1, source_target_pairs={{0,1},{1,2},{2,3},{3,4},{4,5},{5,6},{6,7},{7,8},{8,9},{9,10},{10,1... | collective-permute-start | bytes 122888 | tf_op jit(solution)/shard_map/ppermute | solution.py:579
  23.7 16.1 %collective-permute-start.7 = (f32[80,128]{1,0:T(8,128)S(1)}, f32[80,128]{1,0:T(8,128)S(1)}, u32[]{:S(2)}, u32[]{:S(2)}) collective-permute-start(f32[80,128]{1,0:T(8,128)S(1)} %get-tuple-element.44), channel_id=1, source_target_pairs={{0,15},{1,0},{2,1},{3,2},{4,3},{5,4},{6,5},{7,6},{8,7},{9,8},{10,9... | collective-permute-start | bytes 122888 | tf_op jit(solution)/shard_map/ppermute | solution.py:579
  29.0 5.3 %collective-permute-start.8 = (f32[5,8,128]{2,1,0:T(8,128)S(1)}, f32[5,8,128]{2,1,0:T(8,128)S(1)}, u32[]{:S(2)}, u32[]{:S(2)}) collective-permute-start(f32[5,8,128]{2,1,0:T(8,128)S(1)} %get-tuple-element.45), channel_id=1, source_target_pairs={{0,16},{16,32},{32,48},{48,64},{64,80},{80,96},{96,112},{112,0},{1... | collective-permute-start | bytes 61448 | tf_op jit(solution)/shard_map/ppermute | solution.py:579
  29.0 5.3 %collective-permute-start.9 = (f32[5,8,128]{2,1,0:T(8,128)S(1)}, f32[5,8,128]{2,1,0:T(8,128)S(1)}, u32[]{:S(2)}, u32[]{:S(2)}) collective-permute-start(f32[5,8,128]{2,1,0:T(8,128)S(1)} %get-tuple-element.46), channel_id=1, source_target_pairs={{0,112},{16,0},{32,16},{48,32},{64,48},{80,64},{96,80},{112,96},{1... | collective-permute-start | bytes 61448 | tf_op jit(solution)/shard_map/ppermute | solution.py:579
  34.4 8.6 %collective-permute-start.10 = (f32[8,128]{1,0:T(8,128)S(1)}, f32[8,128]{1,0:T(8,128)S(1)}, u32[]{:S(2)}, u32[]{:S(2)}) collective-permute-start(f32[8,128]{1,0:T(8,128)S(1)} %get-tuple-element.48), channel_id=1, source_target_pairs={{0,1},{1,2},{2,3},{3,4},{4,5},{5,6},{6,7},{7,8},{8,9},{9,10},{10,1... | collective-permute-start | bytes 12296 | tf_op jit(solution)/shard_map/ppermute | solution.py:579
  34.5 8.5 %collective-permute-start.11 = (f32[8,128]{1,0:T(8,128)S(1)}, f32[8,128]{1,0:T(8,128)S(1)}, u32[]{:S(2)}, u32[]{:S(2)}) collective-permute-start(f32[8,128]{1,0:T(8,128)S(1)} %get-tuple-element.49), channel_id=1, source_target_pairs={{0,15},{1,0},{2,1},{3,2},{4,3},{5,4},{6,5},{7,6},{8,7},{9,8},{10,9... | collective-permute-start | bytes 12296 | tf_op jit(solution)/shard_map/ppermute | solution.py:579
  43.0 19.4 %copy-start.3 = (f32[19,16,8,128]{3,2,1,0:T(8,128)S(1)}, f32[19,16,8,128]{3,2,1,0:T(8,128)}, u32[]{:S(2)}) copy-start(f32[19,16,8,128]{3,2,1,0:T(8,128)} %pops.5) | copy-start | bytes 3735556
  44.2 1.2 %collective-permute-start.12 = (f32[32,128]{1,0:T(8,128)S(1)}, f32[32,128]{1,0:T(8,128)S(1)}, u32[]{:S(2)}, u32[]{:S(2)}) collective-permute-start(f32[32,128]{1,0:T(8,128)S(1)} %first_outer.1), channel_id=1, source_target_pairs={{0,16},{16,0},{32,48},{48,32},{64,80},{80,64},{96,112},{112,96},{1... | collective-permute-start | bytes 49160 | tf_op jit(solution)/shard_map/ppermute | solution.py:590
  45.4 3.7 %collective-permute-start.15 = (f32[32,128]{1,0:T(8,128)S(1)}, f32[32,128]{1,0:T(8,128)S(1)}, u32[]{:S(2)}, u32[]{:S(2)}) collective-permute-start(f32[32,128]{1,0:T(8,128)S(1)} %add.30), channel_id=1, source_target_pairs={{0,96},{16,112},{32,0},{48,16},{64,32},{80,48},{96,64},{112,80},{1... | collective-permute-start | bytes 49160 | tf_op jit(solution)/shard_map/ppermute | solution.py:590
  46.8 5.2 %collective-permute-start.14 = (f32[32,128]{1,0:T(8,128)S(1)}, f32[32,128]{1,0:T(8,128)S(1)}, u32[]{:S(2)}, u32[]{:S(2)}) collective-permute-start(f32[32,128]{1,0:T(8,128)S(1)} %add.30), channel_id=1, source_target_pairs={{0,64},{16,80},{32,96},{48,112},{64,0},{80,16},{96,32},{112,48},{1... | collective-permute-start | bytes 49160 | tf_op jit(solution)/shard_map/ppermute | solution.py:590
  46.8 5.2 %collective-permute-start.13 = (f32[32,128]{1,0:T(8,128)S(1)}, f32[32,128]{1,0:T(8,128)S(1)}, u32[]{:S(2)}, u32[]{:S(2)}) collective-permute-start(f32[32,128]{1,0:T(8,128)S(1)} %add.30), channel_id=1, source_target_pairs={{0,32},{16,48},{32,64},{48,80},{64,96},{80,112},{96,0},{112,16},{1... | collective-permute-start | bytes 49160 | tf_op jit(solution)/shard_map/ppermute | solution.py:590
  52.1 3.8 %collective-permute-start.18 = (f32[32,128]{1,0:T(8,128)S(1)}, f32[32,128]{1,0:T(8,128)S(1)}, u32[]{:S(2)}, u32[]{:S(2)}) collective-permute-start(f32[32,128]{1,0:T(8,128)S(1)} %add_add_fusion.1), channel_id=1, source_target_pairs={{0,3},{1,0},{2,1},{3,2},{4,7},{5,4},{6,5},{7,6},{8,11},{9,8},{10,9... | collective-permute-start | bytes 49160 | tf_op jit(solution)/shard_map/ppermute | solution.py:590
  52.2 5.4 %collective-permute-start.17 = (f32[32,128]{1,0:T(8,128)S(1)}, f32[32,128]{1,0:T(8,128)S(1)}, u32[]{:S(2)}, u32[]{:S(2)}) collective-permute-start(f32[32,128]{1,0:T(8,128)S(1)} %add_add_fusion.1), channel_id=1, source_target_pairs={{0,2},{1,3},{2,0},{3,1},{4,6},{5,7},{6,4},{7,5},{8,10},{9,11},{10,... | collective-permute-start | bytes 49160 | tf_op jit(solution)/shard_map/ppermute | solution.py:590
  52.3 6.3 %collective-permute-start.16 = (f32[32,128]{1,0:T(8,128)S(1)}, f32[32,128]{1,0:T(8,128)S(1)}, u32[]{:S(2)}, u32[]{:S(2)}) collective-permute-start(f32[32,128]{1,0:T(8,128)S(1)} %add_add_fusion.1), channel_id=1, source_target_pairs={{0,1},{1,2},{2,3},{3,0},{4,5},{5,6},{6,7},{7,4},{8,9},{9,10},{10,1... | collective-permute-start | bytes 49160 | tf_op jit(solution)/shard_map/ppermute | solution.py:590
  58.6 6.8 %collective-permute-start.21 = (f32[32,128]{1,0:T(8,128)S(1)}, f32[32,128]{1,0:T(8,128)S(1)}, u32[]{:S(2)}, u32[]{:S(2)}) collective-permute-start(f32[32,128]{1,0:T(8,128)S(1)} %add_add_fusion), channel_id=1, source_target_pairs={{0,12},{1,13},{2,14},{3,15},{4,0},{5,1},{6,2},{7,3},{8,4},{9,5},{1... | collective-permute-start | bytes 49160 | tf_op jit(solution)/shard_map/ppermute | solution.py:590
  61.4 5.2 %collective-permute-start.20 = (f32[32,128]{1,0:T(8,128)S(1)}, f32[32,128]{1,0:T(8,128)S(1)}, u32[]{:S(2)}, u32[]{:S(2)}) collective-permute-start(f32[32,128]{1,0:T(8,128)S(1)} %add_add_fusion), channel_id=1, source_target_pairs={{0,8},{1,9},{2,10},{3,11},{4,12},{5,13},{6,14},{7,15},{8,0},{9,1},... | collective-permute-start | bytes 49160 | tf_op jit(solution)/shard_map/ppermute | solution.py:590
  61.4 5.2 %collective-permute-start.19 = (f32[32,128]{1,0:T(8,128)S(1)}, f32[32,128]{1,0:T(8,128)S(1)}, u32[]{:S(2)}, u32[]{:S(2)}) collective-permute-start(f32[32,128]{1,0:T(8,128)S(1)} %add_add_fusion), channel_id=1, source_target_pairs={{0,4},{1,5},{2,6},{3,7},{4,8},{5,9},{6,10},{7,11},{8,12},{9,13},{1... | collective-permute-start | bytes 49160 | tf_op jit(solution)/shard_map/ppermute | solution.py:590
  (7 other events, 60.2 us)

commit v2 on v1

--- a/solution.py
+++ b/solution.py
@@ -128,9 +128,8 @@
     return a[0] * b[0] + a[1] * b[1] + a[2] * b[2]
 
 
-def collide_back(post, q, f, phase, store):
+def collide_back(post, q, u, phase, store):
     q0, q1, q2 = q
-    u = velocity(f)
     omega = 1.0 / (relax_heavy * (1.0 + phase) * 0.5 + relax_light * (1.0 - phase) * 0.5)
     q2u = apply_second(q2, u)
     along = q0 - 4.5 * dot3(u, q2u) + 1.5 * dot3(u, u) * q0
@@ -177,15 +176,19 @@
     return -(flat + twelfth * (roll_z(sign * gy(0) + gz(0), 1) + roll_z(sign * gy(0) - gz(0), -1)))
 
 
-def whole_call(kernel, name, out_shape, args, scratch=(), aliases=None, in_hbm=False):
+def whole_call(kernel, name, out_shape, args, scratch=(), aliases=None, in_hbm=False, specs=None):
     options = {}
     if in_hbm:
         options["in_specs"] = [pl.BlockSpec(memory_space=pl.ANY)] * len(args)
     else:
+        if specs:
+            options["in_specs"] = specs
         options["compiler_params"] = pltpu.CompilerParams(vmem_limit_bytes=24 * 1024 * 1024)
     return pl.pallas_call(
         kernel,
-        out_shape=[jax.ShapeDtypeStruct(shape, kind) for shape, kind in out_shape],
+        out_shape=[
+            pltpu.VMEM(shape, kind) if in_hbm else jax.ShapeDtypeStruct(shape, kind) for shape, kind in out_shape
+        ],
         scratch_shapes=scratch,
         input_output_aliases=aliases or {},
         name=name,
@@ -193,62 +196,92 @@
     )(*args)
 
 
-def take_rows(out, slot, flat, start):
-    out[pl.ds(slot * NX, NX), :] = flat[pl.ds(start, NX, stride=NY), :].astype(f32)
-
-
-def pack_kernel(adj_hbm, *refs):
-    hbm, (x_up, x_down, y_up, y_down), (adj, *fields) = refs[:FIELDS], refs[FIELDS : FIELDS + 4], refs[FIELDS + 4 : -1]
-    sem = refs[-1]
-    copies = [pltpu.make_async_copy(adj_hbm, adj, sem.at[0])]
-    for k in range(FIELDS):
-        copies.append(pltpu.make_async_copy(hbm[k], fields[k], sem.at[k + 1]))
+class Pick:
+    def __init__(self, first, a, b):
+        self.first, self.a, self.b = first, a, b
+
+    def __getitem__(self, index):
+        return jnp.where(self.first, self.a[index], self.b[index])
+
+
+def is_odd(axis):
+    return lax.axis_index(axis) % 2 == 1
+
+
+def sides(axis, a, b):
+    odd = is_odd(axis)
+    return Pick(odd, a, b), Pick(odd, b, a)
+
+
+def put(odd, outs, index, up, down):
+    outs[0][index] = jnp.where(odd, up, down)
+    outs[1][index] = jnp.where(odd, down, up)
+
+
+def put_rows(odd, outs, slot, flat, up, down):
+    rows = [flat[pl.ds(start, NX, stride=NY), :].astype(f32) for start in (up, down)]
+    put(odd, outs, (pl.ds(slot * NX, NX), slice(None)), *rows)
+
+
+def put_pops(adj, x_outs, y_outs):
+    odd_x, odd_y = is_odd("pipe"), is_odd("cross")
+    flat = adj.reshape(19 * NX * NY, NZ)
+    for k in range(5):
+        put(odd_x, x_outs, k, adj[x_plus[k], 0], adj[x_minus[k], NX - 1])
+        put_rows(odd_y, y_outs, k, flat, y_plus[k] * NX * NY, y_minus[k] * NX * NY + NY - 1)
+
+
+def fetch(pairs, sem):
+    copies = [pltpu.make_async_copy(a, b, sem.at[k]) for k, (a, b) in enumerate(pairs)]
     for copy in copies:
         copy.start()
-    for copy in copies:
+    return copies
+
+
+def pack_kernel(adj_hbm, *refs):
+    hbm, (xa, xb, ya, yb), (adj, *fields) = refs[:FIELDS], refs[FIELDS : FIELDS + 4], refs[FIELDS + 4 : -1]
+    for copy in fetch([(adj_hbm, adj), *zip(hbm, fields)], refs[-1]):
         copy.wait()
-    flat = adj.reshape(19 * NX * NY, NZ)
-    for k in range(5):
-        x_up[k] = adj[x_plus[k], 0]
-        x_down[k] = adj[x_minus[k], NX - 1]
-        take_rows(y_up, k, flat, y_plus[k] * NX * NY)
-        take_rows(y_down, k, flat, y_minus[k] * NX * NY + NY - 1)
+    put_pops(adj, (xa, xb), (ya, yb))
+    odd_x, odd_y = is_odd("pipe"), is_odd("cross")
     for k in range(FIELDS):
-        x_up[5 + k] = fields[k][0].astype(f32)
-        x_down[5 + k] = fields[k][NX - 1].astype(f32)
-        rows = fields[k].reshape(NX * NY, NZ)
-        take_rows(y_up, 5 + k, rows, 0)
-        take_rows(y_down, 5 + k, rows, NY - 1)
+        put(odd_x, (xa, xb), 5 + k, fields[k][0].astype(f32), fields[k][NX - 1].astype(f32))
+        put_rows(odd_y, (ya, yb), 5 + k, fields[k].reshape(NX * NY, NZ), 0, NY - 1)
 
 
 def pack(adjoint, fields):
-    face, side = ((5 + FIELDS, NY, NZ), f32), (((5 + FIELDS) * NX, NZ), f32)
+    face, side = ((5 + FIELDS + 2, NY, NZ), f32), (((5 + FIELDS) * NX, NZ), f32)
     scratch = [pltpu.VMEM((19, NX, NY, NZ), f32)]
     scratch += [pltpu.VMEM((NX, NY, NZ), field.dtype) for field in fields]
     scratch.append(pltpu.SemaphoreType.DMA((1 + FIELDS,)))
     return whole_call(pack_kernel, "pack", [face, face, side, side], (adjoint, *fields), scratch, in_hbm=True)
 
 
-edge_up = (10, 7)
-edge_down = (8, 9)
-
-
-def pack_edges_kernel(count, low, high, _, up, down):
-    for out, pops, row in ((up, edge_up, 0), (down, edge_down, NY - 1)):
-        out[pl.ds(0, 1), :] = low[x_minus.index(pops[0]), pl.ds(row, 1), :]
-        out[pl.ds(1, 1), :] = high[x_plus.index(pops[1]), pl.ds(row, 1), :]
-        for k in range(count):
-            out[pl.ds(2 + k, 1), :] = low[5 + k, pl.ds(row, 1), :]
-            out[pl.ds(2 + count + k, 1), :] = high[5 + k, pl.ds(row, 1), :]
-        used = 2 + 2 * count
-        size = out.shape[0]
-        out[pl.ds(used, size - used), :] = jnp.zeros((size - used, NZ), f32)
-
-
-def pack_edges(low, high, count, after):
-    out = ((16 if count else 8, NZ), f32)
+edge_plus = (7, 9)
+edge_minus = (10, 8)
+
+
+def pack_edges_kernel(count, xa, xb, ya, yb, _, xa_out, xb_out):
+    planes = 5 + count
+    for k in range(planes):
+        xa_out[k] = xa[k]
+        xb_out[k] = xb[k]
+    low, high = sides("cross", ya, yb)
+    odd = is_odd("pipe")
+    for e, (rows, pops) in enumerate(((high, y_plus), (low, y_minus))):
+        xa_out[planes + e] = jnp.zeros((NY, NZ), f32)
+        xb_out[planes + e] = jnp.zeros((NY, NZ), f32)
+        starts = [(pops.index(edge_plus[e]), pops.index(edge_minus[e]))] + [(5 + k, 5 + k) for k in range(count)]
+        for r, (up, down) in enumerate(starts):
+            up_row = rows[pl.ds(up * NX, 1), :]
+            down_row = rows[pl.ds(down * NX + NX - 1, 1), :]
+            put(odd, (xa_out, xb_out), (planes + e, pl.ds(r, 1), slice(None)), up_row, down_row)
+
+
+def pack_edges(x_pair, y_halo, count, after):
+    out = ((5 + count + 2, NY, NZ), f32)
     kernel = functools.partial(pack_edges_kernel, count)
-    return whole_call(kernel, "pack_edges", [out, out], (low, high, after))
+    return whole_call(kernel, "pack_edges", [out, out], (*x_pair, *y_halo, after))
 
 
 def fill_sides(pad, lead, y_low, low_slot, y_high, high_slot):
@@ -267,13 +300,13 @@
             pad[y_plus[k], x + 1, pl.ds(LOW + NY, 1), :] = y_high[pl.ds(k * NX + x, 1), :]
 
 
-def fill_pops_outer(pad, x_low, x_high, e_low, e_high):
+def fill_pops_outer(pad, x_low, x_high, planes):
     for k in range(5):
         pad[x_minus[k], 0, pl.ds(LOW, NY), :] = x_low[k]
         pad[x_plus[k], WX - 1, pl.ds(LOW, NY), :] = x_high[k]
-    for row, pops, edge in ((LOW + NY, edge_up, e_high), (LOW - 1, edge_down, e_low)):
-        pad[pops[0], 0, pl.ds(row, 1), :] = edge[pl.ds(0, 1), :]
-        pad[pops[1], WX - 1, pl.ds(row, 1), :] = edge[pl.ds(1, 1), :]
+    for e, row in enumerate((LOW + NY, LOW - 1)):
+        pad[edge_minus[e], 0, pl.ds(row, 1), :] = x_low[planes + e, pl.ds(0, 1), :]
+        pad[edge_plus[e], WX - 1, pl.ds(row, 1), :] = x_high[planes + e, pl.ds(0, 1), :]
 
 
 def fill_field(pad, lead, own, slot, y_low, y_high):
@@ -282,12 +315,11 @@
     fill_sides(pad, lead, y_low, 5 + slot, y_high, 5 + slot)
 
 
-def fill_field_outer(pad, lead, slot, x_low, x_high, e_low, e_high):
-    pad[lead + (0, pl.ds(LOW, NY), slice(None))] = x_low[5 + slot]
-    pad[lead + (WX - 1, pl.ds(LOW, NY), slice(None))] = x_high[5 + slot]
-    for row, edge in ((LOW + NY, e_high), (LOW - 1, e_low)):
-        pad[lead + (0, pl.ds(row, 1), slice(None))] = edge[pl.ds(2 + slot, 1), :]
-        pad[lead + (WX - 1, pl.ds(row, 1), slice(None))] = edge[pl.ds(2 + FIELDS + slot, 1), :]
+def fill_field_outer(pad, lead, slot, x_low, x_high):
+    for x, face in ((0, x_low), (WX - 1, x_high)):
+        pad[lead + (x, pl.ds(LOW, NY), slice(None))] = face[5 + slot]
+        for e, row in enumerate((LOW + NY, LOW - 1)):
+            pad[lead + (x, pl.ds(row, 1), slice(None))] = face[5 + FIELDS + e, pl.ds(1 + slot, 1), :]
 
 
 def propagate_back(adj_pad, fluid_pad, x):
@@ -301,14 +333,14 @@
     return post
 
 
-def step_plane(x, adj_pad, fluid_pad, pops, phase, adj_out, mom_out):
+def step_plane(x, adj_pad, fluid_pad, speed, phase, adj_out, mom_out, at=0):
     post = propagate_back(adj_pad, fluid_pad, x)
     q = moments(post)
 
     def store(i, value):
-        adj_out[i, x] = value
-
-    collide_back(post, q, [pops[i, x] for i in range(19)], phase[x], store)
+        adj_out[i, x - at] = value
+
+    collide_back(post, q, [speed[d, x] for d in range(3)], phase[x], store)
     if mom_out is not None:
         mom_out[0, x] = q[0]
         for k in range(6):
@@ -318,12 +350,13 @@
 inner = range(1, NX - 1)
 
 
-def second_inner_kernel(pops, phase, adj, fluid, y_low, y_high, adj_out, mom_out, adj_pad, fluid_pad):
+def second_inner_kernel(speed, phase, adj, fluid, ya, yb, adj_out, mom_out, adj_pad, fluid_pad):
+    y_low, y_high = sides("cross", ya, yb)
     fill_field(fluid_pad, (), fluid, 2, y_low, y_high)
     fill_pops(adj_pad, adj, range(NX), y_low, y_high)
 
     def plane(x, carry):
-        step_plane(x, adj_pad, fluid_pad, pops, phase, adj_out, mom_out)
+        step_plane(x, adj_pad, fluid_pad, speed, phase, adj_out, mom_out)
         return carry
 
     lax.fori_loop(1, NX - 1, plane, 0)
@@ -339,21 +372,17 @@
 
 
 def second_outer_kernel(
-    pops, phase, adj, fluid, y_low, y_high, x_low, x_high, e_low, e_high, adj_in, mom_in,
-    adj_out, mom_out, x_up, x_down, y_up, y_down, adj_pad, fluid_pad,
+    speed, phase, adj, fluid, ya, yb, xa, xb, adj_in, mom_in,
+    adj_out, mom_out, xa_out, xb_out, ya_out, yb_out, adj_pad, fluid_pad,
 ):
+    (x_low, x_high), (y_low, y_high) = sides("pipe", xa, xb), sides("cross", ya, yb)
     fill_field(fluid_pad, (), fluid, 2, y_low, y_high)
-    fill_field_outer(fluid_pad, (), 2, x_low, x_high, e_low, e_high)
+    fill_field_outer(fluid_pad, (), 2, x_low, x_high)
     fill_pops(adj_pad, adj, (0, 1, NX - 2, NX - 1), y_low, y_high)
-    fill_pops_outer(adj_pad, x_low, x_high, e_low, e_high)
+    fill_pops_outer(adj_pad, x_low, x_high, 5 + FIELDS)
     for x in (0, NX - 1):
-        step_plane(x, adj_pad, fluid_pad, pops, phase, adj_out, mom_out)
-    flat = adj_out.reshape(19 * NX * NY, NZ)
-    for k in range(5):
-        x_up[k] = adj_out[x_plus[k], 0]
-        x_down[k] = adj_out[x_minus[k], NX - 1]
-        take_rows(y_up, k, flat, y_plus[k] * NX * NY)
-        take_rows(y_down, k, flat, y_minus[k] * NX * NY + NY - 1)
+        step_plane(x, adj_pad, fluid_pad, speed, phase, adj_out, mom_out)
+    put_pops(adj_out, (xa_out, xb_out), (ya_out, yb_out))
 
 
 def one_hots(index, row, hit_out, right_out, at):
@@ -371,9 +400,29 @@
 HALO = 2 * NY * NZ + 2 * SIDE
 
 
-def own_kernel(table, phase_a, phase_b, fluid, wall, patch, phi_out, hit_out, right_out):
+def store_velocity(pops, out):
+    def plane(x, carry):
+        u = velocity([pops[i, x] for i in range(19)])
+        for d in range(3):
+            out[d, x] = u[d]
+        return carry
+
+    lax.fori_loop(0, NX, plane, 0)
+
+
+def own_kernel(
+    table_hbm, phase_a_hbm, phase_b_hbm, fluid_hbm, wall_hbm, patch_hbm, pops_hbm,
+    phi_out, hit_out, right_out, wall_out, speed_out,
+    table, phase_a, phase_b, fluid, wall, patch, pops, sem,
+):
+    hbm = (table_hbm, phase_a_hbm, phase_b_hbm, fluid_hbm, wall_hbm, patch_hbm, pops_hbm)
+    copies = fetch(zip(hbm, (table, phase_a, phase_b, fluid, wall, patch, pops)), sem)
+    for copy in copies[:-1]:
+        copy.wait()
+
     def plane(x, carry):
         index = patch[x] & 4095
+        wall_out[x] = wall[x].astype(f32)
         contact = wall[x].astype(f32) * look_up(table, index)
         wet = fluid[x].astype(f32)
         phi_out[0, x] = wet * phase_a[x] + contact
@@ -383,20 +432,23 @@
         return carry
 
     lax.fori_loop(0, NX, plane, 0)
+    copies[-1].wait()
+    store_velocity(pops, speed_out)
 
 
 def middle_kernel(
-    phi, table, fluid, wall, mom, y_low, y_high, x_low, x_high, e_low, e_high,
-    dgrad_out, grad_out, fluid_out, wall_own, wall_face, wall_side, hit_out, right_out,
-    phi_pad,
+    phi, table, fluid, mom, ya, yb, xa, xb, pops_hbm,
+    dgrad_out, grad_out, fluid_out, wall_face, wall_side, hit_out, right_out, speed_out,
+    phi_pad, pops, sem,
 ):
+    (copy_pops,) = fetch([(pops_hbm, pops)], sem)
+    (x_low, x_high), (y_low, y_high) = sides("pipe", xa, xb), sides("cross", ya, yb)
     fill_field(fluid_out, (), fluid, 2, y_low, y_high)
-    fill_field_outer(fluid_out, (), 2, x_low, x_high, e_low, e_high)
+    fill_field_outer(fluid_out, (), 2, x_low, x_high)
 
     def copy(x, carry):
         for t in range(2):
             phi_pad[t, x + 1, pl.ds(LOW, NY), :] = phi[t, x]
-        wall_own[x] = wall[x].astype(f32)
         return carry
 
     lax.fori_loop(0, NX, copy, 0)
@@ -414,17 +466,15 @@
         for r in range(NY):
             one_hots(index, r, hit_out, right_out, (side * NY + r) * NZ)
     base = 2 * NY * NZ
-    for side, (rows, edge, y) in enumerate(((y_low, e_low, LOW - 1), (y_high, e_high, LOW + NY))):
+    for side, (rows, y) in enumerate(((y_low, LOW - 1), (y_high, LOW + NY))):
         index, values = imposed(lambda k: rows[pl.ds((5 + k) * NX, NX), :])
         wall_side[side, pl.ds(1, NX), :] = rows[pl.ds(8 * NX, NX), :]
         for x in range(NX):
             for t in range(2):
                 phi_pad[t, x + 1, pl.ds(y, 1), :] = values[t][x : x + 1, :]
             one_hots(index, x, hit_out, right_out, base + side * SIDE + (x + 1) * NZ)
-    corners = [(edge, first) for edge in (e_low, e_high) for first in (2, 2 + FIELDS)]
-
     def corner_rows(k):
-        rows = [edge[pl.ds(first + k, 1), :] for edge, first in corners]
+        rows = [face[5 + FIELDS + 1 - e, pl.ds(1 + k, 1), :] for e in range(2) for face in (x_low, x_high)]
         return jnp.concatenate(rows + rows, axis=0)
 
     index, values = imposed(corner_rows)
@@ -449,17 +499,23 @@
         return carry
 
     lax.fori_loop(0, NX, plane, 0)
+    copy_pops.wait()
+    store_velocity(pops, speed_out)
 
 
 def own_terms(*args):
     hots = ((64, OWN), jnp.bfloat16)
-    return whole_call(own_kernel, "own_terms", [((2, NX, NY, NZ), f32), hots, hots], args)
+    scratch = [pltpu.VMEM(arg.shape, arg.dtype) for arg in args] + [pltpu.SemaphoreType.DMA((len(args),))]
+    shapes = [((2, NX, NY, NZ), f32), hots, hots, ((NX, NY, NZ), f32), vector]
+    return whole_call(own_kernel, "own_terms", shapes, args, scratch, specs=[pl.BlockSpec(memory_space=pl.ANY)] * len(args))
 
 
 def middle(*args):
-    shapes = [vector, vector, ((WX, ROWS, NZ), f32), ((NX, NY, NZ), f32), ((2, NY, NZ), f32), ((2, WX, NZ), f32)]
-    shapes += [((64, HALO), jnp.bfloat16)] * 2
-    return whole_call(middle_kernel, "middle", shapes, args, [pltpu.VMEM((2, WX, ROWS, NZ), f32)])
+    shapes = [vector, vector, ((WX, ROWS, NZ), f32), ((2, NY, NZ), f32), ((2, WX, NZ), f32)]
+    shapes += [((64, HALO), jnp.bfloat16)] * 2 + [vector]
+    scratch = [pltpu.VMEM((2, WX, ROWS, NZ), f32), pltpu.VMEM((19, NX, NY, NZ), f32), pltpu.SemaphoreType.DMA((1,))]
+    specs = [pl.BlockSpec(memory_space=pltpu.VMEM)] * (len(args) - 1) + [pl.BlockSpec(memory_space=pl.ANY)]
+    return whole_call(middle_kernel, "middle", shapes, args, scratch, specs=specs)
 
 
 def weighted(hit, values):
@@ -500,10 +556,11 @@
 
 
 def first_inner_kernel(
-    adj, fluid_pad, grad, dgrad_in, y_low, y_high, wall, hits, rights,
+    adj, fluid_pad, grad, dgrad_in, ya, yb, wall, hits, rights,
     dgrad_out, acc_out,
     adj_pad, dgrad_pad,
 ):
+    y_low, y_high = sides("cross", ya, yb)
     fill_pops(adj_pad, adj, range(NX), y_low, y_high)
     dgrad_pad[...] = jnp.zeros_like(dgrad_pad)
 
@@ -526,13 +583,14 @@
 
 
 def first_outer_kernel(
-    adj, fluid_pad, grad, dgrad_in, y_low, y_high, x_low, x_high, e_low, e_high, dgrad_inner, acc_in,
+    adj, fluid_pad, grad, dgrad_in, ya, yb, xa, xb, dgrad_inner, acc_in,
     wall, hits, rights, wall_face, wall_side, halo_hits, halo_rights,
     total_out,
     adj_pad, dgrad_pad, rows,
 ):
+    (x_low, x_high), (y_low, y_high) = sides("pipe", xa, xb), sides("cross", ya, yb)
     fill_pops(adj_pad, adj, (0, 1, NX - 2, NX - 1), y_low, y_high)
-    fill_pops_outer(adj_pad, x_low, x_high, e_low, e_high)
+    fill_pops_outer(adj_pad, x_low, x_high, 5)
     for d in range(3):
         for x in (0, 1, 2, 3, NX, NX + 1, NX + 2, NX + 3):
             dgrad_pad[d, x] = jnp.zeros((ROWS, NZ), f32)
@@ -561,36 +619,83 @@
     total_out[...] = jnp.concatenate([both[:32], both[32:]], axis=1)
 
 
+SHARE = 4
+
+
 def first_adjoint_kernel(
-    pops, phase, adj, fluid_pad, y_low, y_high, x_low, x_high, e_low, e_high, adj_out, adj_pad
+    start, speed, phase, adj, fluid_pad, ya, yb, xa, xb, *refs
 ):
-    fill_pops(adj_pad, adj, range(NX), y_low, y_high)
-    fill_pops_outer(adj_pad, x_low, x_high, e_low, e_high)
-
-    def plane(x, carry):
-        step_plane(x, adj_pad, fluid_pad, pops, phase, adj_out, None)
+    out, adj_pad, part, sem = refs[-4:]
+    (x_low, x_high), (y_low, y_high) = sides("pipe", xa, xb), sides("cross", ya, yb)
+    planes = range(max(start - 1, 0), min(start + SHARE + 1, NX))
+    fill_pops(adj_pad, adj, planes, y_low, y_high)
+    if start == 0 or start + SHARE == NX:
+        fill_pops_outer(adj_pad, x_low, x_high, 5)
+
+    def plane(k, carry):
+        step_plane(start + k, adj_pad, fluid_pad, speed, phase, part, None, start)
         return carry
 
-    lax.fori_loop(0, NX, plane, 0)
-
-
-def ring(axis, value, step):
+    lax.fori_loop(0, SHARE, plane, 0)
+    (copy,) = fetch([(part, out.at[:, pl.ds(start, SHARE)])], sem)
+    copy.wait()
+
+
+def first_adjoint(start, args, after, before):
+    args = (*args, after) if before is None else (*args, after, before)
+    specs = [pl.BlockSpec(memory_space=pltpu.VMEM)] * 8 + [pl.BlockSpec(memory_space=pl.ANY)] * (len(args) - 8)
+    return pl.pallas_call(
+        functools.partial(first_adjoint_kernel, start),
+        out_shape=jax.ShapeDtypeStruct(*block),
+        in_specs=specs,
+        out_specs=pl.BlockSpec(memory_space=pl.ANY),
+        scratch_shapes=[
+            pltpu.VMEM((19, WX, ROWS, NZ), f32),
+            pltpu.VMEM((19, SHARE, NY, NZ), f32),
+            pltpu.SemaphoreType.DMA((1,)),
+        ],
+        input_output_aliases={} if before is None else {9: 0},
+        compiler_params=pltpu.CompilerParams(vmem_limit_bytes=24 * 1024 * 1024),
+        name="first_adjoint",
+    )(*args)
+
+
+def swap(axis, a, b):
     count = lax.axis_size(axis)
-    return lax.ppermute(value, axis, [(i, (i + step) % count) for i in range(count)])
-
-
-def group_sum(value, axis, stride, size):
-    count = lax.axis_size(axis)
-    got = []
-    for s in range(1, size):
-        pairs = []
-        for i in range(count):
-            digit = (i // stride) % size
-            pairs.append((i, i + ((digit + s) % size - digit) * stride))
-        got.append(lax.ppermute(value, axis, pairs))
-    for part in got:
-        value = value + part
-    return value
+    near = lax.ppermute(a, axis, [(i, i ^ 1) for i in range(count)])
+    far = lax.ppermute(b, axis, [(i, (i + 2 * (i % 2) - 1) % count) for i in range(count)])
+    return near, far
+
+
+def mirror(index, low, size):
+    digit = index // low % size
+    return index + (size - 1 - 2 * digit) * low
+
+
+def sum_rounds():
+    return (
+        lambda p, c: (p ^ 1, c),
+        lambda p, c: (p ^ 3, c),
+        lambda p, c: (mirror(p, 2, 4) ^ 1, c),
+        lambda p, c: (p ^ 1, c ^ 1),
+        lambda p, c: (p ^ 1, mirror(c, 1, 4)),
+        lambda p, c: (p ^ 1, c ^ 4),
+        lambda p, c: (p ^ 1, mirror(c, 4, 4)),
+    )
+
+
+def exchange(value, place):
+    pipe, cross = lax.axis_size("pipe"), lax.axis_size("cross")
+    pairs = []
+    for p in range(pipe):
+        for c in range(cross):
+            q, d = place(p, c)
+            pairs.append((p * cross + c, q * cross + d))
+    return lax.ppermute(value, ("pipe", "cross"), pairs)
+
+
+def pack_pairs(packed):
+    return packed[:2], packed[2:]
 
 
 def shards(
@@ -606,60 +711,53 @@
 ):
     table = wettability.reshape(32, NZ)
     fields = (phase_first, phase_second, fluid, wall, patch)
-    x_up, x_down, y_up, y_down = pack(adjoint_last, fields)
-    x_high, x_low = ring("pipe", x_up, -1), ring("pipe", x_down, 1)
-    y_high, y_low = ring("cross", y_up, -1), ring("cross", y_down, 1)
-    phi, hits, rights = own_terms(table, *fields)
-    e_up, e_down = pack_edges(x_low, x_high, FIELDS, phi)
-    e_high, e_low = ring("cross", e_up, -1), ring("cross", e_down, 1)
-    given = (pops_second, phase_second, adjoint_last, fluid, y_low, y_high)
+    x_swap, y_swap = pack_pairs(pack(adjoint_last, fields))
+    y_halo = swap("cross", *y_swap)
+    phi, hits, rights, wall_own, speed = own_terms(table, *fields, pops_second)
+    x_halo = swap("pipe", *pack_edges(x_swap, y_halo, FIELDS, phi))
+    given = (speed, phase_second, adjoint_last, fluid, *y_halo)
     adjoint, mom = whole_call(
         second_inner_kernel, "second_inner", [block, seven], given, pad_scratch()
     )
-    outer = (x_low, x_high, e_low, e_high)
-    face, side = ((5, NY, NZ), f32), ((5 * NX, NZ), f32)
-    adjoint, mom, x_up, x_down, y_up, y_down = whole_call(
+    face, side = ((7, NY, NZ), f32), ((5 * NX, NZ), f32)
+    adjoint, mom, *packed = whole_call(
         second_outer_kernel,
         "second_outer",
         [block, seven, face, face, side, side],
-        given + outer + (adjoint, mom),
+        given + x_halo + (adjoint, mom),
         pad_scratch(),
-        {10: 0, 11: 1},
-    )
-    x_high2, x_low2 = ring("pipe", x_up, -1), ring("pipe", x_down, 1)
-    y_high2, y_low2 = ring("cross", y_up, -1), ring("cross", y_down, 1)
-    dgrad, grad, fluid_pad, wall_own, wall_face, wall_side, halo_hits, halo_rights = middle(
-        phi, table, fluid, wall, mom, y_low, y_high, *outer
-    )
-    e_up, e_down = pack_edges(x_low2, x_high2, 0, wall_side)
-    e_high2, e_low2 = ring("cross", e_up, -1), ring("cross", e_down, 1)
-    given = (adjoint, fluid_pad, grad, dgrad, y_low2, y_high2)
+        {8: 0, 9: 1},
+    )
+    x_swap, y_swap = pack_pairs(packed)
+    y_halo2 = swap("cross", *y_swap)
+    dgrad, grad, fluid_pad, wall_face, wall_side, halo_hits, halo_rights, speed = middle(
+        phi, table, fluid, mom, *y_halo, *x_halo, pops_first
+    )
+    x_halo2 = swap("pipe", *pack_edges(x_swap, y_halo2, 0, wall_side))
+    given = (adjoint, fluid_pad, grad, dgrad, *y_halo2)
     nodes = (wall_own, hits, rights)
     adj_scratch = pad_scratch()[:1]
     dgrad_scratch = adj_scratch + [pltpu.VMEM((3, WX + 2, ROWS, NZ), f32)]
     dgrad_inner, acc = whole_call(
         first_inner_kernel, "first_inner", [vector, ((128, 64), f32)], given + nodes, dgrad_scratch
     )
-    outer = (x_low2, x_high2, e_low2, e_high2)
     (total,) = whole_call(
         first_outer_kernel,
         "first_outer",
         [((32, NZ), f32)],
-        given + outer + (dgrad_inner, acc) + nodes + (wall_face, wall_side, halo_hits, halo_rights),
+        given + x_halo2 + (dgrad_inner, acc) + nodes + (wall_face, wall_side, halo_hits, halo_rights),
         dgrad_scratch + [pltpu.VMEM((3, WX + 2, NZ), f32)],
     )
-    (adjoint,) = whole_call(
-        first_adjoint_kernel,
-        "first_adjoint",
-        [block],
-        (pops_first, phase_first, adjoint, fluid_pad, y_low2, y_high2, *outer),
-        adj_scratch,
-    )
-    total = group_sum(total, "pipe", 1, 2)
-    total = group_sum(total, "pipe", 2, 4)
-    total = group_sum(total, "cross", 1, 4)
-    total = group_sum(total, "cross", 4, 4)
-    return adjoint, total.reshape(wettability.shape)
+    args = (speed, phase_first, adjoint, fluid_pad, *y_halo2, *x_halo2)
+    result = None
+    for k, place in enumerate(sum_rounds()):
+        got = exchange(total, place)
+        share = k - 2
+        if 0 <= share < NX // SHARE:
+            result = first_adjoint(share * SHARE, args, total, result)
+            got, result = lax.optimization_barrier((got, result))
+        total = total + got
+    return result, total.reshape(wettability.shape)
 
 
 def solution(mesh):

time: 67.5 us -> 58.3 us (0.86)
  the two profiles are of different devices: /device:TPU:0 before, /device:TPU:1 now
where the time goes in v2:
time: 58.3 us; the launch traced here: 58.1 us
  starting transfers between devices  19.7 us (34%)
  Pallas kernels  19 us (33%)
  waiting for transfers between devices  17.1 us (29%)
  between operations  0.89 us (2%)
  local copies, waits for them, and re-layouts  0.75 us (1%)
  other arithmetic  0.63 us (1%)
    ppermute x7, waiting for transfers between devices, exchange(): return lax.ppermute(value, ('pipe', 'cross'), pairs)  16.5 us
    pallas_call x9, Pallas kernels, whole_call(): pl.pallas_call(kernel, out_shape=[pltpu.VMEM(shape, kind) if in_hbm else...  14 us
    ppermute x4, starting transfers between devices, swap(): lax.ppermute(b, axis, [(i, (i + 2 * (i % 2) - 1) % count) for i in range(...  9.39 us
    ppermute x4, starting transfers between devices, swap(): near = lax.ppermute(a, axis, [(i, i ^ 1) for i in range(count)])  5.99 us
    pallas_call x4, Pallas kernels, first_adjoint(): pl.pallas_call(functools.partial(first_adjoint_kernel, start), out_shape=...  4.95 us
    ppermute x7, starting transfers between devices, exchange(): return lax.ppermute(value, ('pipe', 'cross'), pairs)  4.35 us
  transfers between devices with their start and end apart: 15, of which 9 were waited for; matrix products, arithmetic and copies ran while one was open for 0% of the time, Pallas kernels for 28%

profile of v2, /device:TPU:1, one launch (start us, length us, event | category | flops | bytes accessed | tf_op | source)
XLA Modules:
  0.0 58.1 jit_solution(1579121936828639364)
XLA Ops:
  0.7 1.5 %pack.1 = (f32[12,8,128]{2,1,0:T(8,128)S(1)}, f32[12,8,128]{2,1,0:T(8,128)S(1)}, f32[160,128]{1,0:T(8,128)S(1)}, f32[160,128]{1,0:T(8,128)S(1)}) custom-call(f32[19,16,8,128]{3,2,1,0:T(8,128)} %adj.3, f32[16,8,128]{2,1,0:T(8,128)} %phase.11, f32[16,8,128]{2,1,0:T(8,128)} %phase.7, s32[16,8,128]{2,1,0:T(8,128)} %fluid.5, s32[16,8,128]{2,1,0:T(8,128)} %refs_3_.1, ...), custom_call_target="tpu_custom_call" | custom-call | tf_op jit(solution)/shard_map/pack/pallas_call | solution.py:187
  2.2 2.5 %collective-permute-start = (f32[160,128]{1,0:T(8,128)S(1)}, f32[160,128]{1,0:T(8,128)S(1)}, u32[]{:S(2)}, u32[]{:S(2)}) collective-permute-start(f32[160,128]{1,0:T(8,128)S(1)} %get-tuple-element.42), channel_id=1, source_target_pairs={{0,1},{1,0},{2,3},{3,2},{4,5},{5,4},{6,7},{7,6},{8,9},{9,8},{10,11... | collective-permute-start | bytes 245768 | tf_op jit(solution)/shard_map/ppermute | solution.py:665
  4.8 4.4 %collective-permute-start.1 = (f32[160,128]{1,0:T(8,128)S(1)}, f32[160,128]{1,0:T(8,128)S(1)}, u32[]{:S(2)}, u32[]{:S(2)}) collective-permute-start(f32[160,128]{1,0:T(8,128)S(1)} %get-tuple-element.43), channel_id=1, source_target_pairs={{0,15},{1,2},{2,1},{3,4},{4,3},{5,6},{6,5},{7,8},{8,7},{9,10},{10,... | collective-permute-start | bytes 245768 | tf_op jit(solution)/shard_map/ppermute | solution.py:666
  10.0 3.1 %own_terms.1 = (f32[2,16,8,128]{3,2,1,0:T(8,128)S(1)}, bf16[64,16384]{1,0:T(8,128)(2,1)S(1)}, bf16[64,16384]{1,0:T(8,128)(2,1)S(1)}, f32[16,8,128]{2,1,0:T(8,128)S(1)}, f32[3,16,8,128]{3,2,1,0:T(8,128)S(1)}) custom-call(f32[32,128]{1,0:T(8,128)S(1)} %bitcast.3, f32[16,8,128]{2,1,0:T(8,128)S(1)} %copy-done.1, f32[16,8,128]{2,1,0:T(8,128)S(1)} %copy-done.5, ...), custom_call_target="tpu_custom_call" | custom-call | tf_op jit(solution)/shard_map/own_terms/pallas_call | solution.py:187
  13.1 1.3 %collective-permute-start.2 = (f32[12,8,128]{2,1,0:T(8,128)S(1)}, f32[12,8,128]{2,1,0:T(8,128)S(1)}, u32[]{:S(2)}, u32[]{:S(2)}) collective-permute-start(f32[12,8,128]{2,1,0:T(8,128)S(1)} %get-tuple-element.47), channel_id=1, source_target_pairs={{0,16},{16,0},{32,48},{48,32},{64,80},{80,64},{96,112},{112,96},{1... | collective-permute-start | bytes 147464 | tf_op jit(solution)/shard_map/ppermute | solution.py:665
  14.4 1.3 %collective-permute-start.3 = (f32[12,8,128]{2,1,0:T(8,128)S(1)}, f32[12,8,128]{2,1,0:T(8,128)S(1)}, u32[]{:S(2)}, u32[]{:S(2)}) collective-permute-start(f32[12,8,128]{2,1,0:T(8,128)S(1)} %get-tuple-element.48), channel_id=1, source_target_pairs={{0,112},{16,32},{32,16},{48,64},{64,48},{80,96},{96,80},{112,0},{1... | collective-permute-start | bytes 147464 | tf_op jit(solution)/shard_map/ppermute | solution.py:666
  15.7 1.7 %second_inner.1 = (f32[19,16,8,128]{3,2,1,0:T(8,128)S(1)}, f32[7,16,8,128]{3,2,1,0:T(8,128)S(1)}) custom-call(f32[3,16,8,128]{3,2,1,0:T(8,128)S(1)} %get-tuple-element.41.speed, f32[16,8,128]{2,1,0:T(8,128)S(1)} %copy-done.5, f32[19,16,8,128]{3,2,1,0:T(8,128)S(1)} %copy-done, s32[16,8,128]{2,1,0:T(8,128)S(1)} %copy-done.2, ...), custom_call_target="tpu_custom_call" | custom-call | tf_op jit(solution)/shard_map/second_inner/pallas_call | solution.py:187
  18.2 3.7 %collective-permute-start.5 = (f32[80,128]{1,0:T(8,128)S(1)}, f32[80,128]{1,0:T(8,128)S(1)}, u32[]{:S(2)}, u32[]{:S(2)}) collective-permute-start(f32[80,128]{1,0:T(8,128)S(1)} %get-tuple-element.57), channel_id=1, source_target_pairs={{0,15},{1,2},{2,1},{3,4},{4,3},{5,6},{6,5},{7,8},{8,7},{9,10},{10,... | collective-permute-start | bytes 122888 | tf_op jit(solution)/shard_map/ppermute | solution.py:666
  21.9 3.1 %middle.1 = (f32[3,16,8,128]{3,2,1,0:T(8,128)S(1)}, f32[3,16,8,128]{3,2,1,0:T(8,128)S(1)}, f32[18,24,128]{2,1,0:T(8,128)S(1)}, f32[2,8,128]{2,1,0:T(8,128)S(1)},...) custom-call(f32[2,16,8,128]{3,2,1,0:T(8,128)S(1)} %get-tuple-element, ...), custom_call_target="tpu_custom_call" | custom-call | tf_op jit(solution)/shard_map/middle/pallas_call | solution.py:187
  25.1 2.0 %collective-permute-start.6 = (f32[7,8,128]{2,1,0:T(8,128)S(1)}, f32[7,8,128]{2,1,0:T(8,128)S(1)}, u32[]{:S(2)}, u32[]{:S(2)}) collective-permute-start(f32[7,8,128]{2,1,0:T(8,128)S(1)} %get-tuple-element.61), channel_id=1, source_target_pairs={{0,16},{16,0},{32,48},{48,32},{64,80},{80,64},{96,112},{112,96},{1... | collective-permute-start | bytes 86024 | tf_op jit(solution)/shard_map/ppermute | solution.py:665
  27.1 3.2 %first_inner.1 = (f32[3,16,8,128]{3,2,1,0:T(8,128)S(1)}, f32[128,64]{1,0:T(8,128)S(1)}) custom-call(f32[19,16,8,128]{3,2,1,0:T(8,128)S(1)} %get-tuple-element.51.adj, f32[18,24,128]{2,1,0:T(8,128)S(1)} %get-tuple-element.53.fluid_pad, f32[3,16,8,128]{3,2,1,0:T(8,128)S(1)} %get-tuple-element.54.grad, f32[3,16,8,128]{3,2,1,0:T(8,128)S(1)} %get-tuple-element.55.dgrad_in, ...), custom_call_target="tpu_custom_call" | custom-call | tf_op jit(solution)/shard_map/first_inner/pallas_call | solution.py:187
  30.4 1.1 %first_outer.1 = f32[32,128]{1,0:T(8,128)S(1)} custom-call(f32[19,16,8,128]{3,2,1,0:T(8,128)S(1)} %get-tuple-element.51.adj, f32[18,24,128]{2,1,0:T(8,128)S(1)} %get-tuple-element.53.fluid_pad, f32[3,16,8,128]{3,2,1,0:T(8,128)S(1)} %get-tuple-element.54.grad, f32[3,16,8,128]{3,2,1,0:T(8,128)S(1)} %get-tuple-element.55.dgrad_in, ...), custom_call_target="tpu_custom_call" | custom-call | tf_op jit(solution)/shard_map/first_outer/pallas_call | solution.py:187
  31.6 2.4 %collective-permute-start.8 = (f32[32,128]{1,0:T(8,128)S(1)}, f32[32,128]{1,0:T(8,128)S(1)}, u32[]{:S(2)}, u32[]{:S(2)}) collective-permute-start(f32[32,128]{1,0:T(8,128)S(1)} %first_outer.1), channel_id=1, source_target_pairs={{0,16},{1,17},{2,18},{3,19},{4,20},{5,21},{6,22},{7,23},{8,24},{9,... | collective-permute-start | bytes 49160 | tf_op jit(solution)/shard_map/ppermute | solution.py:694
  34.8 3.2 %collective-permute-done.9 = f32[32,128]{1,0:T(8,128)S(1)} collective-permute-done((f32[32,128]{1,0:T(8,128)S(1)}, f32[32,128]{1,0:T(8,128)S(1)}, u32[]{:S(2)}, u32[]{:S(2)}) %collective-permute-start.9) | collective-permute-done | bytes 16416 | tf_op jit(solution)/shard_map/ppermute | solution.py:694
  38.0 1.3 %collective-permute-start.10 = (f32[32,128]{1,0:T(8,128)S(1)}, f32[32,128]{1,0:T(8,128)S(1)}, u32[]{:S(2)}, u32[]{:S(2)}) collective-permute-start(f32[32,128]{1,0:T(8,128)S(1)} %add.22.refs_0_), channel_id=1, source_target_pairs={{0,112},{1,113},{2,114},{3,115},{4,116},{5,117},{6,118},{7,119},{8... | collective-permute-start | bytes 49160 | tf_op jit(solution)/shard_map/ppermute | solution.py:694
  39.3 1.2 %first_adjoint.4.refs_1_ = f32[19,16,8,128]{3,2,1,0:T(8,128)} custom-call(f32[3,16,8,128]{3,2,1,0:T(8,128)S(1)} %get-tuple-element.71.speed, f32[16,8,128]{2,1,0:T(8,128)S(1)} %copy-done.1, f32[19,16,8,128]{3,2,1,0:T(8,128)S(1)} %get-tuple-element.51.adj, f32[18,24,128]{2,1,0:T(8,128)S(1)} %get-tuple-element.53.fluid_pad, ...), custom_call_target="tpu_custom_call" | custom-call | tf_op jit(solution)/shard_map/first_adjoint/pallas_call | solution.py:647
  40.5 1.8 %collective-permute-done.10 = f32[32,128]{1,0:T(8,128)S(1)} collective-permute-done((f32[32,128]{1,0:T(8,128)S(1)}, f32[32,128]{1,0:T(8,128)S(1)}, u32[]{:S(2)}, u32[]{:S(2)}) %collective-permute-start.10) | collective-permute-done | bytes 16416 | tf_op jit(solution)/shard_map/ppermute | solution.py:694
  42.4 1.2 %first_adjoint.5.refs_1_ = f32[19,16,8,128]{3,2,1,0:T(8,128)} custom-call(f32[3,16,8,128]{3,2,1,0:T(8,128)S(1)} %get-tuple-element.71.speed, f32[16,8,128]{2,1,0:T(8,128)S(1)} %copy-done.1, f32[19,16,8,128]{3,2,1,0:T(8,128)S(1)} %get-tuple-element.51.adj, f32[18,24,128]{2,1,0:T(8,128)S(1)} %get-tuple-element.53.fluid_pad, ...), custom_call_target="tpu_custom_call", output_to_operand_aliasing={{}: (9, {})} | custom-call | tf_op jit(solution)/shard_map/first_adjoint/pallas_call | solution.py:647
  43.6 1.9 %collective-permute-done.11 = f32[32,128]{1,0:T(8,128)S(1)} collective-permute-done((f32[32,128]{1,0:T(8,128)S(1)}, f32[32,128]{1,0:T(8,128)S(1)}, u32[]{:S(2)}, u32[]{:S(2)}) %collective-permute-start.11) | collective-permute-done | bytes 16416 | tf_op jit(solution)/shard_map/ppermute | solution.py:694
  45.5 1.2 %first_adjoint.6.refs_1_ = f32[19,16,8,128]{3,2,1,0:T(8,128)} custom-call(f32[3,16,8,128]{3,2,1,0:T(8,128)S(1)} %get-tuple-element.71.speed, f32[16,8,128]{2,1,0:T(8,128)S(1)} %copy-done.1, f32[19,16,8,128]{3,2,1,0:T(8,128)S(1)} %get-tuple-element.51.adj, f32[18,24,128]{2,1,0:T(8,128)S(1)} %get-tuple-element.53.fluid_pad, ...), custom_call_target="tpu_custom_call", output_to_operand_aliasing={{}: (9, {})} | custom-call | tf_op jit(solution)/shard_map/first_adjoint/pallas_call | solution.py:647
  46.8 3.1 %collective-permute-done.12 = f32[32,128]{1,0:T(8,128)S(1)} collective-permute-done((f32[32,128]{1,0:T(8,128)S(1)}, f32[32,128]{1,0:T(8,128)S(1)}, u32[]{:S(2)}, u32[]{:S(2)}) %collective-permute-start.12) | collective-permute-done | bytes 16416 | tf_op jit(solution)/shard_map/ppermute | solution.py:694
  49.9 1.2 %first_adjoint.7 = f32[19,16,8,128]{3,2,1,0:T(8,128)} custom-call(f32[3,16,8,128]{3,2,1,0:T(8,128)S(1)} %get-tuple-element.71.speed, f32[16,8,128]{2,1,0:T(8,128)S(1)} %copy-done.1, f32[19,16,8,128]{3,2,1,0:T(8,128)S(1)} %get-tuple-element.51.adj, f32[18,24,128]{2,1,0:T(8,128)S(1)} %get-tuple-element.53.fluid_pad, ...), custom_call_target="tpu_custom_call", output_to_operand_aliasing={{}: (9, {})} | custom-call | tf_op jit(solution)/shard_map/first_adjoint/pallas_call | solution.py:647
  51.2 1.9 %collective-permute-done.13 = f32[32,128]{1,0:T(8,128)S(1)} collective-permute-done((f32[32,128]{1,0:T(8,128)S(1)}, f32[32,128]{1,0:T(8,128)S(1)}, u32[]{:S(2)}, u32[]{:S(2)}) %collective-permute-start.13) | collective-permute-done | bytes 16416 | tf_op jit(solution)/shard_map/ppermute | solution.py:694
  53.7 3.7 %collective-permute-done.14 = f32[32,128]{1,0:T(8,128)S(1)} collective-permute-done((f32[32,128]{1,0:T(8,128)S(1)}, f32[32,128]{1,0:T(8,128)S(1)}, u32[]{:S(2)}, u32[]{:S(2)}) %collective-permute-start.14) | collective-permute-done | bytes 16416 | tf_op jit(solution)/shard_map/ppermute | solution.py:694
  (44 shorter events, 3.8 us)
Async XLA Ops:
  0.6 8.6 %copy-start.1 = (f32[16,8,128]{2,1,0:T(8,128)S(1)}, f32[16,8,128]{2,1,0:T(8,128)}, u32[]{:S(2)}) copy-start(f32[16,8,128]{2,1,0:T(8,128)} %phase.11) | copy-start | bytes 196612
  0.6 8.6 %copy-start.2 = (s32[16,8,128]{2,1,0:T(8,128)S(1)}, s32[16,8,128]{2,1,0:T(8,128)}, u32[]{:S(2)}) copy-start(s32[16,8,128]{2,1,0:T(8,128)} %fluid.5) | copy-start | bytes 196612
  0.7 8.6 %copy-start.5 = (f32[16,8,128]{2,1,0:T(8,128)S(1)}, f32[16,8,128]{2,1,0:T(8,128)}, u32[]{:S(2)}) copy-start(f32[16,8,128]{2,1,0:T(8,128)} %phase.7) | copy-start | bytes 196612
  0.7 8.6 %copy-start.7 = (s32[16,8,128]{2,1,0:T(8,128)S(1)}, s32[16,8,128]{2,1,0:T(8,128)}, u32[]{:S(2)}) copy-start(s32[16,8,128]{2,1,0:T(8,128)} %refs_4_.1) | copy-start | bytes 196612
  0.7 8.5 %copy-start.6 = (s32[16,8,128]{2,1,0:T(8,128)S(1)}, s32[16,8,128]{2,1,0:T(8,128)}, u32[]{:S(2)}) copy-start(s32[16,8,128]{2,1,0:T(8,128)} %refs_3_.1) | copy-start | bytes 196612
  0.7 8.5 %copy-start.3 = (f32[19,16,8,128]{3,2,1,0:T(8,128)S(1)}, f32[19,16,8,128]{3,2,1,0:T(8,128)}, u32[]{:S(2)}) copy-start(f32[19,16,8,128]{3,2,1,0:T(8,128)} %pops_hbm.2) | copy-start | bytes 3735556
  2.2 13.5 %copy-start = (f32[19,16,8,128]{3,2,1,0:T(8,128)S(1)}, f32[19,16,8,128]{3,2,1,0:T(8,128)}, u32[]{:S(2)}) copy-start(f32[19,16,8,128]{3,2,1,0:T(8,128)} %adj.3) | copy-start | bytes 3735556
  2.2 10.8 %collective-permute-start = (f32[160,128]{1,0:T(8,128)S(1)}, f32[160,128]{1,0:T(8,128)S(1)}, u32[]{:S(2)}, u32[]{:S(2)}) collective-permute-start(f32[160,128]{1,0:T(8,128)S(1)} %get-tuple-element.42), channel_id=1, source_target_pairs={{0,1},{1,0},{2,3},{3,2},{4,5},{5,4},{6,7},{7,6},{8,9},{9,8},{10,11... | collective-permute-start | bytes 245768 | tf_op jit(solution)/shard_map/ppermute | solution.py:665
  4.8 8.3 %collective-permute-start.1 = (f32[160,128]{1,0:T(8,128)S(1)}, f32[160,128]{1,0:T(8,128)S(1)}, u32[]{:S(2)}, u32[]{:S(2)}) collective-permute-start(f32[160,128]{1,0:T(8,128)S(1)} %get-tuple-element.43), channel_id=1, source_target_pairs={{0,15},{1,2},{2,1},{3,4},{4,3},{5,6},{6,5},{7,8},{8,7},{9,10},{10,... | collective-permute-start | bytes 245768 | tf_op jit(solution)/shard_map/ppermute | solution.py:666
  9.2 0.7 %copy-start.8 = (f32[4096]{0:T(1024)S(1)}, f32[4096]{0:T(1024)}, u32[]{:S(2)}) copy-start(f32[4096]{0:T(1024)} %param.14) | copy-start | bytes 49156
  13.1 4.3 %collective-permute-start.2 = (f32[12,8,128]{2,1,0:T(8,128)S(1)}, f32[12,8,128]{2,1,0:T(8,128)S(1)}, u32[]{:S(2)}, u32[]{:S(2)}) collective-permute-start(f32[12,8,128]{2,1,0:T(8,128)S(1)} %get-tuple-element.47), channel_id=1, source_target_pairs={{0,16},{16,0},{32,48},{48,32},{64,80},{80,64},{96,112},{112,96},{1... | collective-permute-start | bytes 147464 | tf_op jit(solution)/shard_map/ppermute | solution.py:665
  14.4 3.5 %collective-permute-start.3 = (f32[12,8,128]{2,1,0:T(8,128)S(1)}, f32[12,8,128]{2,1,0:T(8,128)S(1)}, u32[]{:S(2)}, u32[]{:S(2)}) collective-permute-start(f32[12,8,128]{2,1,0:T(8,128)S(1)} %get-tuple-element.48), channel_id=1, source_target_pairs={{0,112},{16,32},{32,16},{48,64},{64,48},{80,96},{96,80},{112,0},{1... | collective-permute-start | bytes 147464 | tf_op jit(solution)/shard_map/ppermute | solution.py:666
  18.0 3.9 %copy-start.4 = (f32[19,16,8,128]{3,2,1,0:T(8,128)S(1)}, f32[19,16,8,128]{3,2,1,0:T(8,128)}, u32[]{:S(2)}) copy-start(f32[19,16,8,128]{3,2,1,0:T(8,128)} %pops_hbm.3) | copy-start | bytes 3735556
  18.1 6.9 %collective-permute-start.4 = (f32[80,128]{1,0:T(8,128)S(1)}, f32[80,128]{1,0:T(8,128)S(1)}, u32[]{:S(2)}, u32[]{:S(2)}) collective-permute-start(f32[80,128]{1,0:T(8,128)S(1)} %get-tuple-element.56), channel_id=1, source_target_pairs={{0,1},{1,0},{2,3},{3,2},{4,5},{5,4},{6,7},{7,6},{8,9},{9,8},{10,11... | collective-permute-start | bytes 122888 | tf_op jit(solution)/shard_map/ppermute | solution.py:665
  18.2 6.8 %collective-permute-start.5 = (f32[80,128]{1,0:T(8,128)S(1)}, f32[80,128]{1,0:T(8,128)S(1)}, u32[]{:S(2)}, u32[]{:S(2)}) collective-permute-start(f32[80,128]{1,0:T(8,128)S(1)} %get-tuple-element.57), channel_id=1, source_target_pairs={{0,15},{1,2},{2,1},{3,4},{4,3},{5,6},{6,5},{7,8},{8,7},{9,10},{10,... | collective-permute-start | bytes 122888 | tf_op jit(solution)/shard_map/ppermute | solution.py:666
  25.1 5.2 %collective-permute-start.6 = (f32[7,8,128]{2,1,0:T(8,128)S(1)}, f32[7,8,128]{2,1,0:T(8,128)S(1)}, u32[]{:S(2)}, u32[]{:S(2)}) collective-permute-start(f32[7,8,128]{2,1,0:T(8,128)S(1)} %get-tuple-element.61), channel_id=1, source_target_pairs={{0,16},{16,0},{32,48},{48,32},{64,80},{80,64},{96,112},{112,96},{1... | collective-permute-start | bytes 86024 | tf_op jit(solution)/shard_map/ppermute | solution.py:665
  27.1 3.3 %collective-permute-start.7 = (f32[7,8,128]{2,1,0:T(8,128)S(1)}, f32[7,8,128]{2,1,0:T(8,128)S(1)}, u32[]{:S(2)}, u32[]{:S(2)}) collective-permute-start(f32[7,8,128]{2,1,0:T(8,128)S(1)} %get-tuple-element.62), channel_id=1, source_target_pairs={{0,112},{16,32},{32,16},{48,64},{64,48},{80,96},{96,80},{112,0},{1... | collective-permute-start | bytes 86024 | tf_op jit(solution)/shard_map/ppermute | solution.py:666
  31.6 3.3 %collective-permute-start.8 = (f32[32,128]{1,0:T(8,128)S(1)}, f32[32,128]{1,0:T(8,128)S(1)}, u32[]{:S(2)}, u32[]{:S(2)}) collective-permute-start(f32[32,128]{1,0:T(8,128)S(1)} %first_outer.1), channel_id=1, source_target_pairs={{0,16},{1,17},{2,18},{3,19},{4,20},{5,21},{6,22},{7,23},{8,24},{9,... | collective-permute-start | bytes 49160 | tf_op jit(solution)/shard_map/ppermute | solution.py:694
  34.8 3.2 %collective-permute-start.9 = (f32[32,128]{1,0:T(8,128)S(1)}, f32[32,128]{1,0:T(8,128)S(1)}, u32[]{:S(2)}, u32[]{:S(2)}) collective-permute-start(f32[32,128]{1,0:T(8,128)S(1)} %add.21), channel_id=1, source_target_pairs={{0,48},{1,49},{2,50},{3,51},{4,52},{5,53},{6,54},{7,55},{8,56},{9,... | collective-permute-start | bytes 49160 | tf_op jit(solution)/shard_map/ppermute | solution.py:694
  38.0 4.4 %collective-permute-start.10 = (f32[32,128]{1,0:T(8,128)S(1)}, f32[32,128]{1,0:T(8,128)S(1)}, u32[]{:S(2)}, u32[]{:S(2)}) collective-permute-start(f32[32,128]{1,0:T(8,128)S(1)} %add.22.refs_0_), channel_id=1, source_target_pairs={{0,112},{1,113},{2,114},{3,115},{4,116},{5,117},{6,118},{7,119},{8... | collective-permute-start | bytes 49160 | tf_op jit(solution)/shard_map/ppermute | solution.py:694
  42.4 3.2 %collective-permute-start.11 = (f32[32,128]{1,0:T(8,128)S(1)}, f32[32,128]{1,0:T(8,128)S(1)}, u32[]{:S(2)}, u32[]{:S(2)}) collective-permute-start(f32[32,128]{1,0:T(8,128)S(1)} %add.23.refs_0_), channel_id=1, source_target_pairs={{0,17},{1,16},{2,19},{3,18},{4,21},{5,20},{6,23},{7,22},{8,25},{9,... | collective-permute-start | bytes 49160 | tf_op jit(solution)/shard_map/ppermute | solution.py:694
  45.5 4.4 %collective-permute-start.12 = (f32[32,128]{1,0:T(8,128)S(1)}, f32[32,128]{1,0:T(8,128)S(1)}, u32[]{:S(2)}, u32[]{:S(2)}) collective-permute-start(f32[32,128]{1,0:T(8,128)S(1)} %add.24.refs_0_), channel_id=1, source_target_pairs={{0,19},{1,18},{2,17},{3,16},{4,23},{5,22},{6,21},{7,20},{8,27},{9,... | collective-permute-start | bytes 49160 | tf_op jit(solution)/shard_map/ppermute | solution.py:694
  49.9 3.2 %collective-permute-start.13 = (f32[32,128]{1,0:T(8,128)S(1)}, f32[32,128]{1,0:T(8,128)S(1)}, u32[]{:S(2)}, u32[]{:S(2)}) collective-permute-start(f32[32,128]{1,0:T(8,128)S(1)} %add.25.refs_0_), channel_id=1, source_target_pairs={{0,20},{1,21},{2,22},{3,23},{4,16},{5,17},{6,18},{7,19},{8,28},{9,... | collective-permute-start | bytes 49160 | tf_op jit(solution)/shard_map/ppermute | solution.py:694
  53.1 4.4 %collective-permute-start.14 = (f32[32,128]{1,0:T(8,128)S(1)}, f32[32,128]{1,0:T(8,128)S(1)}, u32[]{:S(2)}, u32[]{:S(2)}) collective-permute-start(f32[32,128]{1,0:T(8,128)S(1)} %add.26), channel_id=1, source_target_pairs={{0,28},{1,29},{2,30},{3,31},{4,24},{5,25},{6,26},{7,27},{8,20},{9,... | collective-permute-start | bytes 49160 | tf_op jit(solution)/shard_map/ppermute | solution.py:694

commit v3 on v2

--- a/solution.py
+++ b/solution.py
@@ -43,12 +43,14 @@
 WX = NX + 2
 LOW = 8
 ROWS = 24
+EXTRA = 33
+OWN_EXTRA = 5
 FIELDS = 5
 f32 = jnp.float32
 
 
-def tile(ref, lead, x, move):
-    index = lead + (x + 1 + move[0], pl.ds(LOW + move[1], NY), slice(None))
+def tile(ref, lead, x, move, low=LOW):
+    index = lead + (x + 1 + move[0], pl.ds(low + move[1], NY), slice(None))
     value = ref[index]
     if move[2]:
         value = pltpu.roll(value, (-move[2]) % NZ, 1)
@@ -238,50 +240,102 @@
     return copies
 
 
+def along(x, y):
+    return [i for i in range(19) if lattice_vel[i][:2] == (x, y)]
+
+
+def corner_rows(adj, fluid, speed, side, sign):
+    x, step = ((0, 1), (NX - 1, -1))[side]
+    y = 0 if sign > 0 else NY - 1
+    flat = adj.reshape(19 * NX * NY, NZ)
+    rows = [flat[pl.ds(x * NY + y, 19, stride=NX * NY), :]]
+    rows += [speed[d][y : y + 1, :] for d in range(3)]
+
+    def row(ref, lead, a, b):
+        return ref[lead + (a, pl.ds(b, 1), slice(None))].astype(f32)
+
+    rows += [row(adj, (p,), x + step, y) for p in along(step, 0)]
+    rows += [row(adj, (p,), x, y + sign) for p in along(0, sign)]
+    (diagonal,) = along(step, sign)
+    rows += [row(adj, (diagonal,), x + step, y + sign), row(adj, (diagonal,), x, y + sign)]
+    return rows + [row(fluid, (), x, y + sign), row(fluid, (), x + step, y + sign), row(fluid, (), x + step, y)]
+
+
 def pack_kernel(adj_hbm, *refs):
-    hbm, (xa, xb, ya, yb), (adj, *fields) = refs[:FIELDS], refs[FIELDS : FIELDS + 4], refs[FIELDS + 4 : -1]
-    for copy in fetch([(adj_hbm, adj), *zip(hbm, fields)], refs[-1]):
+    hbm, pops_hbm, (xa, xb, ya, yb) = refs[:FIELDS], refs[FIELDS], refs[FIELDS + 1 : FIELDS + 5]
+    adj, *fields = refs[FIELDS + 5 : -2]
+    pops, sem = refs[-2:]
+    pairs = [(adj_hbm, adj), *zip(hbm, fields)]
+    pairs += [(pops_hbm.at[:, x], pops.at[:, k]) for k, x in enumerate((0, NX - 1))]
+    for copy in fetch(pairs, sem):
         copy.wait()
     put_pops(adj, (xa, xb), (ya, yb))
     odd_x, odd_y = is_odd("pipe"), is_odd("cross")
     for k in range(FIELDS):
         put(odd_x, (xa, xb), 5 + k, fields[k][0].astype(f32), fields[k][NX - 1].astype(f32))
         put_rows(odd_y, (ya, yb), 5 + k, fields[k].reshape(NX * NY, NZ), 0, NY - 1)
-
-
-def pack(adjoint, fields):
-    face, side = ((5 + FIELDS + 2, NY, NZ), f32), (((5 + FIELDS) * NX, NZ), f32)
+    fluid = fields[2]
+    for side in range(2):
+        speed = velocity([pops[i, side] for i in range(19)])
+        at = (5 + FIELDS) * NX + side * EXTRA
+        for up, down in zip(*[corner_rows(adj, fluid, speed, side, sign) for sign in (1, -1)]):
+            put(odd_y, (ya, yb), (pl.ds(at, up.shape[0]), slice(None)), up, down)
+            at += up.shape[0]
+    flats = [ref.reshape(X_PLANES * NY, NZ) for ref in (xa, xb)]
+    for e, sign in enumerate((1, -1)):
+        y = NY - 1 if sign > 0 else 0
+        both = []
+        for x, step in ((0, 1), (NX - 1, -1)):
+            rows = [adj[p, x, pl.ds(y, 1), :] for p in along(0, -sign)]
+            rows += [adj[p, x + step, pl.ds(y, 1), :] for p in along(step, -sign)]
+            both.append(rows + [fluid[x + step, pl.ds(y, 1), :].astype(f32)])
+        for k, (up, down) in enumerate(zip(*both)):
+            put(odd_x, flats, (pl.ds(corner_at(e) + EXTRA + k, 1), slice(None)), up, down)
+
+
+X_PLANES = 5 + FIELDS + 2 + 10
+
+
+def corner_at(e):
+    return (5 + FIELDS + 2 + 5 * e) * NY
+
+
+def pack(adjoint, fields, pops):
+    face, side = ((X_PLANES, NY, NZ), f32), (((5 + FIELDS) * NX + 2 * EXTRA, NZ), f32)
     scratch = [pltpu.VMEM((19, NX, NY, NZ), f32)]
     scratch += [pltpu.VMEM((NX, NY, NZ), field.dtype) for field in fields]
-    scratch.append(pltpu.SemaphoreType.DMA((1 + FIELDS,)))
-    return whole_call(pack_kernel, "pack", [face, face, side, side], (adjoint, *fields), scratch, in_hbm=True)
+    scratch.append(pltpu.VMEM((19, 2, NY, NZ), f32))
+    scratch.append(pltpu.SemaphoreType.DMA((3 + FIELDS,)))
+    return whole_call(pack_kernel, "pack", [face, face, side, side], (adjoint, *fields, pops), scratch, in_hbm=True)
 
 
 edge_plus = (7, 9)
 edge_minus = (10, 8)
 
 
-def pack_edges_kernel(count, xa, xb, ya, yb, _, xa_out, xb_out):
-    planes = 5 + count
-    for k in range(planes):
+def pack_edges_kernel(xa, xb, ya, yb, _, xa_out, xb_out):
+    planes = 5 + FIELDS
+    for k in [*range(planes), *range(planes + 2, X_PLANES)]:
         xa_out[k] = xa[k]
         xb_out[k] = xb[k]
     low, high = sides("cross", ya, yb)
     odd = is_odd("pipe")
+    flats = [ref.reshape(X_PLANES * NY, NZ) for ref in (xa_out, xb_out)]
     for e, (rows, pops) in enumerate(((high, y_plus), (low, y_minus))):
         xa_out[planes + e] = jnp.zeros((NY, NZ), f32)
         xb_out[planes + e] = jnp.zeros((NY, NZ), f32)
-        starts = [(pops.index(edge_plus[e]), pops.index(edge_minus[e]))] + [(5 + k, 5 + k) for k in range(count)]
+        starts = [(pops.index(edge_plus[e]), pops.index(edge_minus[e]))] + [(5 + k, 5 + k) for k in range(FIELDS)]
         for r, (up, down) in enumerate(starts):
             up_row = rows[pl.ds(up * NX, 1), :]
             down_row = rows[pl.ds(down * NX + NX - 1, 1), :]
             put(odd, (xa_out, xb_out), (planes + e, pl.ds(r, 1), slice(None)), up_row, down_row)
-
-
-def pack_edges(x_pair, y_halo, count, after):
-    out = ((5 + count + 2, NY, NZ), f32)
-    kernel = functools.partial(pack_edges_kernel, count)
-    return whole_call(kernel, "pack_edges", [out, out], (*x_pair, *y_halo, after))
+        up, down = [rows[pl.ds(planes * NX + side * EXTRA, EXTRA), :] for side in range(2)]
+        put(odd, flats, (pl.ds(corner_at(e), EXTRA), slice(None)), up, down)
+
+
+def pack_edges(x_pair, y_halo, after):
+    out = ((X_PLANES, NY, NZ), f32)
+    return whole_call(pack_edges_kernel, "pack_edges", [out, out], (*x_pair, *y_halo, after))
 
 
 def fill_sides(pad, lead, y_low, low_slot, y_high, high_slot):
@@ -300,13 +354,17 @@
             pad[y_plus[k], x + 1, pl.ds(LOW + NY, 1), :] = y_high[pl.ds(k * NX + x, 1), :]
 
 
-def fill_pops_outer(pad, x_low, x_high, planes):
+def fill_pops_outer(pad, x_low, x_high, edge):
     for k in range(5):
         pad[x_minus[k], 0, pl.ds(LOW, NY), :] = x_low[k]
         pad[x_plus[k], WX - 1, pl.ds(LOW, NY), :] = x_high[k]
     for e, row in enumerate((LOW + NY, LOW - 1)):
-        pad[edge_minus[e], 0, pl.ds(row, 1), :] = x_low[planes + e, pl.ds(0, 1), :]
-        pad[edge_plus[e], WX - 1, pl.ds(row, 1), :] = x_high[planes + e, pl.ds(0, 1), :]
+        pad[edge_minus[e], 0, pl.ds(row, 1), :] = edge(0, e)
+        pad[edge_plus[e], WX - 1, pl.ds(row, 1), :] = edge(1, e)
+
+
+def edge_of(edges):
+    return lambda side, e: edges[pl.ds(2 * side + e, 1), :]
 
 
 def fill_field(pad, lead, own, slot, y_low, y_high):
@@ -322,13 +380,13 @@
             pad[lead + (x, pl.ds(row, 1), slice(None))] = face[5 + FIELDS + e, pl.ds(1 + slot, 1), :]
 
 
-def propagate_back(adj_pad, fluid_pad, x):
-    here = tile(fluid_pad, (), x, (0, 0, 0))
-    post = [here * adj_pad[0, x + 1, pl.ds(LOW, NY), :]]
+def propagate_back(adj_pad, fluid_pad, x, low=LOW):
+    here = tile(fluid_pad, (), x, (0, 0, 0), low)
+    post = [here * adj_pad[0, x + 1, pl.ds(low, NY), :]]
     for i in range(1, 19):
-        ahead = tile(fluid_pad, (), x, lattice_vel[i])
-        moved = tile(adj_pad, (i,), x, lattice_vel[i])
-        back = adj_pad[opposite[i], x + 1, pl.ds(LOW, NY), :]
+        ahead = tile(fluid_pad, (), x, lattice_vel[i], low)
+        moved = tile(adj_pad, (i,), x, lattice_vel[i], low)
+        back = adj_pad[opposite[i], x + 1, pl.ds(low, NY), :]
         post.append(here * jnp.where(ahead != 0.0, moved, back))
     return post
 
@@ -359,7 +417,7 @@
         step_plane(x, adj_pad, fluid_pad, speed, phase, adj_out, mom_out)
         return carry
 
-    lax.fori_loop(1, NX - 1, plane, 0)
+    lax.fori_loop(1, NX - 1, plane, 0, unroll=2)
 
 
 block = ((19, NX, NY, NZ), f32)
@@ -371,18 +429,76 @@
     return [pltpu.VMEM((19, WX, ROWS, NZ), f32), pltpu.VMEM((WX, ROWS, NZ), f32)]
 
 
+def corner_edges(adj, fluid, y_sides, x_sides, edges_out, corner_pad, corner_fluid):
+    base = (5 + FIELDS) * NX
+    for side, face in enumerate(x_sides):
+        sx = (-1, 1)[side]
+        x = (0, NX - 1)[side]
+        near, far = 1 - sx, 1 + sx
+        pad, wet = corner_pad.at[side], corner_fluid.at[side]
+        flat = Pick(face.first, *[ref.reshape(X_PLANES * NY, NZ) for ref in (face.a, face.b)])
+        for e, (rows, sy) in enumerate(zip(y_sides, (1, -1))):
+            at = LOW + NY if sy > 0 else LOW - 1
+            inner_y = NY - 1 if sy > 0 else 0
+            first = corner_at(e)
+
+            def got(r):
+                return flat[pl.ds(first + r, 1), :]
+
+            def beside(r):
+                return rows[pl.ds(base + side * EXTRA + r, 1), :]
+
+            def set_pops(pops, plane, row, values):
+                for p, value in zip(pops, values):
+                    pad[p, plane, pl.ds(row, 1), :] = value
+
+            set_pops(range(19), 1, at, [got(r) for r in range(19)])
+            set_pops(along(sx, 0), far, at, [got(22 + r) for r in range(3)])
+            set_pops(along(0, sy), 1, at + sy, [got(25 + r) for r in range(3)])
+            set_pops(along(sx, sy), far, at + sy, [got(28)])
+            set_pops(along(-sx, 0), near, at, [beside(p) for p in along(-sx, 0)])
+            set_pops(along(-sx, sy), near, at + sy, [beside(29)])
+            set_pops(along(0, -sy), 1, at - sy, [got(EXTRA + r) for r in range(3)])
+            set_pops(along(sx, -sy), far, at - sy, [got(EXTRA + 3)])
+            set_pops(along(-sx, -sy), near, at - sy, [adj[p, x, pl.ds(inner_y, 1), :] for p in along(-sx, -sy)])
+            for plane, row, value in (
+                (1, at, face[5 + FIELDS + e, pl.ds(3, 1), :]),
+                (far, at, got(32)),
+                (1, at + sy, got(30)),
+                (far, at + sy, got(31)),
+                (near, at, rows[pl.ds((5 + 2) * NX + x, 1), :]),
+                (near, at + sy, beside(30)),
+                (1, at - sy, face[5 + 2, pl.ds(inner_y, 1), :]),
+                (far, at - sy, got(EXTRA + 4)),
+                (near, at - sy, fluid[x, pl.ds(inner_y, 1), :].astype(f32)),
+            ):
+                wet[plane, pl.ds(row, 1), :] = value
+            low = LOW + 1 if sy > 0 else LOW - 1
+            post = propagate_back(pad, wet, 0, low)
+            u = [jnp.broadcast_to(got(19 + d), (NY, NZ)) for d in range(3)]
+            phase = jnp.broadcast_to(face[5 + FIELDS + e, pl.ds(2, 1), :], (NY, NZ))
+            kept = {}
+            collide_back(post, moments(post), u, phase, kept.__setitem__)
+            (crossing,) = along(sx, sy)
+            edges_out[pl.ds(2 * side + e, 1), :] = kept[crossing][at - low : at - low + 1, :]
+    edges_out[pl.ds(4, 4), :] = jnp.zeros((4, NZ), f32)
+
+
 def second_outer_kernel(
-    speed, phase, adj, fluid, ya, yb, xa, xb, adj_in, mom_in,
-    adj_out, mom_out, xa_out, xb_out, ya_out, yb_out, adj_pad, fluid_pad,
+    speed, phase, adj, fluid, ya, yb, xa, xb, adj_in, mom_in, _,
+    adj_out, mom_out, xa_out, xb_out, ya_out, yb_out, edges_out,
+    adj_pad, fluid_pad, corner_pad, corner_fluid,
 ):
     (x_low, x_high), (y_low, y_high) = sides("pipe", xa, xb), sides("cross", ya, yb)
     fill_field(fluid_pad, (), fluid, 2, y_low, y_high)
     fill_field_outer(fluid_pad, (), 2, x_low, x_high)
     fill_pops(adj_pad, adj, (0, 1, NX - 2, NX - 1), y_low, y_high)
-    fill_pops_outer(adj_pad, x_low, x_high, 5 + FIELDS)
+    faces = (x_low, x_high)
+    fill_pops_outer(adj_pad, x_low, x_high, lambda side, e: faces[side][5 + FIELDS + e, pl.ds(0, 1), :])
     for x in (0, NX - 1):
         step_plane(x, adj_pad, fluid_pad, speed, phase, adj_out, mom_out)
     put_pops(adj_out, (xa_out, xb_out), (ya_out, yb_out))
+    corner_edges(adj, fluid, (y_high, y_low), faces, edges_out, corner_pad, corner_fluid)
 
 
 def one_hots(index, row, hit_out, right_out, at):
@@ -396,8 +512,8 @@
 
 
 OWN = NX * NY * NZ
-SIDE = WX * NZ
-HALO = 2 * NY * NZ + 2 * SIDE
+SIDES = 2 * NX * NZ
+FACES = (2 * NY + 4) * NZ
 
 
 def store_velocity(pops, out):
@@ -407,7 +523,7 @@
             out[d, x] = u[d]
         return carry
 
-    lax.fori_loop(0, NX, plane, 0)
+    lax.fori_loop(0, NX, plane, 0, unroll=2)
 
 
 def own_kernel(
@@ -431,60 +547,61 @@
             one_hots(index, r, hit_out, right_out, pl.multiple_of((x * NY + r) * NZ, NZ))
         return carry
 
-    lax.fori_loop(0, NX, plane, 0)
+    lax.fori_loop(0, NX, plane, 0, unroll=2)
     copies[-1].wait()
     store_velocity(pops, speed_out)
 
 
+def imposed(table, slot):
+    index = slot(4).astype(jnp.int32) & 4095
+    contact = slot(3) * look_up(table, index)
+    return index, [slot(2) * slot(t) + contact for t in range(2)]
+
+
+def side_kernel(table, ya, yb, phi_out, wall_out, hit_out, right_out):
+    for side, rows in enumerate(sides("cross", ya, yb)):
+        index, values = imposed(table, lambda k: rows[pl.ds((5 + k) * NX, NX), :])
+        wall_out[side] = rows[pl.ds(8 * NX, NX), :]
+        for t in range(2):
+            phi_out[side, t] = values[t]
+        for x in range(NX):
+            one_hots(index, x, hit_out, right_out, (side * NX + x) * NZ)
+
+
 def middle_kernel(
-    phi, table, fluid, mom, ya, yb, xa, xb, pops_hbm,
-    dgrad_out, grad_out, fluid_out, wall_face, wall_side, hit_out, right_out, speed_out,
-    phi_pad, pops, sem,
+    phi, table, fluid, mom, ya, yb, xa, xb, phi_side, wall_beside,
+    dgrad_out, grad_out, fluid_out, wall_face, wall_side, hit_out, right_out,
+    phi_pad,
 ):
-    (copy_pops,) = fetch([(pops_hbm, pops)], sem)
     (x_low, x_high), (y_low, y_high) = sides("pipe", xa, xb), sides("cross", ya, yb)
     fill_field(fluid_out, (), fluid, 2, y_low, y_high)
     fill_field_outer(fluid_out, (), 2, x_low, x_high)
-
-    def copy(x, carry):
+    for x in range(NX):
         for t in range(2):
             phi_pad[t, x + 1, pl.ds(LOW, NY), :] = phi[t, x]
-        return carry
-
-    lax.fori_loop(0, NX, copy, 0)
-
-    def imposed(slot):
-        index = slot(4).astype(jnp.int32) & 4095
-        contact = slot(3) * look_up(table, index)
-        return index, [slot(2) * slot(t) + contact for t in range(2)]
-
+            for side, y in enumerate((LOW - 1, LOW + NY)):
+                phi_pad[t, x + 1, pl.ds(y, 1), :] = phi_side[side, t, pl.ds(x, 1), :]
     for side, (face, x) in enumerate(((x_low, 0), (x_high, WX - 1))):
-        index, values = imposed(lambda k: face[5 + k])
+        index, values = imposed(table, lambda k: face[5 + k])
         wall_face[side] = face[8]
+        wall_side[side, pl.ds(1, NX), :] = wall_beside[side]
         for t in range(2):
             phi_pad[t, x, pl.ds(LOW, NY), :] = values[t]
         for r in range(NY):
             one_hots(index, r, hit_out, right_out, (side * NY + r) * NZ)
-    base = 2 * NY * NZ
-    for side, (rows, y) in enumerate(((y_low, LOW - 1), (y_high, LOW + NY))):
-        index, values = imposed(lambda k: rows[pl.ds((5 + k) * NX, NX), :])
-        wall_side[side, pl.ds(1, NX), :] = rows[pl.ds(8 * NX, NX), :]
-        for x in range(NX):
-            for t in range(2):
-                phi_pad[t, x + 1, pl.ds(y, 1), :] = values[t][x : x + 1, :]
-            one_hots(index, x, hit_out, right_out, base + side * SIDE + (x + 1) * NZ)
-    def corner_rows(k):
+
+    def corner_tile(k):
         rows = [face[5 + FIELDS + 1 - e, pl.ds(1 + k, 1), :] for e in range(2) for face in (x_low, x_high)]
         return jnp.concatenate(rows + rows, axis=0)
 
-    index, values = imposed(corner_rows)
-    on_wall = corner_rows(3)
+    index, values = imposed(table, corner_tile)
+    on_wall = corner_tile(3)
     for r in range(4):
         side, x, y = r // 2, (WX - 1) * (r % 2), (LOW - 1, LOW + NY)[r // 2]
         wall_side[side, pl.ds(x, 1), :] = on_wall[r : r + 1, :]
         for t in range(2):
             phi_pad[t, x, pl.ds(y, 1), :] = values[t][r : r + 1, :]
-        one_hots(index, r, hit_out, right_out, base + side * SIDE + x * NZ)
+        one_hots(index, r, hit_out, right_out, (2 * NY + r) * NZ)
 
     def plane(x, carry):
         def view(t):
@@ -498,9 +615,13 @@
             dgrad_out[d, x] = dgrad[d]
         return carry
 
-    lax.fori_loop(0, NX, plane, 0)
-    copy_pops.wait()
-    store_velocity(pops, speed_out)
+    lax.fori_loop(0, NX, plane, 0, unroll=2)
+
+
+def speed_kernel(pops_hbm, _, out, pops, sem):
+    for copy in fetch([(pops_hbm, pops)], sem):
+        copy.wait()
+    store_velocity(pops, out)
 
 
 def own_terms(*args):
@@ -510,12 +631,21 @@
     return whole_call(own_kernel, "own_terms", shapes, args, scratch, specs=[pl.BlockSpec(memory_space=pl.ANY)] * len(args))
 
 
+def side_terms(*args):
+    shapes = [((2, 2, NX, NZ), f32), ((2, NX, NZ), f32)] + [((64, SIDES), jnp.bfloat16)] * 2
+    return whole_call(side_kernel, "side_terms", shapes, args)
+
+
 def middle(*args):
     shapes = [vector, vector, ((WX, ROWS, NZ), f32), ((2, NY, NZ), f32), ((2, WX, NZ), f32)]
-    shapes += [((64, HALO), jnp.bfloat16)] * 2 + [vector]
-    scratch = [pltpu.VMEM((2, WX, ROWS, NZ), f32), pltpu.VMEM((19, NX, NY, NZ), f32), pltpu.SemaphoreType.DMA((1,))]
-    specs = [pl.BlockSpec(memory_space=pltpu.VMEM)] * (len(args) - 1) + [pl.BlockSpec(memory_space=pl.ANY)]
-    return whole_call(middle_kernel, "middle", shapes, args, scratch, specs=specs)
+    shapes += [((64, FACES), jnp.bfloat16)] * 2
+    return whole_call(middle_kernel, "middle", shapes, args, [pltpu.VMEM((2, WX, ROWS, NZ), f32)])
+
+
+def first_speed(pops, after):
+    scratch = [pltpu.VMEM((19, NX, NY, NZ), f32), pltpu.SemaphoreType.DMA((1,))]
+    specs = [pl.BlockSpec(memory_space=pl.ANY)] * 2
+    return whole_call(speed_kernel, "first_speed", [vector], (pops, after), scratch, specs=specs)[0]
 
 
 def weighted(hit, values):
@@ -572,7 +702,7 @@
         gradient_plane(x, adj_pad, fluid_pad, grad, dgrad_in, out)
         return carry
 
-    lax.fori_loop(1, NX - 1, plane, 0)
+    lax.fori_loop(1, NX - 1, plane, 0, unroll=2)
     acc_out[...] = jnp.zeros_like(acc_out)
 
     def group(g, carry):
@@ -583,14 +713,14 @@
 
 
 def first_outer_kernel(
-    adj, fluid_pad, grad, dgrad_in, ya, yb, xa, xb, dgrad_inner, acc_in,
-    wall, hits, rights, wall_face, wall_side, halo_hits, halo_rights,
+    adj, fluid_pad, grad, dgrad_in, ya, yb, xa, xb, edges, dgrad_inner, acc_in,
+    wall, hits, rights, wall_face, wall_side, face_hits, face_rights, side_hits, side_rights,
     total_out,
     adj_pad, dgrad_pad, rows,
 ):
     (x_low, x_high), (y_low, y_high) = sides("pipe", xa, xb), sides("cross", ya, yb)
     fill_pops(adj_pad, adj, (0, 1, NX - 2, NX - 1), y_low, y_high)
-    fill_pops_outer(adj_pad, x_low, x_high, 5)
+    fill_pops_outer(adj_pad, x_low, x_high, edge_of(edges))
     for d in range(3):
         for x in (0, 1, 2, 3, NX, NX + 1, NX + 2, NX + 3):
             dgrad_pad[d, x] = jnp.zeros((ROWS, NZ), f32)
@@ -610,51 +740,56 @@
         total = total + table_sum(weighted(hits[:, nodes], values[2 * k : 2 * k + 2]), rights[:, nodes])
     values = [plane_adjoint(dgrad_pad, x) * wall_face[k] for k, x in enumerate((0, WX - 1))]
     flat = dgrad_pad.reshape(3 * (WX + 2) * ROWS, NZ)
+    beside, corners = [], []
     for side, (row, sign) in enumerate(((LOW, 1.0), (LOW + NY - 1, -1.0))):
         for d in range(3):
             rows[d] = flat[pl.ds(d * (WX + 2) * ROWS + row, WX + 2, stride=ROWS), :]
-        values.append(side_adjoint(rows, sign) * wall_side[side])
-    total = total + table_sum(weighted(halo_hits[...], values), halo_rights[...])
+        value = side_adjoint(rows, sign) * wall_side[side]
+        beside.append(value[1 : WX - 1])
+        corners += [value[:1], value[WX - 1 :]]
+    values.append(jnp.concatenate(corners, axis=0))
+    total = total + table_sum(weighted(face_hits[...], values), face_rights[...])
+    total = total + table_sum(weighted(side_hits[...], beside), side_rights[...])
     both = total[:64] + total[64:]
     total_out[...] = jnp.concatenate([both[:32], both[32:]], axis=1)
 
 
-SHARE = 4
+shares = ((0, 6), (6, 5), (11, 5))
 
 
 def first_adjoint_kernel(
-    start, speed, phase, adj, fluid_pad, ya, yb, xa, xb, *refs
+    start, count, speed, phase, adj, fluid_pad, ya, yb, xa, xb, edges, *refs
 ):
     out, adj_pad, part, sem = refs[-4:]
     (x_low, x_high), (y_low, y_high) = sides("pipe", xa, xb), sides("cross", ya, yb)
-    planes = range(max(start - 1, 0), min(start + SHARE + 1, NX))
+    planes = range(max(start - 1, 0), min(start + count + 1, NX))
     fill_pops(adj_pad, adj, planes, y_low, y_high)
-    if start == 0 or start + SHARE == NX:
-        fill_pops_outer(adj_pad, x_low, x_high, 5)
+    if start == 0 or start + count == NX:
+        fill_pops_outer(adj_pad, x_low, x_high, edge_of(edges))
 
     def plane(k, carry):
         step_plane(start + k, adj_pad, fluid_pad, speed, phase, part, None, start)
         return carry
 
-    lax.fori_loop(0, SHARE, plane, 0)
-    (copy,) = fetch([(part, out.at[:, pl.ds(start, SHARE)])], sem)
+    lax.fori_loop(0, count, plane, 0)
+    (copy,) = fetch([(part, out.at[:, pl.ds(start, count)])], sem)
     copy.wait()
 
 
-def first_adjoint(start, args, after, before):
+def first_adjoint(start, count, args, after, before):
     args = (*args, after) if before is None else (*args, after, before)
-    specs = [pl.BlockSpec(memory_space=pltpu.VMEM)] * 8 + [pl.BlockSpec(memory_space=pl.ANY)] * (len(args) - 8)
+    specs = [pl.BlockSpec(memory_space=pltpu.VMEM)] * 9 + [pl.BlockSpec(memory_space=pl.ANY)] * (len(args) - 9)
     return pl.pallas_call(
-        functools.partial(first_adjoint_kernel, start),
+        functools.partial(first_adjoint_kernel, start, count),
         out_shape=jax.ShapeDtypeStruct(*block),
         in_specs=specs,
         out_specs=pl.BlockSpec(memory_space=pl.ANY),
         scratch_shapes=[
             pltpu.VMEM((19, WX, ROWS, NZ), f32),
-            pltpu.VMEM((19, SHARE, NY, NZ), f32),
+            pltpu.VMEM((19, count, NY, NZ), f32),
             pltpu.SemaphoreType.DMA((1,)),
         ],
-        input_output_aliases={} if before is None else {9: 0},
+        input_output_aliases={} if before is None else {10: 0},
         compiler_params=pltpu.CompilerParams(vmem_limit_bytes=24 * 1024 * 1024),
         name="first_adjoint",
     )(*args)
@@ -674,13 +809,22 @@
 
 def sum_rounds():
     return (
-        lambda p, c: (p ^ 1, c),
-        lambda p, c: (p ^ 3, c),
-        lambda p, c: (mirror(p, 2, 4) ^ 1, c),
-        lambda p, c: (p ^ 1, c ^ 1),
-        lambda p, c: (p ^ 1, mirror(c, 1, 4)),
-        lambda p, c: (p ^ 1, c ^ 4),
-        lambda p, c: (p ^ 1, mirror(c, 4, 4)),
+        (lambda p, c: (p ^ 1, c),),
+        (
+            lambda p, c: (mirror(p, 2, 4) ^ 1, c),
+            lambda p, c: (p ^ 3, c),
+            lambda p, c: (mirror(p, 2, 4) ^ 3, c),
+        ),
+        (
+            lambda p, c: (p ^ 1, mirror(c, 1, 4)),
+            lambda p, c: (p ^ 1, c ^ 1),
+            lambda p, c: (p ^ 1, mirror(c, 1, 4) ^ 1),
+        ),
+        (
+            lambda p, c: (p ^ 1, mirror(c, 4, 4)),
+            lambda p, c: (p ^ 1, c ^ 4),
+            lambda p, c: (p ^ 1, mirror(c, 4, 4) ^ 4),
+        ),
     )
 
 
@@ -711,29 +855,29 @@
 ):
     table = wettability.reshape(32, NZ)
     fields = (phase_first, phase_second, fluid, wall, patch)
-    x_swap, y_swap = pack_pairs(pack(adjoint_last, fields))
+    x_swap, y_swap = pack_pairs(pack(adjoint_last, fields, pops_second))
     y_halo = swap("cross", *y_swap)
     phi, hits, rights, wall_own, speed = own_terms(table, *fields, pops_second)
-    x_halo = swap("pipe", *pack_edges(x_swap, y_halo, FIELDS, phi))
+    x_halo = swap("pipe", *pack_edges(x_swap, y_halo, phi))
+    phi_side, wall_beside, side_hits, side_rights = side_terms(table, *y_halo)
     given = (speed, phase_second, adjoint_last, fluid, *y_halo)
     adjoint, mom = whole_call(
         second_inner_kernel, "second_inner", [block, seven], given, pad_scratch()
     )
-    face, side = ((7, NY, NZ), f32), ((5 * NX, NZ), f32)
-    adjoint, mom, *packed = whole_call(
+    face, side = ((5, NY, NZ), f32), ((5 * NX, NZ), f32)
+    adjoint, mom, *packed, edges = whole_call(
         second_outer_kernel,
         "second_outer",
-        [block, seven, face, face, side, side],
-        given + x_halo + (adjoint, mom),
-        pad_scratch(),
+        [block, seven, face, face, side, side, ((8, NZ), f32)],
+        given + x_halo + (adjoint, mom, phi_side),
+        pad_scratch() + [pltpu.VMEM((2, 19, 3, ROWS, NZ), f32), pltpu.VMEM((2, 3, ROWS, NZ), f32)],
         {8: 0, 9: 1},
     )
     x_swap, y_swap = pack_pairs(packed)
-    y_halo2 = swap("cross", *y_swap)
-    dgrad, grad, fluid_pad, wall_face, wall_side, halo_hits, halo_rights, speed = middle(
-        phi, table, fluid, mom, *y_halo, *x_halo, pops_first
+    y_halo2, x_halo2 = swap("cross", *y_swap), swap("pipe", *x_swap)
+    dgrad, grad, fluid_pad, wall_face, wall_side, face_hits, face_rights = middle(
+        phi, table, fluid, mom, *y_halo, *x_halo, phi_side, wall_beside
     )
-    x_halo2 = swap("pipe", *pack_edges(x_swap, y_halo2, 0, wall_side))
     given = (adjoint, fluid_pad, grad, dgrad, *y_halo2)
     nodes = (wall_own, hits, rights)
     adj_scratch = pad_scratch()[:1]
@@ -745,18 +889,18 @@
         first_outer_kernel,
         "first_outer",
         [((32, NZ), f32)],
-        given + x_halo2 + (dgrad_inner, acc) + nodes + (wall_face, wall_side, halo_hits, halo_rights),
+        given + x_halo2 + (edges, dgrad_inner, acc) + nodes + (wall_face, wall_side, face_hits, face_rights, side_hits, side_rights),
         dgrad_scratch + [pltpu.VMEM((3, WX + 2, NZ), f32)],
     )
-    args = (speed, phase_first, adjoint, fluid_pad, *y_halo2, *x_halo2)
+    args = (first_speed(pops_first, total), phase_first, adjoint, fluid_pad, *y_halo2, *x_halo2, edges)
     result = None
-    for k, place in enumerate(sum_rounds()):
-        got = exchange(total, place)
-        share = k - 2
-        if 0 <= share < NX // SHARE:
-            result = first_adjoint(share * SHARE, args, total, result)
-            got, result = lax.optimization_barrier((got, result))
-        total = total + got
+    for k, places in enumerate(sum_rounds()):
+        got = [exchange(total, place) for place in places]
+        if k:
+            result = first_adjoint(*shares[k - 1], args, total, result)
+            *got, result = lax.optimization_barrier((*got, result))
+        for part in got:
+            total = total + part
     return result, total.reshape(wettability.shape)
 
 

time: 58.3 us -> 54.9 us (0.942)
  starting transfers between devices: 19.7 us -> 32.1 us
  waiting for transfers between devices: 17.1 us -> 5.32 us
  Pallas kernels: 19 us -> 15.7 us
  local copies, waits for them, and re-layouts: 0.75 us -> 0.04 us
    ppermute x7 -> x10, waiting for transfers between devices: 16.5 us -> 3.97 us  [exchange(): return lax.ppermute(value, ('pipe', 'cross'), pairs)]
    ppermute x7 -> x10, starting transfers between devices: 4.35 us -> 15.6 us  [exchange(): return lax.ppermute(value, ('pipe', 'cross'), pairs)]
    pallas_call x9 -> x10, Pallas kernels: 14 us -> 11.5 us  [whole_call(): pl.pallas_call(kernel, out_shape=[pltpu.VMEM(shape, kind) if in_hbm else...]
    ppermute x4, starting transfers between devices: 9.39 us -> 10.3 us  [swap(): lax.ppermute(b, axis, [(i, (i + 2 * (i % 2) - 1) % count) for i in range(...]
    ppermute x4, waiting for transfers between devices: 0.58 us -> 1.34 us  [swap(): lax.ppermute(b, axis, [(i, (i + 2 * (i % 2) - 1) % count) for i in range(...]
    pallas_call x4 -> x3, Pallas kernels: 4.95 us -> 4.23 us  [first_adjoint(): pl.pallas_call(functools.partial(first_adjoint_kernel, start, count), out...]
    unnamed x18, local copies, waits for them, and re-layouts: 0.75 us -> 0.04 us
  transfers between devices with their start and end apart: 15 -> 18, of which waited for: 9 -> 5; matrix products, arithmetic and copies ran while one was open for 0% -> 0% of each run, Pallas kernels for 28% -> 23%
where the time goes in v3:
time: 54.9 us; the launch traced here: 54.8 us
  starting transfers between devices  32.1 us (58%)
  Pallas kernels  15.7 us (29%)
  waiting for transfers between devices  5.32 us (10%)
  between operations  0.95 us (2%)
  other arithmetic  0.63 us (1%)
    ppermute x10, starting transfers between devices, exchange(): return lax.ppermute(value, ('pipe', 'cross'), pairs)  15.6 us
    pallas_call x10, Pallas kernels, whole_call(): pl.pallas_call(kernel, out_shape=[pltpu.VMEM(shape, kind) if in_hbm else...  11.5 us
    ppermute x4, starting transfers between devices, swap(): lax.ppermute(b, axis, [(i, (i + 2 * (i % 2) - 1) % count) for i in range(...  10.3 us
    ppermute x4, starting transfers between devices, swap(): near = lax.ppermute(a, axis, [(i, i ^ 1) for i in range(count)])  6.18 us
    pallas_call x3, Pallas kernels, first_adjoint(): pl.pallas_call(functools.partial(first_adjoint_kernel, start, count), out...  4.23 us
    ppermute x10, waiting for transfers between devices, exchange(): return lax.ppermute(value, ('pipe', 'cross'), pairs)  3.97 us
    ppermute x4, waiting for transfers between devices, swap(): lax.ppermute(b, axis, [(i, (i + 2 * (i % 2) - 1) % count) for i in range(...  1.34 us
  transfers between devices with their start and end apart: 18, of which 5 were waited for; matrix products, arithmetic and copies ran while one was open for 0% of the time, Pallas kernels for 23%

profile of v3, /device:TPU:1, one launch (start us, length us, event | category | flops | bytes accessed | tf_op | source)
XLA Modules:
  0.0 54.8 jit_solution(16145947310199849877)
XLA Ops:
  0.7 1.7 %pack.1 = (f32[22,8,128]{2,1,0:T(8,128)S(1)}, f32[22,8,128]{2,1,0:T(8,128)S(1)}, f32[226,128]{1,0:T(8,128)S(1)}, f32[226,128]{1,0:T(8,128)S(1)}) custom-call(f32[19,16,8,128]{3,2,1,0:T(8,128)} %adj.3, f32[16,8,128]{2,1,0:T(8,128)} %phase.9, f32[16,8,128]{2,1,0:T(8,128)} %phase.6, s32[16,8,128]{2,1,0:T(8,128)} %fluid.5, s32[16,8,128]{2,1,0:T(8,128)} %refs_3_.1, ...), custom_call_target="tpu_custom_call" | custom-call | tf_op jit(solution)/shard_map/pack/pallas_call | solution.py:189
  2.4 2.5 %collective-permute-start = (f32[226,128]{1,0:T(8,128)S(1)}, f32[226,128]{1,0:T(8,128)S(1)}, u32[]{:S(2)}, u32[]{:S(2)}) collective-permute-start(f32[226,128]{1,0:T(8,128)S(1)} %get-tuple-element.48), channel_id=1, source_target_pairs={{0,1},{1,0},{2,3},{3,2},{4,5},{5,4},{6,7},{7,6},{8,9},{9,8},{10,11... | collective-permute-start | bytes 347144 | tf_op jit(solution)/shard_map/ppermute | solution.py:800
  4.9 4.4 %collective-permute-start.1 = (f32[226,128]{1,0:T(8,128)S(1)}, f32[226,128]{1,0:T(8,128)S(1)}, u32[]{:S(2)}, u32[]{:S(2)}) collective-permute-start(f32[226,128]{1,0:T(8,128)S(1)} %get-tuple-element.49), channel_id=1, source_target_pairs={{0,15},{1,2},{2,1},{3,4},{4,3},{5,6},{6,5},{7,8},{8,7},{9,10},{10,... | collective-permute-start | bytes 347144 | tf_op jit(solution)/shard_map/ppermute | solution.py:801
  9.4 2.5 %own_terms.1 = (f32[2,16,8,128]{3,2,1,0:T(8,128)S(1)}, bf16[64,16384]{1,0:T(8,128)(2,1)S(1)}, bf16[64,16384]{1,0:T(8,128)(2,1)S(1)}, f32[16,8,128]{2,1,0:T(8,128)S(1)}, f32[3,16,8,128]{3,2,1,0:T(8,128)S(1)}) custom-call(f32[32,128]{1,0:T(8,128)S(1)} %bitcast.3, f32[16,8,128]{2,1,0:T(8,128)S(1)} %copy-done.3, f32[16,8,128]{2,1,0:T(8,128)S(1)} %copy-done.5, ...), custom_call_target="tpu_custom_call" | custom-call | tf_op jit(solution)/shard_map/own_terms/pallas_call | solution.py:189
  12.0 2.2 %collective-permute-start.2 = (f32[22,8,128]{2,1,0:T(8,128)S(1)}, f32[22,8,128]{2,1,0:T(8,128)S(1)}, u32[]{:S(2)}, u32[]{:S(2)}) collective-permute-start(f32[22,8,128]{2,1,0:T(8,128)S(1)} %get-tuple-element.53), channel_id=1, source_target_pairs={{0,16},{16,0},{32,48},{48,32},{64,80},{80,64},{96,112},{112,96},{1... | collective-permute-start | bytes 270344 | tf_op jit(solution)/shard_map/ppermute | solution.py:800
  14.2 1.3 %collective-permute-start.3 = (f32[22,8,128]{2,1,0:T(8,128)S(1)}, f32[22,8,128]{2,1,0:T(8,128)S(1)}, u32[]{:S(2)}, u32[]{:S(2)}) collective-permute-start(f32[22,8,128]{2,1,0:T(8,128)S(1)} %get-tuple-element.54), channel_id=1, source_target_pairs={{0,112},{16,32},{32,16},{48,64},{64,48},{80,96},{96,80},{112,0},{1... | collective-permute-start | bytes 270344 | tf_op jit(solution)/shard_map/ppermute | solution.py:801
  15.9 1.2 %second_inner.1 = (f32[19,16,8,128]{3,2,1,0:T(8,128)S(1)}, f32[7,16,8,128]{3,2,1,0:T(8,128)S(1)}) custom-call(f32[3,16,8,128]{3,2,1,0:T(8,128)S(1)} %get-tuple-element.47.speed, f32[16,8,128]{2,1,0:T(8,128)S(1)} %copy-done.5, f32[19,16,8,128]{3,2,1,0:T(8,128)S(1)} %copy-done, s32[16,8,128]{2,1,0:T(8,128)S(1)} %copy-done.2, ...), custom_call_target="tpu_custom_call" | custom-call | tf_op jit(solution)/shard_map/second_inner/pallas_call | solution.py:189
  17.1 1.3 %collective-permute-done.3.xb = f32[22,8,128]{2,1,0:T(8,128)S(1)} collective-permute-done((f32[22,8,128]{2,1,0:T(8,128)S(1)}, f32[22,8,128]{2,1,0:T(8,128)S(1)}, u32[]{:S(2)}, u32[]{:S(2)}) %collective-permute-start.3) | collective-permute-done | bytes 90144 | tf_op jit(solution)/shard_map/ppermute | solution.py:801
  18.8 4.5 %collective-permute-start.5 = (f32[80,128]{1,0:T(8,128)S(1)}, f32[80,128]{1,0:T(8,128)S(1)}, u32[]{:S(2)}, u32[]{:S(2)}) collective-permute-start(f32[80,128]{1,0:T(8,128)S(1)} %get-tuple-element.65), channel_id=1, source_target_pairs={{0,15},{1,2},{2,1},{3,4},{4,3},{5,6},{6,5},{7,8},{8,7},{9,10},{10,... | collective-permute-start | bytes 122888 | tf_op jit(solution)/shard_map/ppermute | solution.py:801
  23.3 1.4 %collective-permute-start.6 = (f32[5,8,128]{2,1,0:T(8,128)S(1)}, f32[5,8,128]{2,1,0:T(8,128)S(1)}, u32[]{:S(2)}, u32[]{:S(2)}) collective-permute-start(f32[5,8,128]{2,1,0:T(8,128)S(1)} %get-tuple-element.66), channel_id=1, source_target_pairs={{0,16},{16,0},{32,48},{48,32},{64,80},{80,64},{96,112},{112,96},{1... | collective-permute-start | bytes 61448 | tf_op jit(solution)/shard_map/ppermute | solution.py:800
  24.8 1.1 %middle.1 = (f32[3,16,8,128]{3,2,1,0:T(8,128)S(1)}, f32[3,16,8,128]{3,2,1,0:T(8,128)S(1)}, f32[18,24,128]{2,1,0:T(8,128)S(1)}, f32[2,8,128]{2,1,0:T(8,128)S(1)},...) custom-call(f32[2,16,8,128]{3,2,1,0:T(8,128)S(1)} %get-tuple-element.52._.phi, ...), custom_call_target="tpu_custom_call" | custom-call | tf_op jit(solution)/shard_map/middle/pallas_call | solution.py:189
  25.9 2.6 %first_inner.1 = (f32[3,16,8,128]{3,2,1,0:T(8,128)S(1)}, f32[128,64]{1,0:T(8,128)S(1)}) custom-call(f32[19,16,8,128]{3,2,1,0:T(8,128)S(1)} %get-tuple-element.58.adj, f32[18,24,128]{2,1,0:T(8,128)S(1)} %get-tuple-element.61.fluid_pad, f32[3,16,8,128]{3,2,1,0:T(8,128)S(1)} %get-tuple-element.62.grad, f32[3,16,8,128]{3,2,1,0:T(8,128)S(1)} %get-tuple-element.63.dgrad_in, ...), custom_call_target="tpu_custom_call" | custom-call | tf_op jit(solution)/shard_map/first_inner/pallas_call | solution.py:189
  28.5 1.2 %first_outer.1._ = f32[32,128]{1,0:T(8,128)S(1)} custom-call(f32[19,16,8,128]{3,2,1,0:T(8,128)S(1)} %get-tuple-element.58.adj, f32[18,24,128]{2,1,0:T(8,128)S(1)} %get-tuple-element.61.fluid_pad, f32[3,16,8,128]{3,2,1,0:T(8,128)S(1)} %get-tuple-element.62.grad, f32[3,16,8,128]{3,2,1,0:T(8,128)S(1)} %get-tuple-element.63.dgrad_in, ...), custom_call_target="tpu_custom_call" | custom-call | tf_op jit(solution)/shard_map/first_outer/pallas_call | solution.py:189
  29.7 2.7 %collective-permute-start.8 = (f32[32,128]{1,0:T(8,128)S(1)}, f32[32,128]{1,0:T(8,128)S(1)}, u32[]{:S(2)}, u32[]{:S(2)}) collective-permute-start(f32[32,128]{1,0:T(8,128)S(1)} %first_outer.1._), channel_id=1, source_target_pairs={{0,16},{1,17},{2,18},{3,19},{4,20},{5,21},{6,22},{7,23},{8,24},{9,... | collective-permute-start | bytes 49160 | tf_op jit(solution)/shard_map/ppermute | solution.py:838
  32.3 0.8 %collective-permute-done.8 = f32[32,128]{1,0:T(8,128)S(1)} collective-permute-done((f32[32,128]{1,0:T(8,128)S(1)}, f32[32,128]{1,0:T(8,128)S(1)}, u32[]{:S(2)}, u32[]{:S(2)}) %collective-permute-start.8) | collective-permute-done | bytes 16416 | tf_op jit(solution)/shard_map/ppermute | solution.py:838
  33.2 1.6 %collective-permute-start.11 = (f32[32,128]{1,0:T(8,128)S(1)}, f32[32,128]{1,0:T(8,128)S(1)}, u32[]{:S(2)}, u32[]{:S(2)}) collective-permute-start(f32[32,128]{1,0:T(8,128)S(1)} %add.30.refs_0_), channel_id=1, source_target_pairs={{0,80},{1,81},{2,82},{3,83},{4,84},{5,85},{6,86},{7,87},{8,88},{9,... | collective-permute-start | bytes 49160 | tf_op jit(solution)/shard_map/ppermute | solution.py:838
  34.7 2.2 %collective-permute-start.9 = (f32[32,128]{1,0:T(8,128)S(1)}, f32[32,128]{1,0:T(8,128)S(1)}, u32[]{:S(2)}, u32[]{:S(2)}) collective-permute-start(f32[32,128]{1,0:T(8,128)S(1)} %add.30.refs_0_), channel_id=1, source_target_pairs={{0,112},{1,113},{2,114},{3,115},{4,116},{5,117},{6,118},{7,119},{8... | collective-permute-start | bytes 49160 | tf_op jit(solution)/shard_map/ppermute | solution.py:838
  37.5 1.5 %first_adjoint.3.refs_1_ = f32[19,16,8,128]{3,2,1,0:T(8,128)} custom-call(f32[3,16,8,128]{3,2,1,0:T(8,128)S(1)} %first_speed.1.speed, f32[16,8,128]{2,1,0:T(8,128)S(1)} %copy-done.3, f32[19,16,8,128]{3,2,1,0:T(8,128)S(1)} %get-tuple-element.58.adj, f32[18,24,128]{2,1,0:T(8,128)S(1)} %get-tuple-element.61.fluid_pad, f32[80,128]{1,0:T(8,128)S(1)} %collective-permute-done.4.ya, ...), custom_call_target="tpu_custom_call" | custom-call | tf_op jit(solution)/shard_map/first_adjoint/pallas_call | solution.py:782
  39.6 3.3 %collective-permute-start.12 = (f32[32,128]{1,0:T(8,128)S(1)}, f32[32,128]{1,0:T(8,128)S(1)}, u32[]{:S(2)}, u32[]{:S(2)}) collective-permute-start(f32[32,128]{1,0:T(8,128)S(1)} %add_add_fusion.1.refs_0_), channel_id=1, source_target_pairs={{0,19},{1,18},{2,17},{3,16},{4,23},{5,22},{6,21},{7,20},{8,27},{9,... | collective-permute-start | bytes 49160 | tf_op jit(solution)/shard_map/ppermute | solution.py:838
  42.9 1.4 %first_adjoint.4.refs_1_ = f32[19,16,8,128]{3,2,1,0:T(8,128)} custom-call(f32[3,16,8,128]{3,2,1,0:T(8,128)S(1)} %first_speed.1.speed, f32[16,8,128]{2,1,0:T(8,128)S(1)} %copy-done.3, f32[19,16,8,128]{3,2,1,0:T(8,128)S(1)} %get-tuple-element.58.adj, f32[18,24,128]{2,1,0:T(8,128)S(1)} %get-tuple-element.61.fluid_pad, ...), custom_call_target="tpu_custom_call", output_to_operand_aliasing={{}: (10, {})} | custom-call | tf_op jit(solution)/shard_map/first_adjoint/pallas_call | solution.py:782
  44.3 2.5 %collective-permute-start.17 = (f32[32,128]{1,0:T(8,128)S(1)}, f32[32,128]{1,0:T(8,128)S(1)}, u32[]{:S(2)}, u32[]{:S(2)}) collective-permute-start(f32[32,128]{1,0:T(8,128)S(1)} %add_add_fusion.refs_0_), channel_id=1, source_target_pairs={{0,24},{1,25},{2,26},{3,27},{4,28},{5,29},{6,30},{7,31},{8,16},{9,... | collective-permute-start | bytes 49160 | tf_op jit(solution)/shard_map/ppermute | solution.py:838
  46.8 3.0 %collective-permute-start.16 = (f32[32,128]{1,0:T(8,128)S(1)}, f32[32,128]{1,0:T(8,128)S(1)}, u32[]{:S(2)}, u32[]{:S(2)}) collective-permute-start(f32[32,128]{1,0:T(8,128)S(1)} %add_add_fusion.refs_0_), channel_id=1, source_target_pairs={{0,20},{1,21},{2,22},{3,23},{4,16},{5,17},{6,18},{7,19},{8,28},{9,... | collective-permute-start | bytes 49160 | tf_op jit(solution)/shard_map/ppermute | solution.py:838
  49.8 1.4 %first_adjoint.5 = f32[19,16,8,128]{3,2,1,0:T(8,128)} custom-call(f32[3,16,8,128]{3,2,1,0:T(8,128)S(1)} %first_speed.1.speed, f32[16,8,128]{2,1,0:T(8,128)S(1)} %copy-done.3, f32[19,16,8,128]{3,2,1,0:T(8,128)S(1)} %get-tuple-element.58.adj, f32[18,24,128]{2,1,0:T(8,128)S(1)} %get-tuple-element.61.fluid_pad, ...), custom_call_target="tpu_custom_call", output_to_operand_aliasing={{}: (10, {})} | custom-call | tf_op jit(solution)/shard_map/first_adjoint/pallas_call | solution.py:782
  51.4 2.8 %collective-permute-done.15 = f32[32,128]{1,0:T(8,128)S(1)} collective-permute-done((f32[32,128]{1,0:T(8,128)S(1)}, f32[32,128]{1,0:T(8,128)S(1)}, u32[]{:S(2)}, u32[]{:S(2)}) %collective-permute-start.15) | collective-permute-done | bytes 16416 | tf_op jit(solution)/shard_map/ppermute | solution.py:838
  (47 shorter events, 3.0 us)
Async XLA Ops:
  0.6 8.7 %copy-start.2 = (s32[16,8,128]{2,1,0:T(8,128)S(1)}, s32[16,8,128]{2,1,0:T(8,128)}, u32[]{:S(2)}) copy-start(s32[16,8,128]{2,1,0:T(8,128)} %fluid.5) | copy-start | bytes 196612
  0.6 8.7 %copy-start.3 = (f32[16,8,128]{2,1,0:T(8,128)S(1)}, f32[16,8,128]{2,1,0:T(8,128)}, u32[]{:S(2)}) copy-start(f32[16,8,128]{2,1,0:T(8,128)} %phase.9) | copy-start | bytes 196612
  0.7 8.7 %copy-start.5 = (f32[16,8,128]{2,1,0:T(8,128)S(1)}, f32[16,8,128]{2,1,0:T(8,128)}, u32[]{:S(2)}) copy-start(f32[16,8,128]{2,1,0:T(8,128)} %phase.6) | copy-start | bytes 196612
  0.7 8.7 %copy-start.7 = (s32[16,8,128]{2,1,0:T(8,128)S(1)}, s32[16,8,128]{2,1,0:T(8,128)}, u32[]{:S(2)}) copy-start(s32[16,8,128]{2,1,0:T(8,128)} %refs_4_.1) | copy-start | bytes 196612
  0.7 8.7 %copy-start.6 = (s32[16,8,128]{2,1,0:T(8,128)S(1)}, s32[16,8,128]{2,1,0:T(8,128)}, u32[]{:S(2)}) copy-start(s32[16,8,128]{2,1,0:T(8,128)} %refs_3_.1) | copy-start | bytes 196612
  2.4 13.5 %copy-start = (f32[19,16,8,128]{3,2,1,0:T(8,128)S(1)}, f32[19,16,8,128]{3,2,1,0:T(8,128)}, u32[]{:S(2)}) copy-start(f32[19,16,8,128]{3,2,1,0:T(8,128)} %adj.3) | copy-start | bytes 3735556
  2.4 9.5 %collective-permute-start = (f32[226,128]{1,0:T(8,128)S(1)}, f32[226,128]{1,0:T(8,128)S(1)}, u32[]{:S(2)}, u32[]{:S(2)}) collective-permute-start(f32[226,128]{1,0:T(8,128)S(1)} %get-tuple-element.48), channel_id=1, source_target_pairs={{0,1},{1,0},{2,3},{3,2},{4,5},{5,4},{6,7},{7,6},{8,9},{9,8},{10,11... | collective-permute-start | bytes 347144 | tf_op jit(solution)/shard_map/ppermute | solution.py:800
  4.9 7.0 %collective-permute-start.1 = (f32[226,128]{1,0:T(8,128)S(1)}, f32[226,128]{1,0:T(8,128)S(1)}, u32[]{:S(2)}, u32[]{:S(2)}) collective-permute-start(f32[226,128]{1,0:T(8,128)S(1)} %get-tuple-element.49), channel_id=1, source_target_pairs={{0,15},{1,2},{2,1},{3,4},{4,3},{5,6},{6,5},{7,8},{8,7},{9,10},{10,... | collective-permute-start | bytes 347144 | tf_op jit(solution)/shard_map/ppermute | solution.py:801
  12.0 5.1 %collective-permute-start.2 = (f32[22,8,128]{2,1,0:T(8,128)S(1)}, f32[22,8,128]{2,1,0:T(8,128)S(1)}, u32[]{:S(2)}, u32[]{:S(2)}) collective-permute-start(f32[22,8,128]{2,1,0:T(8,128)S(1)} %get-tuple-element.53), channel_id=1, source_target_pairs={{0,16},{16,0},{32,48},{48,32},{64,80},{80,64},{96,112},{112,96},{1... | collective-permute-start | bytes 270344 | tf_op jit(solution)/shard_map/ppermute | solution.py:800
  14.2 4.2 %collective-permute-start.3 = (f32[22,8,128]{2,1,0:T(8,128)S(1)}, f32[22,8,128]{2,1,0:T(8,128)S(1)}, u32[]{:S(2)}, u32[]{:S(2)}) collective-permute-start(f32[22,8,128]{2,1,0:T(8,128)S(1)} %get-tuple-element.54), channel_id=1, source_target_pairs={{0,112},{16,32},{32,16},{48,64},{64,48},{80,96},{96,80},{112,0},{1... | collective-permute-start | bytes 270344 | tf_op jit(solution)/shard_map/ppermute | solution.py:801
  18.7 7.1 %collective-permute-start.4 = (f32[80,128]{1,0:T(8,128)S(1)}, f32[80,128]{1,0:T(8,128)S(1)}, u32[]{:S(2)}, u32[]{:S(2)}) collective-permute-start(f32[80,128]{1,0:T(8,128)S(1)} %get-tuple-element.64), channel_id=1, source_target_pairs={{0,1},{1,0},{2,3},{3,2},{4,5},{5,4},{6,7},{7,6},{8,9},{9,8},{10,11... | collective-permute-start | bytes 122888 | tf_op jit(solution)/shard_map/ppermute | solution.py:800
  18.8 7.0 %collective-permute-start.5 = (f32[80,128]{1,0:T(8,128)S(1)}, f32[80,128]{1,0:T(8,128)S(1)}, u32[]{:S(2)}, u32[]{:S(2)}) collective-permute-start(f32[80,128]{1,0:T(8,128)S(1)} %get-tuple-element.65), channel_id=1, source_target_pairs={{0,15},{1,2},{2,1},{3,4},{4,3},{5,6},{6,5},{7,8},{8,7},{9,10},{10,... | collective-permute-start | bytes 122888 | tf_op jit(solution)/shard_map/ppermute | solution.py:801
  23.3 5.1 %collective-permute-start.6 = (f32[5,8,128]{2,1,0:T(8,128)S(1)}, f32[5,8,128]{2,1,0:T(8,128)S(1)}, u32[]{:S(2)}, u32[]{:S(2)}) collective-permute-start(f32[5,8,128]{2,1,0:T(8,128)S(1)} %get-tuple-element.66), channel_id=1, source_target_pairs={{0,16},{16,0},{32,48},{48,32},{64,80},{80,64},{96,112},{112,96},{1... | collective-permute-start | bytes 61448 | tf_op jit(solution)/shard_map/ppermute | solution.py:800
  24.7 3.8 %collective-permute-start.7 = (f32[5,8,128]{2,1,0:T(8,128)S(1)}, f32[5,8,128]{2,1,0:T(8,128)S(1)}, u32[]{:S(2)}, u32[]{:S(2)}) collective-permute-start(f32[5,8,128]{2,1,0:T(8,128)S(1)} %get-tuple-element.67), channel_id=1, source_target_pairs={{0,112},{16,32},{32,16},{48,64},{64,48},{80,96},{96,80},{112,0},{1... | collective-permute-start | bytes 61448 | tf_op jit(solution)/shard_map/ppermute | solution.py:801
  29.7 3.5 %collective-permute-start.8 = (f32[32,128]{1,0:T(8,128)S(1)}, f32[32,128]{1,0:T(8,128)S(1)}, u32[]{:S(2)}, u32[]{:S(2)}) collective-permute-start(f32[32,128]{1,0:T(8,128)S(1)} %first_outer.1._), channel_id=1, source_target_pairs={{0,16},{1,17},{2,18},{3,19},{4,20},{5,21},{6,22},{7,23},{8,24},{9,... | collective-permute-start | bytes 49160 | tf_op jit(solution)/shard_map/ppermute | solution.py:838
  33.2 5.9 %collective-permute-start.11 = (f32[32,128]{1,0:T(8,128)S(1)}, f32[32,128]{1,0:T(8,128)S(1)}, u32[]{:S(2)}, u32[]{:S(2)}) collective-permute-start(f32[32,128]{1,0:T(8,128)S(1)} %add.30.refs_0_), channel_id=1, source_target_pairs={{0,80},{1,81},{2,82},{3,83},{4,84},{5,85},{6,86},{7,87},{8,88},{9,... | collective-permute-start | bytes 49160 | tf_op jit(solution)/shard_map/ppermute | solution.py:838
  34.7 4.3 %collective-permute-start.10 = (f32[32,128]{1,0:T(8,128)S(1)}, f32[32,128]{1,0:T(8,128)S(1)}, u32[]{:S(2)}, u32[]{:S(2)}) collective-permute-start(f32[32,128]{1,0:T(8,128)S(1)} %add.30.refs_0_), channel_id=1, source_target_pairs={{0,48},{1,49},{2,50},{3,51},{4,52},{5,53},{6,54},{7,55},{8,56},{9,... | collective-permute-start | bytes 49160 | tf_op jit(solution)/shard_map/ppermute | solution.py:838
  34.7 4.4 %collective-permute-start.9 = (f32[32,128]{1,0:T(8,128)S(1)}, f32[32,128]{1,0:T(8,128)S(1)}, u32[]{:S(2)}, u32[]{:S(2)}) collective-permute-start(f32[32,128]{1,0:T(8,128)S(1)} %add.30.refs_0_), channel_id=1, source_target_pairs={{0,112},{1,113},{2,114},{3,115},{4,116},{5,117},{6,118},{7,119},{8... | collective-permute-start | bytes 49160 | tf_op jit(solution)/shard_map/ppermute | solution.py:838
  39.1 5.1 %collective-permute-start.14 = (f32[32,128]{1,0:T(8,128)S(1)}, f32[32,128]{1,0:T(8,128)S(1)}, u32[]{:S(2)}, u32[]{:S(2)}) collective-permute-start(f32[32,128]{1,0:T(8,128)S(1)} %add_add_fusion.1.refs_0_), channel_id=1, source_target_pairs={{0,18},{1,19},{2,16},{3,17},{4,22},{5,23},{6,20},{7,21},{8,26},{9,... | collective-permute-start | bytes 49160 | tf_op jit(solution)/shard_map/ppermute | solution.py:838
  39.2 5.1 %collective-permute-start.13 = (f32[32,128]{1,0:T(8,128)S(1)}, f32[32,128]{1,0:T(8,128)S(1)}, u32[]{:S(2)}, u32[]{:S(2)}) collective-permute-start(f32[32,128]{1,0:T(8,128)S(1)} %add_add_fusion.1.refs_0_), channel_id=1, source_target_pairs={{0,17},{1,16},{2,19},{3,18},{4,21},{5,20},{6,23},{7,22},{8,25},{9,... | collective-permute-start | bytes 49160 | tf_op jit(solution)/shard_map/ppermute | solution.py:838
  39.6 4.7 %collective-permute-start.12 = (f32[32,128]{1,0:T(8,128)S(1)}, f32[32,128]{1,0:T(8,128)S(1)}, u32[]{:S(2)}, u32[]{:S(2)}) collective-permute-start(f32[32,128]{1,0:T(8,128)S(1)} %add_add_fusion.1.refs_0_), channel_id=1, source_target_pairs={{0,19},{1,18},{2,17},{3,16},{4,23},{5,22},{6,21},{7,20},{8,27},{9,... | collective-permute-start | bytes 49160 | tf_op jit(solution)/shard_map/ppermute | solution.py:838
  44.3 6.8 %collective-permute-start.17 = (f32[32,128]{1,0:T(8,128)S(1)}, f32[32,128]{1,0:T(8,128)S(1)}, u32[]{:S(2)}, u32[]{:S(2)}) collective-permute-start(f32[32,128]{1,0:T(8,128)S(1)} %add_add_fusion.refs_0_), channel_id=1, source_target_pairs={{0,24},{1,25},{2,26},{3,27},{4,28},{5,29},{6,30},{7,31},{8,16},{9,... | collective-permute-start | bytes 49160 | tf_op jit(solution)/shard_map/ppermute | solution.py:838
  46.8 4.6 %collective-permute-start.16 = (f32[32,128]{1,0:T(8,128)S(1)}, f32[32,128]{1,0:T(8,128)S(1)}, u32[]{:S(2)}, u32[]{:S(2)}) collective-permute-start(f32[32,128]{1,0:T(8,128)S(1)} %add_add_fusion.refs_0_), channel_id=1, source_target_pairs={{0,20},{1,21},{2,22},{3,23},{4,16},{5,17},{6,18},{7,19},{8,28},{9,... | collective-permute-start | bytes 49160 | tf_op jit(solution)/shard_map/ppermute | solution.py:838
  49.8 4.4 %collective-permute-start.15 = (f32[32,128]{1,0:T(8,128)S(1)}, f32[32,128]{1,0:T(8,128)S(1)}, u32[]{:S(2)}, u32[]{:S(2)}) collective-permute-start(f32[32,128]{1,0:T(8,128)S(1)} %add_add_fusion.refs_0_), channel_id=1, source_target_pairs={{0,28},{1,29},{2,30},{3,31},{4,24},{5,25},{6,26},{7,27},{8,20},{9,... | collective-permute-start | bytes 49160 | tf_op jit(solution)/shard_map/ppermute | solution.py:838
  (3 other events, 25.9 us)

commit v4 on v3

--- a/solution.py
+++ b/solution.py
@@ -417,7 +417,7 @@
         step_plane(x, adj_pad, fluid_pad, speed, phase, adj_out, mom_out)
         return carry
 
-    lax.fori_loop(1, NX - 1, plane, 0, unroll=2)
+    lax.fori_loop(1, NX - 1, plane, 0, unroll=7)
 
 
 block = ((19, NX, NY, NZ), f32)
@@ -523,7 +523,7 @@
             out[d, x] = u[d]
         return carry
 
-    lax.fori_loop(0, NX, plane, 0, unroll=2)
+    lax.fori_loop(0, NX, plane, 0, unroll=4)
 
 
 def own_kernel(
@@ -547,7 +547,7 @@
             one_hots(index, r, hit_out, right_out, pl.multiple_of((x * NY + r) * NZ, NZ))
         return carry
 
-    lax.fori_loop(0, NX, plane, 0, unroll=2)
+    lax.fori_loop(0, NX, plane, 0, unroll=4)
     copies[-1].wait()
     store_velocity(pops, speed_out)
 
@@ -615,7 +615,7 @@
             dgrad_out[d, x] = dgrad[d]
         return carry
 
-    lax.fori_loop(0, NX, plane, 0, unroll=2)
+    lax.fori_loop(0, NX, plane, 0, unroll=4)
 
 
 def speed_kernel(pops_hbm, _, out, pops, sem):
@@ -702,7 +702,7 @@
         gradient_plane(x, adj_pad, fluid_pad, grad, dgrad_in, out)
         return carry
 
-    lax.fori_loop(1, NX - 1, plane, 0, unroll=2)
+    lax.fori_loop(1, NX - 1, plane, 0, unroll=7)
     acc_out[...] = jnp.zeros_like(acc_out)
 
     def group(g, carry):
@@ -811,18 +811,18 @@
     return (
         (lambda p, c: (p ^ 1, c),),
         (
+            lambda p, c: (p ^ 3, c),
             lambda p, c: (mirror(p, 2, 4) ^ 1, c),
-            lambda p, c: (p ^ 3, c),
             lambda p, c: (mirror(p, 2, 4) ^ 3, c),
         ),
         (
+            lambda p, c: (p ^ 1, c ^ 1),
             lambda p, c: (p ^ 1, mirror(c, 1, 4)),
-            lambda p, c: (p ^ 1, c ^ 1),
             lambda p, c: (p ^ 1, mirror(c, 1, 4) ^ 1),
         ),
         (
+            lambda p, c: (p ^ 1, c ^ 4),
             lambda p, c: (p ^ 1, mirror(c, 4, 4)),
-            lambda p, c: (p ^ 1, c ^ 4),
             lambda p, c: (p ^ 1, mirror(c, 4, 4) ^ 4),
         ),
     )

time: 54.9 us -> 50.1 us (0.913)
  starting transfers between devices: 32.1 us -> 28.6 us
  Pallas kernels: 15.7 us -> 14.6 us
    ppermute x10, starting transfers between devices: 15.6 us -> 12.2 us  [exchange(): return lax.ppermute(value, ('pipe', 'cross'), pairs)]
    pallas_call x10, Pallas kernels: 11.5 us -> 10.4 us  [whole_call(): pl.pallas_call(kernel, out_shape=[pltpu.VMEM(shape, kind) if in_hbm else...]
    ppermute x10, waiting for transfers between devices: 3.97 us -> 3.02 us  [exchange(): return lax.ppermute(value, ('pipe', 'cross'), pairs)]
    ppermute x4, waiting for transfers between devices: 1.34 us -> 2.21 us  [swap(): lax.ppermute(b, axis, [(i, (i + 2 * (i % 2) - 1) % count) for i in range(...]
  transfers between devices with their start and end apart: 18 -> 18, of which waited for: 5 -> 7; matrix products, arithmetic and copies ran while one was open for 0% -> 0% of each run, Pallas kernels for 23% -> 23%
where the time goes in v4:
time: 50.1 us; the launch traced here: 50 us
  starting transfers between devices  28.6 us (57%)
  Pallas kernels  14.6 us (29%)
  waiting for transfers between devices  5.24 us (10%)
  between operations  0.92 us (2%)
  other arithmetic  0.63 us (1%)
    ppermute x10, starting transfers between devices, exchange(): return lax.ppermute(value, ('pipe', 'cross'), pairs)  12.2 us
    pallas_call x10, Pallas kernels, whole_call(): pl.pallas_call(kernel, out_shape=[pltpu.VMEM(shape, kind) if in_hbm else...  10.4 us
    ppermute x4, starting transfers between devices, swap(): lax.ppermute(b, axis, [(i, (i + 2 * (i % 2) - 1) % count) for i in range(...  10.3 us
    ppermute x4, starting transfers between devices, swap(): near = lax.ppermute(a, axis, [(i, i ^ 1) for i in range(count)])  6.1 us
    pallas_call x3, Pallas kernels, first_adjoint(): pl.pallas_call(functools.partial(first_adjoint_kernel, start, count), out...  4.23 us
    ppermute x10, waiting for transfers between devices, exchange(): return lax.ppermute(value, ('pipe', 'cross'), pairs)  3.02 us
    ppermute x4, waiting for transfers between devices, swap(): lax.ppermute(b, axis, [(i, (i + 2 * (i % 2) - 1) % count) for i in range(...  2.21 us
  transfers between devices with their start and end apart: 18, of which 7 were waited for; matrix products, arithmetic and copies ran while one was open for 0% of the time, Pallas kernels for 23%

profile of v4, /device:TPU:1, one launch (start us, length us, event | category | flops | bytes accessed | tf_op | source)
XLA Modules:
  0.0 50.0 jit_solution(129425428326364853)
XLA Ops:
  0.7 1.7 %pack.1 = (f32[22,8,128]{2,1,0:T(8,128)S(1)}, f32[22,8,128]{2,1,0:T(8,128)S(1)}, f32[226,128]{1,0:T(8,128)S(1)}, f32[226,128]{1,0:T(8,128)S(1)}) custom-call(f32[19,16,8,128]{3,2,1,0:T(8,128)} %adj.3, f32[16,8,128]{2,1,0:T(8,128)} %phase.9, f32[16,8,128]{2,1,0:T(8,128)} %phase.6, s32[16,8,128]{2,1,0:T(8,128)} %fluid.5, s32[16,8,128]{2,1,0:T(8,128)} %refs_3_.1, ...), custom_call_target="tpu_custom_call" | custom-call | tf_op jit(solution)/shard_map/pack/pallas_call | solution.py:189
  2.4 2.5 %collective-permute-start = (f32[226,128]{1,0:T(8,128)S(1)}, f32[226,128]{1,0:T(8,128)S(1)}, u32[]{:S(2)}, u32[]{:S(2)}) collective-permute-start(f32[226,128]{1,0:T(8,128)S(1)} %get-tuple-element.48), channel_id=1, source_target_pairs={{0,1},{1,0},{2,3},{3,2},{4,5},{5,4},{6,7},{7,6},{8,9},{9,8},{10,11... | collective-permute-start | bytes 347144 | tf_op jit(solution)/shard_map/ppermute | solution.py:800
  4.9 4.4 %collective-permute-start.1 = (f32[226,128]{1,0:T(8,128)S(1)}, f32[226,128]{1,0:T(8,128)S(1)}, u32[]{:S(2)}, u32[]{:S(2)}) collective-permute-start(f32[226,128]{1,0:T(8,128)S(1)} %get-tuple-element.49), channel_id=1, source_target_pairs={{0,15},{1,2},{2,1},{3,4},{4,3},{5,6},{6,5},{7,8},{8,7},{9,10},{10,... | collective-permute-start | bytes 347144 | tf_op jit(solution)/shard_map/ppermute | solution.py:801
  9.4 2.6 %own_terms.1 = (f32[2,16,8,128]{3,2,1,0:T(8,128)S(1)}, bf16[64,16384]{1,0:T(8,128)(2,1)S(1)}, bf16[64,16384]{1,0:T(8,128)(2,1)S(1)}, f32[16,8,128]{2,1,0:T(8,128)S(1)}, f32[3,16,8,128]{3,2,1,0:T(8,128)S(1)}) custom-call(f32[32,128]{1,0:T(8,128)S(1)} %bitcast.3, f32[16,8,128]{2,1,0:T(8,128)S(1)} %copy-done.3, f32[16,8,128]{2,1,0:T(8,128)S(1)} %copy-done.5, ...), custom_call_target="tpu_custom_call" | custom-call | tf_op jit(solution)/shard_map/own_terms/pallas_call | solution.py:189
  12.1 2.1 %collective-permute-start.2 = (f32[22,8,128]{2,1,0:T(8,128)S(1)}, f32[22,8,128]{2,1,0:T(8,128)S(1)}, u32[]{:S(2)}, u32[]{:S(2)}) collective-permute-start(f32[22,8,128]{2,1,0:T(8,128)S(1)} %get-tuple-element.53), channel_id=1, source_target_pairs={{0,16},{16,0},{32,48},{48,32},{64,80},{80,64},{96,112},{112,96},{1... | collective-permute-start | bytes 270344 | tf_op jit(solution)/shard_map/ppermute | solution.py:800
  14.2 1.3 %collective-permute-start.3 = (f32[22,8,128]{2,1,0:T(8,128)S(1)}, f32[22,8,128]{2,1,0:T(8,128)S(1)}, u32[]{:S(2)}, u32[]{:S(2)}) collective-permute-start(f32[22,8,128]{2,1,0:T(8,128)S(1)} %get-tuple-element.54), channel_id=1, source_target_pairs={{0,112},{16,32},{32,16},{48,64},{64,48},{80,96},{96,80},{112,0},{1... | collective-permute-start | bytes 270344 | tf_op jit(solution)/shard_map/ppermute | solution.py:801
  16.7 1.7 %collective-permute-done.3.xb = f32[22,8,128]{2,1,0:T(8,128)S(1)} collective-permute-done((f32[22,8,128]{2,1,0:T(8,128)S(1)}, f32[22,8,128]{2,1,0:T(8,128)S(1)}, u32[]{:S(2)}, u32[]{:S(2)}) %collective-permute-start.3) | collective-permute-done | bytes 90144 | tf_op jit(solution)/shard_map/ppermute | solution.py:801
  18.8 4.5 %collective-permute-start.5 = (f32[80,128]{1,0:T(8,128)S(1)}, f32[80,128]{1,0:T(8,128)S(1)}, u32[]{:S(2)}, u32[]{:S(2)}) collective-permute-start(f32[80,128]{1,0:T(8,128)S(1)} %get-tuple-element.65), channel_id=1, source_target_pairs={{0,15},{1,2},{2,1},{3,4},{4,3},{5,6},{6,5},{7,8},{8,7},{9,10},{10,... | collective-permute-start | bytes 122888 | tf_op jit(solution)/shard_map/ppermute | solution.py:801
  23.3 1.4 %collective-permute-start.6 = (f32[5,8,128]{2,1,0:T(8,128)S(1)}, f32[5,8,128]{2,1,0:T(8,128)S(1)}, u32[]{:S(2)}, u32[]{:S(2)}) collective-permute-start(f32[5,8,128]{2,1,0:T(8,128)S(1)} %get-tuple-element.66), channel_id=1, source_target_pairs={{0,16},{16,0},{32,48},{48,32},{64,80},{80,64},{96,112},{112,96},{1... | collective-permute-start | bytes 61448 | tf_op jit(solution)/shard_map/ppermute | solution.py:800
  24.8 0.8 %middle.1 = (f32[3,16,8,128]{3,2,1,0:T(8,128)S(1)}, f32[3,16,8,128]{3,2,1,0:T(8,128)S(1)}, f32[18,24,128]{2,1,0:T(8,128)S(1)}, f32[2,8,128]{2,1,0:T(8,128)S(1)},...) custom-call(f32[2,16,8,128]{3,2,1,0:T(8,128)S(1)} %get-tuple-element.52._.phi, ...), custom_call_target="tpu_custom_call" | custom-call | tf_op jit(solution)/shard_map/middle/pallas_call | solution.py:189
  25.6 2.2 %first_inner.1 = (f32[3,16,8,128]{3,2,1,0:T(8,128)S(1)}, f32[128,64]{1,0:T(8,128)S(1)}) custom-call(f32[19,16,8,128]{3,2,1,0:T(8,128)S(1)} %get-tuple-element.58.adj, f32[18,24,128]{2,1,0:T(8,128)S(1)} %get-tuple-element.61.fluid_pad, f32[3,16,8,128]{3,2,1,0:T(8,128)S(1)} %get-tuple-element.62.grad, f32[3,16,8,128]{3,2,1,0:T(8,128)S(1)} %get-tuple-element.63.dgrad_in, ...), custom_call_target="tpu_custom_call" | custom-call | tf_op jit(solution)/shard_map/first_inner/pallas_call | solution.py:189
  28.2 1.1 %first_outer.1._ = f32[32,128]{1,0:T(8,128)S(1)} custom-call(f32[19,16,8,128]{3,2,1,0:T(8,128)S(1)} %get-tuple-element.58.adj, f32[18,24,128]{2,1,0:T(8,128)S(1)} %get-tuple-element.61.fluid_pad, f32[3,16,8,128]{3,2,1,0:T(8,128)S(1)} %get-tuple-element.62.grad, f32[3,16,8,128]{3,2,1,0:T(8,128)S(1)} %get-tuple-element.63.dgrad_in, ...), custom_call_target="tpu_custom_call" | custom-call | tf_op jit(solution)/shard_map/first_outer/pallas_call | solution.py:189
  29.4 2.2 %collective-permute-start.8 = (f32[32,128]{1,0:T(8,128)S(1)}, f32[32,128]{1,0:T(8,128)S(1)}, u32[]{:S(2)}, u32[]{:S(2)}) collective-permute-start(f32[32,128]{1,0:T(8,128)S(1)} %first_outer.1._), channel_id=1, source_target_pairs={{0,16},{1,17},{2,18},{3,19},{4,20},{5,21},{6,22},{7,23},{8,24},{9,... | collective-permute-start | bytes 49160 | tf_op jit(solution)/shard_map/ppermute | solution.py:838
  31.6 0.8 %collective-permute-done.8 = f32[32,128]{1,0:T(8,128)S(1)} collective-permute-done((f32[32,128]{1,0:T(8,128)S(1)}, f32[32,128]{1,0:T(8,128)S(1)}, u32[]{:S(2)}, u32[]{:S(2)}) %collective-permute-start.8) | collective-permute-done | bytes 16416 | tf_op jit(solution)/shard_map/ppermute | solution.py:838
  32.4 1.6 %collective-permute-start.11 = (f32[32,128]{1,0:T(8,128)S(1)}, f32[32,128]{1,0:T(8,128)S(1)}, u32[]{:S(2)}, u32[]{:S(2)}) collective-permute-start(f32[32,128]{1,0:T(8,128)S(1)} %add.30.refs_0_), channel_id=1, source_target_pairs={{0,80},{1,81},{2,82},{3,83},{4,84},{5,85},{6,86},{7,87},{8,88},{9,... | collective-permute-start | bytes 49160 | tf_op jit(solution)/shard_map/ppermute | solution.py:838
  34.3 1.3 %collective-permute-start.9 = (f32[32,128]{1,0:T(8,128)S(1)}, f32[32,128]{1,0:T(8,128)S(1)}, u32[]{:S(2)}, u32[]{:S(2)}) collective-permute-start(f32[32,128]{1,0:T(8,128)S(1)} %add.30.refs_0_), channel_id=1, source_target_pairs={{0,48},{1,49},{2,50},{3,51},{4,52},{5,53},{6,54},{7,55},{8,56},{9,... | collective-permute-start | bytes 49160 | tf_op jit(solution)/shard_map/ppermute | solution.py:838
  36.1 1.5 %first_adjoint.3.refs_1_ = f32[19,16,8,128]{3,2,1,0:T(8,128)} custom-call(f32[3,16,8,128]{3,2,1,0:T(8,128)S(1)} %first_speed.1.speed, f32[16,8,128]{2,1,0:T(8,128)S(1)} %copy-done.3, f32[19,16,8,128]{3,2,1,0:T(8,128)S(1)} %get-tuple-element.58.adj, f32[18,24,128]{2,1,0:T(8,128)S(1)} %get-tuple-element.61.fluid_pad, f32[80,128]{1,0:T(8,128)S(1)} %collective-permute-done.4.ya, ...), custom_call_target="tpu_custom_call" | custom-call | tf_op jit(solution)/shard_map/first_adjoint/pallas_call | solution.py:782
  37.6 0.8 %collective-permute-done.10 = f32[32,128]{1,0:T(8,128)S(1)} collective-permute-done((f32[32,128]{1,0:T(8,128)S(1)}, f32[32,128]{1,0:T(8,128)S(1)}, u32[]{:S(2)}, u32[]{:S(2)}) %collective-permute-start.10) | collective-permute-done | bytes 16416 | tf_op jit(solution)/shard_map/ppermute | solution.py:838
  38.9 2.8 %collective-permute-start.12 = (f32[32,128]{1,0:T(8,128)S(1)}, f32[32,128]{1,0:T(8,128)S(1)}, u32[]{:S(2)}, u32[]{:S(2)}) collective-permute-start(f32[32,128]{1,0:T(8,128)S(1)} %add_add_fusion.1.refs_0_), channel_id=1, source_target_pairs={{0,17},{1,16},{2,19},{3,18},{4,21},{5,20},{6,23},{7,22},{8,25},{9,... | collective-permute-start | bytes 49160 | tf_op jit(solution)/shard_map/ppermute | solution.py:838
  41.6 1.4 %first_adjoint.4.refs_1_ = f32[19,16,8,128]{3,2,1,0:T(8,128)} custom-call(f32[3,16,8,128]{3,2,1,0:T(8,128)S(1)} %first_speed.1.speed, f32[16,8,128]{2,1,0:T(8,128)S(1)} %copy-done.3, f32[19,16,8,128]{3,2,1,0:T(8,128)S(1)} %get-tuple-element.58.adj, f32[18,24,128]{2,1,0:T(8,128)S(1)} %get-tuple-element.61.fluid_pad, ...), custom_call_target="tpu_custom_call", output_to_operand_aliasing={{}: (10, {})} | custom-call | tf_op jit(solution)/shard_map/first_adjoint/pallas_call | solution.py:782
  43.2 1.5 %collective-permute-start.17 = (f32[32,128]{1,0:T(8,128)S(1)}, f32[32,128]{1,0:T(8,128)S(1)}, u32[]{:S(2)}, u32[]{:S(2)}) collective-permute-start(f32[32,128]{1,0:T(8,128)S(1)} %add_add_fusion.refs_0_), channel_id=1, source_target_pairs={{0,24},{1,25},{2,26},{3,27},{4,28},{5,29},{6,30},{7,31},{8,16},{9,... | collective-permute-start | bytes 49160 | tf_op jit(solution)/shard_map/ppermute | solution.py:838
  44.7 1.6 %collective-permute-start.16 = (f32[32,128]{1,0:T(8,128)S(1)}, f32[32,128]{1,0:T(8,128)S(1)}, u32[]{:S(2)}, u32[]{:S(2)}) collective-permute-start(f32[32,128]{1,0:T(8,128)S(1)} %add_add_fusion.refs_0_), channel_id=1, source_target_pairs={{0,28},{1,29},{2,30},{3,31},{4,24},{5,25},{6,26},{7,27},{8,20},{9,... | collective-permute-start | bytes 49160 | tf_op jit(solution)/shard_map/ppermute | solution.py:838
  46.8 1.4 %first_adjoint.5 = f32[19,16,8,128]{3,2,1,0:T(8,128)} custom-call(f32[3,16,8,128]{3,2,1,0:T(8,128)S(1)} %first_speed.1.speed, f32[16,8,128]{2,1,0:T(8,128)S(1)} %copy-done.3, f32[19,16,8,128]{3,2,1,0:T(8,128)S(1)} %get-tuple-element.58.adj, f32[18,24,128]{2,1,0:T(8,128)S(1)} %get-tuple-element.61.fluid_pad, ...), custom_call_target="tpu_custom_call", output_to_operand_aliasing={{}: (10, {})} | custom-call | tf_op jit(solution)/shard_map/first_adjoint/pallas_call | solution.py:782
  48.1 0.9 %collective-permute-done.16 = f32[32,128]{1,0:T(8,128)S(1)} collective-permute-done((f32[32,128]{1,0:T(8,128)S(1)}, f32[32,128]{1,0:T(8,128)S(1)}, u32[]{:S(2)}, u32[]{:S(2)}) %collective-permute-start.16) | collective-permute-done | bytes 16416 | tf_op jit(solution)/shard_map/ppermute | solution.py:838
  (47 shorter events, 5.1 us)
Async XLA Ops:
  0.6 8.7 %copy-start.2 = (s32[16,8,128]{2,1,0:T(8,128)S(1)}, s32[16,8,128]{2,1,0:T(8,128)}, u32[]{:S(2)}) copy-start(s32[16,8,128]{2,1,0:T(8,128)} %fluid.5) | copy-start | bytes 196612
  0.6 8.7 %copy-start.3 = (f32[16,8,128]{2,1,0:T(8,128)S(1)}, f32[16,8,128]{2,1,0:T(8,128)}, u32[]{:S(2)}) copy-start(f32[16,8,128]{2,1,0:T(8,128)} %phase.9) | copy-start | bytes 196612
  0.7 8.7 %copy-start.5 = (f32[16,8,128]{2,1,0:T(8,128)S(1)}, f32[16,8,128]{2,1,0:T(8,128)}, u32[]{:S(2)}) copy-start(f32[16,8,128]{2,1,0:T(8,128)} %phase.6) | copy-start | bytes 196612
  0.7 8.7 %copy-start.7 = (s32[16,8,128]{2,1,0:T(8,128)S(1)}, s32[16,8,128]{2,1,0:T(8,128)}, u32[]{:S(2)}) copy-start(s32[16,8,128]{2,1,0:T(8,128)} %refs_4_.1) | copy-start | bytes 196612
  0.7 8.7 %copy-start.6 = (s32[16,8,128]{2,1,0:T(8,128)S(1)}, s32[16,8,128]{2,1,0:T(8,128)}, u32[]{:S(2)}) copy-start(s32[16,8,128]{2,1,0:T(8,128)} %refs_3_.1) | copy-start | bytes 196612
  2.4 13.5 %copy-start = (f32[19,16,8,128]{3,2,1,0:T(8,128)S(1)}, f32[19,16,8,128]{3,2,1,0:T(8,128)}, u32[]{:S(2)}) copy-start(f32[19,16,8,128]{3,2,1,0:T(8,128)} %adj.3) | copy-start | bytes 3735556
  2.4 9.6 %collective-permute-start = (f32[226,128]{1,0:T(8,128)S(1)}, f32[226,128]{1,0:T(8,128)S(1)}, u32[]{:S(2)}, u32[]{:S(2)}) collective-permute-start(f32[226,128]{1,0:T(8,128)S(1)} %get-tuple-element.48), channel_id=1, source_target_pairs={{0,1},{1,0},{2,3},{3,2},{4,5},{5,4},{6,7},{7,6},{8,9},{9,8},{10,11... | collective-permute-start | bytes 347144 | tf_op jit(solution)/shard_map/ppermute | solution.py:800
  4.9 7.1 %collective-permute-start.1 = (f32[226,128]{1,0:T(8,128)S(1)}, f32[226,128]{1,0:T(8,128)S(1)}, u32[]{:S(2)}, u32[]{:S(2)}) collective-permute-start(f32[226,128]{1,0:T(8,128)S(1)} %get-tuple-element.49), channel_id=1, source_target_pairs={{0,15},{1,2},{2,1},{3,4},{4,3},{5,6},{6,5},{7,8},{8,7},{9,10},{10,... | collective-permute-start | bytes 347144 | tf_op jit(solution)/shard_map/ppermute | solution.py:801
  12.1 4.6 %collective-permute-start.2 = (f32[22,8,128]{2,1,0:T(8,128)S(1)}, f32[22,8,128]{2,1,0:T(8,128)S(1)}, u32[]{:S(2)}, u32[]{:S(2)}) collective-permute-start(f32[22,8,128]{2,1,0:T(8,128)S(1)} %get-tuple-element.53), channel_id=1, source_target_pairs={{0,16},{16,0},{32,48},{48,32},{64,80},{80,64},{96,112},{112,96},{1... | collective-permute-start | bytes 270344 | tf_op jit(solution)/shard_map/ppermute | solution.py:800
  14.2 4.2 %collective-permute-start.3 = (f32[22,8,128]{2,1,0:T(8,128)S(1)}, f32[22,8,128]{2,1,0:T(8,128)S(1)}, u32[]{:S(2)}, u32[]{:S(2)}) collective-permute-start(f32[22,8,128]{2,1,0:T(8,128)S(1)} %get-tuple-element.54), channel_id=1, source_target_pairs={{0,112},{16,32},{32,16},{48,64},{64,48},{80,96},{96,80},{112,0},{1... | collective-permute-start | bytes 270344 | tf_op jit(solution)/shard_map/ppermute | solution.py:801
  18.7 6.8 %collective-permute-start.4 = (f32[80,128]{1,0:T(8,128)S(1)}, f32[80,128]{1,0:T(8,128)S(1)}, u32[]{:S(2)}, u32[]{:S(2)}) collective-permute-start(f32[80,128]{1,0:T(8,128)S(1)} %get-tuple-element.64), channel_id=1, source_target_pairs={{0,1},{1,0},{2,3},{3,2},{4,5},{5,4},{6,7},{7,6},{8,9},{9,8},{10,11... | collective-permute-start | bytes 122888 | tf_op jit(solution)/shard_map/ppermute | solution.py:800
  18.8 6.7 %collective-permute-start.5 = (f32[80,128]{1,0:T(8,128)S(1)}, f32[80,128]{1,0:T(8,128)S(1)}, u32[]{:S(2)}, u32[]{:S(2)}) collective-permute-start(f32[80,128]{1,0:T(8,128)S(1)} %get-tuple-element.65), channel_id=1, source_target_pairs={{0,15},{1,2},{2,1},{3,4},{4,3},{5,6},{6,5},{7,8},{8,7},{9,10},{10,... | collective-permute-start | bytes 122888 | tf_op jit(solution)/shard_map/ppermute | solution.py:801
  23.3 4.4 %collective-permute-start.6 = (f32[5,8,128]{2,1,0:T(8,128)S(1)}, f32[5,8,128]{2,1,0:T(8,128)S(1)}, u32[]{:S(2)}, u32[]{:S(2)}) collective-permute-start(f32[5,8,128]{2,1,0:T(8,128)S(1)} %get-tuple-element.66), channel_id=1, source_target_pairs={{0,16},{16,0},{32,48},{48,32},{64,80},{80,64},{96,112},{112,96},{1... | collective-permute-start | bytes 61448 | tf_op jit(solution)/shard_map/ppermute | solution.py:800
  24.7 3.5 %collective-permute-start.7 = (f32[5,8,128]{2,1,0:T(8,128)S(1)}, f32[5,8,128]{2,1,0:T(8,128)S(1)}, u32[]{:S(2)}, u32[]{:S(2)}) collective-permute-start(f32[5,8,128]{2,1,0:T(8,128)S(1)} %get-tuple-element.67), channel_id=1, source_target_pairs={{0,112},{16,32},{32,16},{48,64},{64,48},{80,96},{96,80},{112,0},{1... | collective-permute-start | bytes 61448 | tf_op jit(solution)/shard_map/ppermute | solution.py:801
  29.4 3.1 %collective-permute-start.8 = (f32[32,128]{1,0:T(8,128)S(1)}, f32[32,128]{1,0:T(8,128)S(1)}, u32[]{:S(2)}, u32[]{:S(2)}) collective-permute-start(f32[32,128]{1,0:T(8,128)S(1)} %first_outer.1._), channel_id=1, source_target_pairs={{0,16},{1,17},{2,18},{3,19},{4,20},{5,21},{6,22},{7,23},{8,24},{9,... | collective-permute-start | bytes 49160 | tf_op jit(solution)/shard_map/ppermute | solution.py:838
  32.4 5.2 %collective-permute-start.11 = (f32[32,128]{1,0:T(8,128)S(1)}, f32[32,128]{1,0:T(8,128)S(1)}, u32[]{:S(2)}, u32[]{:S(2)}) collective-permute-start(f32[32,128]{1,0:T(8,128)S(1)} %add.30.refs_0_), channel_id=1, source_target_pairs={{0,80},{1,81},{2,82},{3,83},{4,84},{5,85},{6,86},{7,87},{8,88},{9,... | collective-permute-start | bytes 49160 | tf_op jit(solution)/shard_map/ppermute | solution.py:838
  34.0 4.4 %collective-permute-start.10 = (f32[32,128]{1,0:T(8,128)S(1)}, f32[32,128]{1,0:T(8,128)S(1)}, u32[]{:S(2)}, u32[]{:S(2)}) collective-permute-start(f32[32,128]{1,0:T(8,128)S(1)} %add.30.refs_0_), channel_id=1, source_target_pairs={{0,112},{1,113},{2,114},{3,115},{4,116},{5,117},{6,118},{7,119},{8... | collective-permute-start | bytes 49160 | tf_op jit(solution)/shard_map/ppermute | solution.py:838
  34.3 4.1 %collective-permute-start.9 = (f32[32,128]{1,0:T(8,128)S(1)}, f32[32,128]{1,0:T(8,128)S(1)}, u32[]{:S(2)}, u32[]{:S(2)}) collective-permute-start(f32[32,128]{1,0:T(8,128)S(1)} %add.30.refs_0_), channel_id=1, source_target_pairs={{0,48},{1,49},{2,50},{3,51},{4,52},{5,53},{6,54},{7,55},{8,56},{9,... | collective-permute-start | bytes 49160 | tf_op jit(solution)/shard_map/ppermute | solution.py:838
  38.4 4.8 %collective-permute-start.14 = (f32[32,128]{1,0:T(8,128)S(1)}, f32[32,128]{1,0:T(8,128)S(1)}, u32[]{:S(2)}, u32[]{:S(2)}) collective-permute-start(f32[32,128]{1,0:T(8,128)S(1)} %add_add_fusion.1.refs_0_), channel_id=1, source_target_pairs={{0,18},{1,19},{2,16},{3,17},{4,22},{5,23},{6,20},{7,21},{8,26},{9,... | collective-permute-start | bytes 49160 | tf_op jit(solution)/shard_map/ppermute | solution.py:838
  38.5 4.7 %collective-permute-start.13 = (f32[32,128]{1,0:T(8,128)S(1)}, f32[32,128]{1,0:T(8,128)S(1)}, u32[]{:S(2)}, u32[]{:S(2)}) collective-permute-start(f32[32,128]{1,0:T(8,128)S(1)} %add_add_fusion.1.refs_0_), channel_id=1, source_target_pairs={{0,19},{1,18},{2,17},{3,16},{4,23},{5,22},{6,21},{7,20},{8,27},{9,... | collective-permute-start | bytes 49160 | tf_op jit(solution)/shard_map/ppermute | solution.py:838
  38.9 4.3 %collective-permute-start.12 = (f32[32,128]{1,0:T(8,128)S(1)}, f32[32,128]{1,0:T(8,128)S(1)}, u32[]{:S(2)}, u32[]{:S(2)}) collective-permute-start(f32[32,128]{1,0:T(8,128)S(1)} %add_add_fusion.1.refs_0_), channel_id=1, source_target_pairs={{0,17},{1,16},{2,19},{3,18},{4,21},{5,20},{6,23},{7,22},{8,25},{9,... | collective-permute-start | bytes 49160 | tf_op jit(solution)/shard_map/ppermute | solution.py:838
  43.2 5.0 %collective-permute-start.17 = (f32[32,128]{1,0:T(8,128)S(1)}, f32[32,128]{1,0:T(8,128)S(1)}, u32[]{:S(2)}, u32[]{:S(2)}) collective-permute-start(f32[32,128]{1,0:T(8,128)S(1)} %add_add_fusion.refs_0_), channel_id=1, source_target_pairs={{0,24},{1,25},{2,26},{3,27},{4,28},{5,29},{6,30},{7,31},{8,16},{9,... | collective-permute-start | bytes 49160 | tf_op jit(solution)/shard_map/ppermute | solution.py:838
  44.7 4.4 %collective-permute-start.16 = (f32[32,128]{1,0:T(8,128)S(1)}, f32[32,128]{1,0:T(8,128)S(1)}, u32[]{:S(2)}, u32[]{:S(2)}) collective-permute-start(f32[32,128]{1,0:T(8,128)S(1)} %add_add_fusion.refs_0_), channel_id=1, source_target_pairs={{0,28},{1,29},{2,30},{3,31},{4,24},{5,25},{6,26},{7,27},{8,20},{9,... | collective-permute-start | bytes 49160 | tf_op jit(solution)/shard_map/ppermute | solution.py:838
  46.2 3.2 %collective-permute-start.15 = (f32[32,128]{1,0:T(8,128)S(1)}, f32[32,128]{1,0:T(8,128)S(1)}, u32[]{:S(2)}, u32[]{:S(2)}) collective-permute-start(f32[32,128]{1,0:T(8,128)S(1)} %add_add_fusion.refs_0_), channel_id=1, source_target_pairs={{0,20},{1,21},{2,22},{3,23},{4,16},{5,17},{6,18},{7,19},{8,28},{9,... | collective-permute-start | bytes 49160 | tf_op jit(solution)/shard_map/ppermute | solution.py:838
  (3 other events, 24.8 us)

commit v5 on v4

--- a/solution.py
+++ b/solution.py
@@ -313,7 +313,7 @@
 edge_minus = (10, 8)
 
 
-def pack_edges_kernel(xa, xb, ya, yb, _, xa_out, xb_out):
+def pack_edges_kernel(xa, xb, yb, ya, _, xa_out, xb_out):
     planes = 5 + FIELDS
     for k in [*range(planes), *range(planes + 2, X_PLANES)]:
         xa_out[k] = xa[k]
@@ -335,7 +335,7 @@
 
 def pack_edges(x_pair, y_halo, after):
     out = ((X_PLANES, NY, NZ), f32)
-    return whole_call(pack_edges_kernel, "pack_edges", [out, out], (*x_pair, *y_halo, after))
+    return whole_call(pack_edges_kernel, "pack_edges", [out, out], (*x_pair, *y_halo[::-1], after))
 
 
 def fill_sides(pad, lead, y_low, low_slot, y_high, high_slot):
@@ -408,7 +408,7 @@
 inner = range(1, NX - 1)
 
 
-def second_inner_kernel(speed, phase, adj, fluid, ya, yb, adj_out, mom_out, adj_pad, fluid_pad):
+def second_inner_kernel(speed, phase, adj, fluid, yb, ya, adj_out, mom_out, adj_pad, fluid_pad):
     y_low, y_high = sides("cross", ya, yb)
     fill_field(fluid_pad, (), fluid, 2, y_low, y_high)
     fill_pops(adj_pad, adj, range(NX), y_low, y_high)
@@ -485,7 +485,7 @@
 
 
 def second_outer_kernel(
-    speed, phase, adj, fluid, ya, yb, xa, xb, adj_in, mom_in, _,
+    speed, phase, adj, fluid, yb, ya, xa, xb, adj_in, mom_in, _,
     adj_out, mom_out, xa_out, xb_out, ya_out, yb_out, edges_out,
     adj_pad, fluid_pad, corner_pad, corner_fluid,
 ):
@@ -558,7 +558,7 @@
     return index, [slot(2) * slot(t) + contact for t in range(2)]
 
 
-def side_kernel(table, ya, yb, phi_out, wall_out, hit_out, right_out):
+def side_kernel(table, yb, ya, phi_out, wall_out, hit_out, right_out):
     for side, rows in enumerate(sides("cross", ya, yb)):
         index, values = imposed(table, lambda k: rows[pl.ds((5 + k) * NX, NX), :])
         wall_out[side] = rows[pl.ds(8 * NX, NX), :]
@@ -676,12 +676,12 @@
     return gradient_adjoint(lambda d, a, b: pad[d, x + 1 + a, pl.ds(LOW + b, NY), :])
 
 
-GROUP = 4
+GROUP = 6
 
 
 def own_group(start, dgrad_pad, wall, hits, rights):
     values = [plane_adjoint(dgrad_pad, start + k + 1) * wall[start + k] for k in range(GROUP)]
-    nodes = pl.ds(pl.multiple_of(start * NY * NZ, NY * NZ), GROUP * NY * NZ)
+    nodes = pl.ds(start * NY * NZ, GROUP * NY * NZ)
     return table_sum(weighted(hits[:, nodes], values), rights[:, nodes])
 
 
@@ -703,13 +703,10 @@
         return carry
 
     lax.fori_loop(1, NX - 1, plane, 0, unroll=7)
-    acc_out[...] = jnp.zeros_like(acc_out)
-
-    def group(g, carry):
-        acc_out[...] += own_group(2 + g * GROUP, dgrad_pad, wall, hits, rights)
-        return carry
-
-    lax.fori_loop(0, (NX - 4) // GROUP, group, 0)
+    total = own_group(2, dgrad_pad, wall, hits, rights)
+    for start in range(2 + GROUP, NX - 2, GROUP):
+        total = total + own_group(start, dgrad_pad, wall, hits, rights)
+    acc_out[...] = total
 
 
 def first_outer_kernel(
@@ -859,8 +856,8 @@
     y_halo = swap("cross", *y_swap)
     phi, hits, rights, wall_own, speed = own_terms(table, *fields, pops_second)
     x_halo = swap("pipe", *pack_edges(x_swap, y_halo, phi))
-    phi_side, wall_beside, side_hits, side_rights = side_terms(table, *y_halo)
-    given = (speed, phase_second, adjoint_last, fluid, *y_halo)
+    phi_side, wall_beside, side_hits, side_rights = side_terms(table, *y_halo[::-1])
+    given = (speed, phase_second, adjoint_last, fluid, *y_halo[::-1])
     adjoint, mom = whole_call(
         second_inner_kernel, "second_inner", [block, seven], given, pad_scratch()
     )

time: 50.1 us -> 49.4 us (0.986)
  starting transfers between devices: 28.6 us -> 26.4 us
  waiting for transfers between devices: 5.24 us -> 7.17 us
    ppermute x4, starting transfers between devices: 6.1 us -> 3.54 us  [swap(): near = lax.ppermute(a, axis, [(i, i ^ 1) for i in range(count)])]
    ppermute x4, starting transfers between devices: 10.3 us -> 11.4 us  [swap(): lax.ppermute(b, axis, [(i, (i + 2 * (i % 2) - 1) % count) for i in range(...]
    ppermute x4, waiting for transfers between devices: 0.01 us -> 0.84 us  [swap(): near = lax.ppermute(a, axis, [(i, i ^ 1) for i in range(count)])]
    ppermute x4, waiting for transfers between devices: 2.21 us -> 3.01 us  [swap(): lax.ppermute(b, axis, [(i, (i + 2 * (i % 2) - 1) % count) for i in range(...]
    ppermute x10, starting transfers between devices: 12.2 us -> 11.4 us  [exchange(): return lax.ppermute(value, ('pipe', 'cross'), pairs)]
  transfers between devices with their start and end apart: 18 -> 18, of which waited for: 7 -> 11; matrix products, arithmetic and copies ran while one was open for 0% -> 0% of each run, Pallas kernels for 23% -> 22%
where the time goes in v5:
time: 49.4 us; the launch traced here: 49.3 us
  starting transfers between devices  26.4 us (53%)
  Pallas kernels  14.1 us (29%)
  waiting for transfers between devices  7.17 us (15%)
  between operations  0.9 us (2%)
  other arithmetic  0.63 us (1%)
    ppermute x4, starting transfers between devices, swap(): lax.ppermute(b, axis, [(i, (i + 2 * (i % 2) - 1) % count) for i in range(...  11.4 us
    ppermute x10, starting transfers between devices, exchange(): return lax.ppermute(value, ('pipe', 'cross'), pairs)  11.4 us
    pallas_call x10, Pallas kernels, whole_call(): pl.pallas_call(kernel, out_shape=[pltpu.VMEM(shape, kind) if in_hbm else...  9.89 us
    pallas_call x3, Pallas kernels, first_adjoint(): pl.pallas_call(functools.partial(first_adjoint_kernel, start, count), out...  4.23 us
    ppermute x4, starting transfers between devices, swap(): near = lax.ppermute(a, axis, [(i, i ^ 1) for i in range(count)])  3.54 us
    ppermute x10, waiting for transfers between devices, exchange(): return lax.ppermute(value, ('pipe', 'cross'), pairs)  3.32 us
    ppermute x4, waiting for transfers between devices, swap(): lax.ppermute(b, axis, [(i, (i + 2 * (i % 2) - 1) % count) for i in range(...  3.01 us
  transfers between devices with their start and end apart: 18, of which 11 were waited for; matrix products, arithmetic and copies ran while one was open for 0% of the time, Pallas kernels for 22%

profile of v5, /device:TPU:1, one launch (start us, length us, event | category | flops | bytes accessed | tf_op | source)
XLA Modules:
  0.0 49.3 jit_solution(3068541680121375832)
XLA Ops:
  0.7 1.7 %pack.1 = (f32[22,8,128]{2,1,0:T(8,128)S(1)}, f32[22,8,128]{2,1,0:T(8,128)S(1)}, f32[226,128]{1,0:T(8,128)S(1)}, f32[226,128]{1,0:T(8,128)S(1)}) custom-call(f32[19,16,8,128]{3,2,1,0:T(8,128)} %adj.3, f32[16,8,128]{2,1,0:T(8,128)} %phase.9, f32[16,8,128]{2,1,0:T(8,128)} %phase.6, s32[16,8,128]{2,1,0:T(8,128)} %fluid.5, s32[16,8,128]{2,1,0:T(8,128)} %refs_3_.1, ...), custom_call_target="tpu_custom_call" | custom-call | tf_op jit(solution)/shard_map/pack/pallas_call | solution.py:189
  2.4 6.9 %collective-permute-start = (f32[226,128]{1,0:T(8,128)S(1)}, f32[226,128]{1,0:T(8,128)S(1)}, u32[]{:S(2)}, u32[]{:S(2)}) collective-permute-start(f32[226,128]{1,0:T(8,128)S(1)} %get-tuple-element.48), channel_id=1, source_target_pairs={{0,15},{1,2},{2,1},{3,4},{4,3},{5,6},{6,5},{7,8},{8,7},{9,10},{10,... | collective-permute-start | bytes 347144 | tf_op jit(solution)/shard_map/ppermute | solution.py:798
  9.3 2.6 %own_terms.1 = (f32[2,16,8,128]{3,2,1,0:T(8,128)S(1)}, bf16[64,16384]{1,0:T(8,128)(2,1)S(1)}, bf16[64,16384]{1,0:T(8,128)(2,1)S(1)}, f32[16,8,128]{2,1,0:T(8,128)S(1)}, f32[3,16,8,128]{3,2,1,0:T(8,128)S(1)}) custom-call(f32[32,128]{1,0:T(8,128)S(1)} %bitcast.3, f32[16,8,128]{2,1,0:T(8,128)S(1)} %copy-done.3, f32[16,8,128]{2,1,0:T(8,128)S(1)} %copy-done.5, ...), custom_call_target="tpu_custom_call" | custom-call | tf_op jit(solution)/shard_map/own_terms/pallas_call | solution.py:189
  12.2 0.8 %collective-permute-done.1.ya = f32[226,128]{1,0:T(8,128)S(1)} collective-permute-done((f32[226,128]{1,0:T(8,128)S(1)}, f32[226,128]{1,0:T(8,128)S(1)}, u32[]{:S(2)}, u32[]{:S(2)}) %collective-permute-start.1) | collective-permute-done | bytes 115744 | tf_op jit(solution)/shard_map/ppermute | solution.py:797
  13.1 2.1 %collective-permute-start.2 = (f32[22,8,128]{2,1,0:T(8,128)S(1)}, f32[22,8,128]{2,1,0:T(8,128)S(1)}, u32[]{:S(2)}, u32[]{:S(2)}) collective-permute-start(f32[22,8,128]{2,1,0:T(8,128)S(1)} %get-tuple-element.53), channel_id=1, source_target_pairs={{0,16},{16,0},{32,48},{48,32},{64,80},{80,64},{96,112},{112,96},{1... | collective-permute-start | bytes 270344 | tf_op jit(solution)/shard_map/ppermute | solution.py:797
  15.2 1.3 %collective-permute-start.3 = (f32[22,8,128]{2,1,0:T(8,128)S(1)}, f32[22,8,128]{2,1,0:T(8,128)S(1)}, u32[]{:S(2)}, u32[]{:S(2)}) collective-permute-start(f32[22,8,128]{2,1,0:T(8,128)S(1)} %get-tuple-element.54), channel_id=1, source_target_pairs={{0,112},{16,32},{32,16},{48,64},{64,48},{80,96},{96,80},{112,0},{1... | collective-permute-start | bytes 270344 | tf_op jit(solution)/shard_map/ppermute | solution.py:798
  17.7 1.7 %collective-permute-done.3.xb = f32[22,8,128]{2,1,0:T(8,128)S(1)} collective-permute-done((f32[22,8,128]{2,1,0:T(8,128)S(1)}, f32[22,8,128]{2,1,0:T(8,128)S(1)}, u32[]{:S(2)}, u32[]{:S(2)}) %collective-permute-start.3) | collective-permute-done | bytes 90144 | tf_op jit(solution)/shard_map/ppermute | solution.py:798
  19.8 3.3 %collective-permute-start.5 = (f32[80,128]{1,0:T(8,128)S(1)}, f32[80,128]{1,0:T(8,128)S(1)}, u32[]{:S(2)}, u32[]{:S(2)}) collective-permute-start(f32[80,128]{1,0:T(8,128)S(1)} %get-tuple-element.65), channel_id=1, source_target_pairs={{0,15},{1,2},{2,1},{3,4},{4,3},{5,6},{6,5},{7,8},{8,7},{9,10},{10,... | collective-permute-start | bytes 122888 | tf_op jit(solution)/shard_map/ppermute | solution.py:798
  23.1 1.4 %collective-permute-start.6 = (f32[5,8,128]{2,1,0:T(8,128)S(1)}, f32[5,8,128]{2,1,0:T(8,128)S(1)}, u32[]{:S(2)}, u32[]{:S(2)}) collective-permute-start(f32[5,8,128]{2,1,0:T(8,128)S(1)} %get-tuple-element.66), channel_id=1, source_target_pairs={{0,16},{16,0},{32,48},{48,32},{64,80},{80,64},{96,112},{112,96},{1... | collective-permute-start | bytes 61448 | tf_op jit(solution)/shard_map/ppermute | solution.py:797
  24.5 0.8 %middle.1 = (f32[3,16,8,128]{3,2,1,0:T(8,128)S(1)}, f32[3,16,8,128]{3,2,1,0:T(8,128)S(1)}, f32[18,24,128]{2,1,0:T(8,128)S(1)}, f32[2,8,128]{2,1,0:T(8,128)S(1)},...) custom-call(f32[2,16,8,128]{3,2,1,0:T(8,128)S(1)} %get-tuple-element.52._.phi, ...), custom_call_target="tpu_custom_call" | custom-call | tf_op jit(solution)/shard_map/middle/pallas_call | solution.py:189
  26.1 1.7 %first_inner.1 = (f32[3,16,8,128]{3,2,1,0:T(8,128)S(1)}, f32[128,64]{1,0:T(8,128)S(1)}) custom-call(f32[19,16,8,128]{3,2,1,0:T(8,128)S(1)} %get-tuple-element.58.adj, f32[18,24,128]{2,1,0:T(8,128)S(1)} %get-tuple-element.61.fluid_pad, f32[3,16,8,128]{3,2,1,0:T(8,128)S(1)} %get-tuple-element.62.grad, f32[3,16,8,128]{3,2,1,0:T(8,128)S(1)} %get-tuple-element.63.dgrad_in, ...), custom_call_target="tpu_custom_call" | custom-call | tf_op jit(solution)/shard_map/first_inner/pallas_call | solution.py:189
  28.0 1.1 %first_outer.1._ = f32[32,128]{1,0:T(8,128)S(1)} custom-call(f32[19,16,8,128]{3,2,1,0:T(8,128)S(1)} %get-tuple-element.58.adj, f32[18,24,128]{2,1,0:T(8,128)S(1)} %get-tuple-element.61.fluid_pad, f32[3,16,8,128]{3,2,1,0:T(8,128)S(1)} %get-tuple-element.62.grad, f32[3,16,8,128]{3,2,1,0:T(8,128)S(1)} %get-tuple-element.63.dgrad_in, ...), custom_call_target="tpu_custom_call" | custom-call | tf_op jit(solution)/shard_map/first_outer/pallas_call | solution.py:189
  29.1 2.2 %collective-permute-start.8 = (f32[32,128]{1,0:T(8,128)S(1)}, f32[32,128]{1,0:T(8,128)S(1)}, u32[]{:S(2)}, u32[]{:S(2)}) collective-permute-start(f32[32,128]{1,0:T(8,128)S(1)} %first_outer.1._), channel_id=1, source_target_pairs={{0,16},{1,17},{2,18},{3,19},{4,20},{5,21},{6,22},{7,23},{8,24},{9,... | collective-permute-start | bytes 49160 | tf_op jit(solution)/shard_map/ppermute | solution.py:835
  31.3 0.8 %collective-permute-done.8 = f32[32,128]{1,0:T(8,128)S(1)} collective-permute-done((f32[32,128]{1,0:T(8,128)S(1)}, f32[32,128]{1,0:T(8,128)S(1)}, u32[]{:S(2)}, u32[]{:S(2)}) %collective-permute-start.8) | collective-permute-done | bytes 16416 | tf_op jit(solution)/shard_map/ppermute | solution.py:835
  32.1 1.9 %collective-permute-start.11 = (f32[32,128]{1,0:T(8,128)S(1)}, f32[32,128]{1,0:T(8,128)S(1)}, u32[]{:S(2)}, u32[]{:S(2)}) collective-permute-start(f32[32,128]{1,0:T(8,128)S(1)} %add.30.refs_0_), channel_id=1, source_target_pairs={{0,80},{1,81},{2,82},{3,83},{4,84},{5,85},{6,86},{7,87},{8,88},{9,... | collective-permute-start | bytes 49160 | tf_op jit(solution)/shard_map/ppermute | solution.py:835
  34.0 0.8 %collective-permute-start.10 = (f32[32,128]{1,0:T(8,128)S(1)}, f32[32,128]{1,0:T(8,128)S(1)}, u32[]{:S(2)}, u32[]{:S(2)}) collective-permute-start(f32[32,128]{1,0:T(8,128)S(1)} %add.30.refs_0_), channel_id=1, source_target_pairs={{0,112},{1,113},{2,114},{3,115},{4,116},{5,117},{6,118},{7,119},{8... | collective-permute-start | bytes 49160 | tf_op jit(solution)/shard_map/ppermute | solution.py:835
  35.8 1.5 %first_adjoint.3.refs_1_ = f32[19,16,8,128]{3,2,1,0:T(8,128)} custom-call(f32[3,16,8,128]{3,2,1,0:T(8,128)S(1)} %first_speed.1.speed, f32[16,8,128]{2,1,0:T(8,128)S(1)} %copy-done.3, f32[19,16,8,128]{3,2,1,0:T(8,128)S(1)} %get-tuple-element.58.adj, f32[18,24,128]{2,1,0:T(8,128)S(1)} %get-tuple-element.61.fluid_pad, f32[80,128]{1,0:T(8,128)S(1)} %collective-permute-done.4.ya, ...), custom_call_target="tpu_custom_call" | custom-call | tf_op jit(solution)/shard_map/first_adjoint/pallas_call | solution.py:779
  37.3 1.1 %collective-permute-done.10 = f32[32,128]{1,0:T(8,128)S(1)} collective-permute-done((f32[32,128]{1,0:T(8,128)S(1)}, f32[32,128]{1,0:T(8,128)S(1)}, u32[]{:S(2)}, u32[]{:S(2)}) %collective-permute-start.10) | collective-permute-done | bytes 16416 | tf_op jit(solution)/shard_map/ppermute | solution.py:835
  38.5 0.9 %collective-permute-start.13 = (f32[32,128]{1,0:T(8,128)S(1)}, f32[32,128]{1,0:T(8,128)S(1)}, u32[]{:S(2)}, u32[]{:S(2)}) collective-permute-start(f32[32,128]{1,0:T(8,128)S(1)} %add_add_fusion.1.refs_0_), channel_id=1, source_target_pairs={{0,19},{1,18},{2,17},{3,16},{4,23},{5,22},{6,21},{7,20},{8,27},{9,... | collective-permute-start | bytes 49160 | tf_op jit(solution)/shard_map/ppermute | solution.py:835
  39.4 2.0 %collective-permute-start.12 = (f32[32,128]{1,0:T(8,128)S(1)}, f32[32,128]{1,0:T(8,128)S(1)}, u32[]{:S(2)}, u32[]{:S(2)}) collective-permute-start(f32[32,128]{1,0:T(8,128)S(1)} %add_add_fusion.1.refs_0_), channel_id=1, source_target_pairs={{0,17},{1,16},{2,19},{3,18},{4,21},{5,20},{6,23},{7,22},{8,25},{9,... | collective-permute-start | bytes 49160 | tf_op jit(solution)/shard_map/ppermute | solution.py:835
  41.4 1.4 %first_adjoint.4.refs_1_ = f32[19,16,8,128]{3,2,1,0:T(8,128)} custom-call(f32[3,16,8,128]{3,2,1,0:T(8,128)S(1)} %first_speed.1.speed, f32[16,8,128]{2,1,0:T(8,128)S(1)} %copy-done.3, f32[19,16,8,128]{3,2,1,0:T(8,128)S(1)} %get-tuple-element.58.adj, f32[18,24,128]{2,1,0:T(8,128)S(1)} %get-tuple-element.61.fluid_pad, ...), custom_call_target="tpu_custom_call", output_to_operand_aliasing={{}: (10, {})} | custom-call | tf_op jit(solution)/shard_map/first_adjoint/pallas_call | solution.py:779
  43.1 0.8 %collective-permute-start.17 = (f32[32,128]{1,0:T(8,128)S(1)}, f32[32,128]{1,0:T(8,128)S(1)}, u32[]{:S(2)}, u32[]{:S(2)}) collective-permute-start(f32[32,128]{1,0:T(8,128)S(1)} %add_add_fusion.refs_0_), channel_id=1, source_target_pairs={{0,24},{1,25},{2,26},{3,27},{4,28},{5,29},{6,30},{7,31},{8,16},{9,... | collective-permute-start | bytes 49160 | tf_op jit(solution)/shard_map/ppermute | solution.py:835
  43.9 1.6 %collective-permute-start.16 = (f32[32,128]{1,0:T(8,128)S(1)}, f32[32,128]{1,0:T(8,128)S(1)}, u32[]{:S(2)}, u32[]{:S(2)}) collective-permute-start(f32[32,128]{1,0:T(8,128)S(1)} %add_add_fusion.refs_0_), channel_id=1, source_target_pairs={{0,28},{1,29},{2,30},{3,31},{4,24},{5,25},{6,26},{7,27},{8,20},{9,... | collective-permute-start | bytes 49160 | tf_op jit(solution)/shard_map/ppermute | solution.py:835
  46.2 1.4 %first_adjoint.5 = f32[19,16,8,128]{3,2,1,0:T(8,128)} custom-call(f32[3,16,8,128]{3,2,1,0:T(8,128)S(1)} %first_speed.1.speed, f32[16,8,128]{2,1,0:T(8,128)S(1)} %copy-done.3, f32[19,16,8,128]{3,2,1,0:T(8,128)S(1)} %get-tuple-element.58.adj, f32[18,24,128]{2,1,0:T(8,128)S(1)} %get-tuple-element.61.fluid_pad, ...), custom_call_target="tpu_custom_call", output_to_operand_aliasing={{}: (10, {})} | custom-call | tf_op jit(solution)/shard_map/first_adjoint/pallas_call | solution.py:779
  (47 shorter events, 6.8 us)
Async XLA Ops:
  0.6 8.6 %copy-start.2 = (s32[16,8,128]{2,1,0:T(8,128)S(1)}, s32[16,8,128]{2,1,0:T(8,128)}, u32[]{:S(2)}) copy-start(s32[16,8,128]{2,1,0:T(8,128)} %fluid.5) | copy-start | bytes 196612
  0.6 8.6 %copy-start.3 = (f32[16,8,128]{2,1,0:T(8,128)S(1)}, f32[16,8,128]{2,1,0:T(8,128)}, u32[]{:S(2)}) copy-start(f32[16,8,128]{2,1,0:T(8,128)} %phase.9) | copy-start | bytes 196612
  0.7 8.6 %copy-start.5 = (f32[16,8,128]{2,1,0:T(8,128)S(1)}, f32[16,8,128]{2,1,0:T(8,128)}, u32[]{:S(2)}) copy-start(f32[16,8,128]{2,1,0:T(8,128)} %phase.6) | copy-start | bytes 196612
  0.7 8.6 %copy-start.7 = (s32[16,8,128]{2,1,0:T(8,128)S(1)}, s32[16,8,128]{2,1,0:T(8,128)}, u32[]{:S(2)}) copy-start(s32[16,8,128]{2,1,0:T(8,128)} %refs_4_.1) | copy-start | bytes 196612
  0.7 8.6 %copy-start.6 = (s32[16,8,128]{2,1,0:T(8,128)S(1)}, s32[16,8,128]{2,1,0:T(8,128)}, u32[]{:S(2)}) copy-start(s32[16,8,128]{2,1,0:T(8,128)} %refs_3_.1) | copy-start | bytes 196612
  2.4 14.5 %copy-start = (f32[19,16,8,128]{3,2,1,0:T(8,128)S(1)}, f32[19,16,8,128]{3,2,1,0:T(8,128)}, u32[]{:S(2)}) copy-start(f32[19,16,8,128]{3,2,1,0:T(8,128)} %adj.3) | copy-start | bytes 3735556
  2.4 9.8 %collective-permute-start = (f32[226,128]{1,0:T(8,128)S(1)}, f32[226,128]{1,0:T(8,128)S(1)}, u32[]{:S(2)}, u32[]{:S(2)}) collective-permute-start(f32[226,128]{1,0:T(8,128)S(1)} %get-tuple-element.48), channel_id=1, source_target_pairs={{0,15},{1,2},{2,1},{3,4},{4,3},{5,6},{6,5},{7,8},{8,7},{9,10},{10,... | collective-permute-start | bytes 347144 | tf_op jit(solution)/shard_map/ppermute | solution.py:798
  9.3 3.8 %collective-permute-start.1 = (f32[226,128]{1,0:T(8,128)S(1)}, f32[226,128]{1,0:T(8,128)S(1)}, u32[]{:S(2)}, u32[]{:S(2)}) collective-permute-start(f32[226,128]{1,0:T(8,128)S(1)} %get-tuple-element.49), channel_id=1, source_target_pairs={{0,1},{1,0},{2,3},{3,2},{4,5},{5,4},{6,7},{7,6},{8,9},{9,8},{10,11... | collective-permute-start | bytes 347144 | tf_op jit(solution)/shard_map/ppermute | solution.py:797
  13.1 4.6 %collective-permute-start.2 = (f32[22,8,128]{2,1,0:T(8,128)S(1)}, f32[22,8,128]{2,1,0:T(8,128)S(1)}, u32[]{:S(2)}, u32[]{:S(2)}) collective-permute-start(f32[22,8,128]{2,1,0:T(8,128)S(1)} %get-tuple-element.53), channel_id=1, source_target_pairs={{0,16},{16,0},{32,48},{48,32},{64,80},{80,64},{96,112},{112,96},{1... | collective-permute-start | bytes 270344 | tf_op jit(solution)/shard_map/ppermute | solution.py:797
  15.2 4.2 %collective-permute-start.3 = (f32[22,8,128]{2,1,0:T(8,128)S(1)}, f32[22,8,128]{2,1,0:T(8,128)S(1)}, u32[]{:S(2)}, u32[]{:S(2)}) collective-permute-start(f32[22,8,128]{2,1,0:T(8,128)S(1)} %get-tuple-element.54), channel_id=1, source_target_pairs={{0,112},{16,32},{32,16},{48,64},{64,48},{80,96},{96,80},{112,0},{1... | collective-permute-start | bytes 270344 | tf_op jit(solution)/shard_map/ppermute | solution.py:798
  19.7 5.6 %collective-permute-start.4 = (f32[80,128]{1,0:T(8,128)S(1)}, f32[80,128]{1,0:T(8,128)S(1)}, u32[]{:S(2)}, u32[]{:S(2)}) collective-permute-start(f32[80,128]{1,0:T(8,128)S(1)} %get-tuple-element.64), channel_id=1, source_target_pairs={{0,1},{1,0},{2,3},{3,2},{4,5},{5,4},{6,7},{7,6},{8,9},{9,8},{10,11... | collective-permute-start | bytes 122888 | tf_op jit(solution)/shard_map/ppermute | solution.py:797
  19.8 6.3 %collective-permute-start.5 = (f32[80,128]{1,0:T(8,128)S(1)}, f32[80,128]{1,0:T(8,128)S(1)}, u32[]{:S(2)}, u32[]{:S(2)}) collective-permute-start(f32[80,128]{1,0:T(8,128)S(1)} %get-tuple-element.65), channel_id=1, source_target_pairs={{0,15},{1,2},{2,1},{3,4},{4,3},{5,6},{6,5},{7,8},{8,7},{9,10},{10,... | collective-permute-start | bytes 122888 | tf_op jit(solution)/shard_map/ppermute | solution.py:798
  23.1 4.7 %collective-permute-start.6 = (f32[5,8,128]{2,1,0:T(8,128)S(1)}, f32[5,8,128]{2,1,0:T(8,128)S(1)}, u32[]{:S(2)}, u32[]{:S(2)}) collective-permute-start(f32[5,8,128]{2,1,0:T(8,128)S(1)} %get-tuple-element.66), channel_id=1, source_target_pairs={{0,16},{16,0},{32,48},{48,32},{64,80},{80,64},{96,112},{112,96},{1... | collective-permute-start | bytes 61448 | tf_op jit(solution)/shard_map/ppermute | solution.py:797
  24.5 3.5 %collective-permute-start.7 = (f32[5,8,128]{2,1,0:T(8,128)S(1)}, f32[5,8,128]{2,1,0:T(8,128)S(1)}, u32[]{:S(2)}, u32[]{:S(2)}) collective-permute-start(f32[5,8,128]{2,1,0:T(8,128)S(1)} %get-tuple-element.67), channel_id=1, source_target_pairs={{0,112},{16,32},{32,16},{48,64},{64,48},{80,96},{96,80},{112,0},{1... | collective-permute-start | bytes 61448 | tf_op jit(solution)/shard_map/ppermute | solution.py:798
  29.1 3.0 %collective-permute-start.8 = (f32[32,128]{1,0:T(8,128)S(1)}, f32[32,128]{1,0:T(8,128)S(1)}, u32[]{:S(2)}, u32[]{:S(2)}) collective-permute-start(f32[32,128]{1,0:T(8,128)S(1)} %first_outer.1._), channel_id=1, source_target_pairs={{0,16},{1,17},{2,18},{3,19},{4,20},{5,21},{6,22},{7,23},{8,24},{9,... | collective-permute-start | bytes 49160 | tf_op jit(solution)/shard_map/ppermute | solution.py:835
  32.1 5.2 %collective-permute-start.11 = (f32[32,128]{1,0:T(8,128)S(1)}, f32[32,128]{1,0:T(8,128)S(1)}, u32[]{:S(2)}, u32[]{:S(2)}) collective-permute-start(f32[32,128]{1,0:T(8,128)S(1)} %add.30.refs_0_), channel_id=1, source_target_pairs={{0,80},{1,81},{2,82},{3,83},{4,84},{5,85},{6,86},{7,87},{8,88},{9,... | collective-permute-start | bytes 49160 | tf_op jit(solution)/shard_map/ppermute | solution.py:835
  34.0 4.4 %collective-permute-start.10 = (f32[32,128]{1,0:T(8,128)S(1)}, f32[32,128]{1,0:T(8,128)S(1)}, u32[]{:S(2)}, u32[]{:S(2)}) collective-permute-start(f32[32,128]{1,0:T(8,128)S(1)} %add.30.refs_0_), channel_id=1, source_target_pairs={{0,112},{1,113},{2,114},{3,115},{4,116},{5,117},{6,118},{7,119},{8... | collective-permute-start | bytes 49160 | tf_op jit(solution)/shard_map/ppermute | solution.py:835
  34.8 3.6 %collective-permute-start.9 = (f32[32,128]{1,0:T(8,128)S(1)}, f32[32,128]{1,0:T(8,128)S(1)}, u32[]{:S(2)}, u32[]{:S(2)}) collective-permute-start(f32[32,128]{1,0:T(8,128)S(1)} %add.30.refs_0_), channel_id=1, source_target_pairs={{0,48},{1,49},{2,50},{3,51},{4,52},{5,53},{6,54},{7,55},{8,56},{9,... | collective-permute-start | bytes 49160 | tf_op jit(solution)/shard_map/ppermute | solution.py:835
  38.4 4.7 %collective-permute-start.14 = (f32[32,128]{1,0:T(8,128)S(1)}, f32[32,128]{1,0:T(8,128)S(1)}, u32[]{:S(2)}, u32[]{:S(2)}) collective-permute-start(f32[32,128]{1,0:T(8,128)S(1)} %add_add_fusion.1.refs_0_), channel_id=1, source_target_pairs={{0,18},{1,19},{2,16},{3,17},{4,22},{5,23},{6,20},{7,21},{8,26},{9,... | collective-permute-start | bytes 49160 | tf_op jit(solution)/shard_map/ppermute | solution.py:835
  38.5 4.7 %collective-permute-start.13 = (f32[32,128]{1,0:T(8,128)S(1)}, f32[32,128]{1,0:T(8,128)S(1)}, u32[]{:S(2)}, u32[]{:S(2)}) collective-permute-start(f32[32,128]{1,0:T(8,128)S(1)} %add_add_fusion.1.refs_0_), channel_id=1, source_target_pairs={{0,19},{1,18},{2,17},{3,16},{4,23},{5,22},{6,21},{7,20},{8,27},{9,... | collective-permute-start | bytes 49160 | tf_op jit(solution)/shard_map/ppermute | solution.py:835
  39.4 3.7 %collective-permute-start.12 = (f32[32,128]{1,0:T(8,128)S(1)}, f32[32,128]{1,0:T(8,128)S(1)}, u32[]{:S(2)}, u32[]{:S(2)}) collective-permute-start(f32[32,128]{1,0:T(8,128)S(1)} %add_add_fusion.1.refs_0_), channel_id=1, source_target_pairs={{0,17},{1,16},{2,19},{3,18},{4,21},{5,20},{6,23},{7,22},{8,25},{9,... | collective-permute-start | bytes 49160 | tf_op jit(solution)/shard_map/ppermute | solution.py:835
  43.1 4.8 %collective-permute-start.17 = (f32[32,128]{1,0:T(8,128)S(1)}, f32[32,128]{1,0:T(8,128)S(1)}, u32[]{:S(2)}, u32[]{:S(2)}) collective-permute-start(f32[32,128]{1,0:T(8,128)S(1)} %add_add_fusion.refs_0_), channel_id=1, source_target_pairs={{0,24},{1,25},{2,26},{3,27},{4,28},{5,29},{6,30},{7,31},{8,16},{9,... | collective-permute-start | bytes 49160 | tf_op jit(solution)/shard_map/ppermute | solution.py:835
  43.9 4.4 %collective-permute-start.16 = (f32[32,128]{1,0:T(8,128)S(1)}, f32[32,128]{1,0:T(8,128)S(1)}, u32[]{:S(2)}, u32[]{:S(2)}) collective-permute-start(f32[32,128]{1,0:T(8,128)S(1)} %add_add_fusion.refs_0_), channel_id=1, source_target_pairs={{0,28},{1,29},{2,30},{3,31},{4,24},{5,25},{6,26},{7,27},{8,20},{9,... | collective-permute-start | bytes 49160 | tf_op jit(solution)/shard_map/ppermute | solution.py:835
  45.5 3.2 %collective-permute-start.15 = (f32[32,128]{1,0:T(8,128)S(1)}, f32[32,128]{1,0:T(8,128)S(1)}, u32[]{:S(2)}, u32[]{:S(2)}) collective-permute-start(f32[32,128]{1,0:T(8,128)S(1)} %add_add_fusion.refs_0_), channel_id=1, source_target_pairs={{0,20},{1,21},{2,22},{3,23},{4,16},{5,17},{6,18},{7,19},{8,28},{9,... | collective-permute-start | bytes 49160 | tf_op jit(solution)/shard_map/ppermute | solution.py:835
  (3 other events, 24.5 us)

commit v6 on v5

--- a/solution.py
+++ b/solution.py
@@ -227,7 +227,7 @@
 
 def put_pops(adj, x_outs, y_outs):
     odd_x, odd_y = is_odd("pipe"), is_odd("cross")
-    flat = adj.reshape(19 * NX * NY, NZ)
+    flat = adj.reshape(adj.shape[0] * NX * NY, NZ)
     for k in range(5):
         put(odd_x, x_outs, k, adj[x_plus[k], 0], adj[x_minus[k], NX - 1])
         put_rows(odd_y, y_outs, k, flat, y_plus[k] * NX * NY, y_minus[k] * NX * NY + NY - 1)
@@ -247,7 +247,7 @@
 def corner_rows(adj, fluid, speed, side, sign):
     x, step = ((0, 1), (NX - 1, -1))[side]
     y = 0 if sign > 0 else NY - 1
-    flat = adj.reshape(19 * NX * NY, NZ)
+    flat = adj.reshape(adj.shape[0] * NX * NY, NZ)
     rows = [flat[pl.ds(x * NY + y, 19, stride=NX * NY), :]]
     rows += [speed[d][y : y + 1, :] for d in range(3)]
 
@@ -265,7 +265,7 @@
     hbm, pops_hbm, (xa, xb, ya, yb) = refs[:FIELDS], refs[FIELDS], refs[FIELDS + 1 : FIELDS + 5]
     adj, *fields = refs[FIELDS + 5 : -2]
     pops, sem = refs[-2:]
-    pairs = [(adj_hbm, adj), *zip(hbm, fields)]
+    pairs = [(adj_hbm, adj.at[pl.ds(0, 19)]), *zip(hbm, fields)]
     pairs += [(pops_hbm.at[:, x], pops.at[:, k]) for k, x in enumerate((0, NX - 1))]
     for copy in fetch(pairs, sem):
         copy.wait()
@@ -293,6 +293,7 @@
             put(odd_x, flats, (pl.ds(corner_at(e) + EXTRA + k, 1), slice(None)), up, down)
 
 
+Y_ROWS = (5 + FIELDS) * NX + 80
 X_PLANES = 5 + FIELDS + 2 + 10
 
 
@@ -301,8 +302,8 @@
 
 
 def pack(adjoint, fields, pops):
-    face, side = ((X_PLANES, NY, NZ), f32), (((5 + FIELDS) * NX + 2 * EXTRA, NZ), f32)
-    scratch = [pltpu.VMEM((19, NX, NY, NZ), f32)]
+    face, side = ((X_PLANES, NY, NZ), f32), ((Y_ROWS, NZ), f32)
+    scratch = [pltpu.VMEM((24, NX, NY, NZ), f32)]
     scratch += [pltpu.VMEM((NX, NY, NZ), field.dtype) for field in fields]
     scratch.append(pltpu.VMEM((19, 2, NY, NZ), f32))
     scratch.append(pltpu.SemaphoreType.DMA((3 + FIELDS,)))
@@ -692,7 +693,7 @@
 ):
     y_low, y_high = sides("cross", ya, yb)
     fill_pops(adj_pad, adj, range(NX), y_low, y_high)
-    dgrad_pad[...] = jnp.zeros_like(dgrad_pad)
+    dgrad_pad[pl.ds(0, 3)] = jnp.zeros((3, WX + 2, ROWS, NZ), f32)
 
     def out(d, x, value):
         dgrad_out[d, x] = value
@@ -736,11 +737,11 @@
         nodes = pl.ds(start * NY * NZ, 2 * NY * NZ)
         total = total + table_sum(weighted(hits[:, nodes], values[2 * k : 2 * k + 2]), rights[:, nodes])
     values = [plane_adjoint(dgrad_pad, x) * wall_face[k] for k, x in enumerate((0, WX - 1))]
-    flat = dgrad_pad.reshape(3 * (WX + 2) * ROWS, NZ)
+    flat = dgrad_pad.reshape(4 * (WX + 2) * ROWS, NZ)
     beside, corners = [], []
     for side, (row, sign) in enumerate(((LOW, 1.0), (LOW + NY - 1, -1.0))):
         for d in range(3):
-            rows[d] = flat[pl.ds(d * (WX + 2) * ROWS + row, WX + 2, stride=ROWS), :]
+            rows[d, pl.ds(0, WX + 2), :] = flat[pl.ds(d * (WX + 2) * ROWS + row, WX + 2, stride=ROWS), :]
         value = side_adjoint(rows, sign) * wall_side[side]
         beside.append(value[1 : WX - 1])
         corners += [value[:1], value[WX - 1 :]]
@@ -878,7 +879,7 @@
     given = (adjoint, fluid_pad, grad, dgrad, *y_halo2)
     nodes = (wall_own, hits, rights)
     adj_scratch = pad_scratch()[:1]
-    dgrad_scratch = adj_scratch + [pltpu.VMEM((3, WX + 2, ROWS, NZ), f32)]
+    dgrad_scratch = adj_scratch + [pltpu.VMEM((4, WX + 2, ROWS, NZ), f32)]
     dgrad_inner, acc = whole_call(
         first_inner_kernel, "first_inner", [vector, ((128, 64), f32)], given + nodes, dgrad_scratch
     )
@@ -887,7 +888,7 @@
         "first_outer",
         [((32, NZ), f32)],
         given + x_halo2 + (edges, dgrad_inner, acc) + nodes + (wall_face, wall_side, face_hits, face_rights, side_hits, side_rights),
-        dgrad_scratch + [pltpu.VMEM((3, WX + 2, NZ), f32)],
+        dgrad_scratch + [pltpu.VMEM((4, 32, NZ), f32)],
     )
     args = (first_speed(pops_first, total), phase_first, adjoint, fluid_pad, *y_halo2, *x_halo2, edges)
     result = None

time: 49.4 us -> 49.5 us (level)
  no operation moved by 1% of the time
where the time goes in v6:
time: 49.5 us; the launch traced here: 49.3 us
  starting transfers between devices  26.4 us (53%)
  Pallas kernels  14.1 us (28%)
  waiting for transfers between devices  7.26 us (15%)
  between operations  0.9 us (2%)
  other arithmetic  0.63 us (1%)
    ppermute x4, starting transfers between devices, swap(): lax.ppermute(b, axis, [(i, (i + 2 * (i % 2) - 1) % count) for i in range(...  11.5 us
    ppermute x10, starting transfers between devices, exchange(): return lax.ppermute(value, ('pipe', 'cross'), pairs)  11.4 us
    pallas_call x10, Pallas kernels, whole_call(): pl.pallas_call(kernel, out_shape=[pltpu.VMEM(shape, kind) if in_hbm else...  9.89 us
    pallas_call x3, Pallas kernels, first_adjoint(): pl.pallas_call(functools.partial(first_adjoint_kernel, start, count), out...  4.23 us
    ppermute x4, starting transfers between devices, swap(): near = lax.ppermute(a, axis, [(i, i ^ 1) for i in range(count)])  3.49 us
    ppermute x10, waiting for transfers between devices, exchange(): return lax.ppermute(value, ('pipe', 'cross'), pairs)  3.33 us
    ppermute x4, waiting for transfers between devices, swap(): lax.ppermute(b, axis, [(i, (i + 2 * (i % 2) - 1) % count) for i in range(...  3.1 us
  transfers between devices with their start and end apart: 18, of which 11 were waited for; matrix products, arithmetic and copies ran while one was open for 0% of the time, Pallas kernels for 22%

profile of v6, /device:TPU:1, one launch (start us, length us, event | category | flops | bytes accessed | tf_op | source)
XLA Modules:
  0.0 49.3 jit_solution(7682589945284168371)
XLA Ops:
  0.7 1.7 %pack.1 = (f32[22,8,128]{2,1,0:T(8,128)S(1)}, f32[22,8,128]{2,1,0:T(8,128)S(1)}, f32[240,128]{1,0:T(8,128)S(1)}, f32[240,128]{1,0:T(8,128)S(1)}) custom-call(f32[19,16,8,128]{3,2,1,0:T(8,128)} %adj.3, f32[16,8,128]{2,1,0:T(8,128)} %phase.9, f32[16,8,128]{2,1,0:T(8,128)} %phase.6, s32[16,8,128]{2,1,0:T(8,128)} %fluid.5, s32[16,8,128]{2,1,0:T(8,128)} %refs_3_.1, ...), custom_call_target="tpu_custom_call" | custom-call | tf_op jit(solution)/shard_map/pack/pallas_call | solution.py:189
  2.4 6.9 %collective-permute-start = (f32[240,128]{1,0:T(8,128)S(1)}, f32[240,128]{1,0:T(8,128)S(1)}, u32[]{:S(2)}, u32[]{:S(2)}) collective-permute-start(f32[240,128]{1,0:T(8,128)S(1)} %get-tuple-element.48), channel_id=1, source_target_pairs={{0,15},{1,2},{2,1},{3,4},{4,3},{5,6},{6,5},{7,8},{8,7},{9,10},{10,... | collective-permute-start | bytes 368648 | tf_op jit(solution)/shard_map/ppermute | solution.py:799
  9.3 2.6 %own_terms.1 = (f32[2,16,8,128]{3,2,1,0:T(8,128)S(1)}, bf16[64,16384]{1,0:T(8,128)(2,1)S(1)}, bf16[64,16384]{1,0:T(8,128)(2,1)S(1)}, f32[16,8,128]{2,1,0:T(8,128)S(1)}, f32[3,16,8,128]{3,2,1,0:T(8,128)S(1)}) custom-call(f32[32,128]{1,0:T(8,128)S(1)} %bitcast.3, f32[16,8,128]{2,1,0:T(8,128)S(1)} %copy-done.3, f32[16,8,128]{2,1,0:T(8,128)S(1)} %copy-done.5, ...), custom_call_target="tpu_custom_call" | custom-call | tf_op jit(solution)/shard_map/own_terms/pallas_call | solution.py:189
  12.3 0.8 %collective-permute-done.1.ya = f32[240,128]{1,0:T(8,128)S(1)} collective-permute-done((f32[240,128]{1,0:T(8,128)S(1)}, f32[240,128]{1,0:T(8,128)S(1)}, u32[]{:S(2)}, u32[]{:S(2)}) %collective-permute-start.1) | collective-permute-done | bytes 122912 | tf_op jit(solution)/shard_map/ppermute | solution.py:798
  13.2 2.0 %collective-permute-start.2 = (f32[22,8,128]{2,1,0:T(8,128)S(1)}, f32[22,8,128]{2,1,0:T(8,128)S(1)}, u32[]{:S(2)}, u32[]{:S(2)}) collective-permute-start(f32[22,8,128]{2,1,0:T(8,128)S(1)} %get-tuple-element.53), channel_id=1, source_target_pairs={{0,16},{16,0},{32,48},{48,32},{64,80},{80,64},{96,112},{112,96},{1... | collective-permute-start | bytes 270344 | tf_op jit(solution)/shard_map/ppermute | solution.py:798
  15.2 1.3 %collective-permute-start.3 = (f32[22,8,128]{2,1,0:T(8,128)S(1)}, f32[22,8,128]{2,1,0:T(8,128)S(1)}, u32[]{:S(2)}, u32[]{:S(2)}) collective-permute-start(f32[22,8,128]{2,1,0:T(8,128)S(1)} %get-tuple-element.54), channel_id=1, source_target_pairs={{0,112},{16,32},{32,16},{48,64},{64,48},{80,96},{96,80},{112,0},{1... | collective-permute-start | bytes 270344 | tf_op jit(solution)/shard_map/ppermute | solution.py:799
  17.7 1.7 %collective-permute-done.3.xb = f32[22,8,128]{2,1,0:T(8,128)S(1)} collective-permute-done((f32[22,8,128]{2,1,0:T(8,128)S(1)}, f32[22,8,128]{2,1,0:T(8,128)S(1)}, u32[]{:S(2)}, u32[]{:S(2)}) %collective-permute-start.3) | collective-permute-done | bytes 90144 | tf_op jit(solution)/shard_map/ppermute | solution.py:799
  19.9 3.3 %collective-permute-start.5 = (f32[80,128]{1,0:T(8,128)S(1)}, f32[80,128]{1,0:T(8,128)S(1)}, u32[]{:S(2)}, u32[]{:S(2)}) collective-permute-start(f32[80,128]{1,0:T(8,128)S(1)} %get-tuple-element.65), channel_id=1, source_target_pairs={{0,15},{1,2},{2,1},{3,4},{4,3},{5,6},{6,5},{7,8},{8,7},{9,10},{10,... | collective-permute-start | bytes 122888 | tf_op jit(solution)/shard_map/ppermute | solution.py:799
  23.2 1.4 %collective-permute-start.6 = (f32[5,8,128]{2,1,0:T(8,128)S(1)}, f32[5,8,128]{2,1,0:T(8,128)S(1)}, u32[]{:S(2)}, u32[]{:S(2)}) collective-permute-start(f32[5,8,128]{2,1,0:T(8,128)S(1)} %get-tuple-element.66), channel_id=1, source_target_pairs={{0,16},{16,0},{32,48},{48,32},{64,80},{80,64},{96,112},{112,96},{1... | collective-permute-start | bytes 61448 | tf_op jit(solution)/shard_map/ppermute | solution.py:798
  24.6 0.8 %middle.1 = (f32[3,16,8,128]{3,2,1,0:T(8,128)S(1)}, f32[3,16,8,128]{3,2,1,0:T(8,128)S(1)}, f32[18,24,128]{2,1,0:T(8,128)S(1)}, f32[2,8,128]{2,1,0:T(8,128)S(1)},...) custom-call(f32[2,16,8,128]{3,2,1,0:T(8,128)S(1)} %get-tuple-element.52._.phi, ...), custom_call_target="tpu_custom_call" | custom-call | tf_op jit(solution)/shard_map/middle/pallas_call | solution.py:189
  26.1 1.7 %first_inner.1 = (f32[3,16,8,128]{3,2,1,0:T(8,128)S(1)}, f32[128,64]{1,0:T(8,128)S(1)}) custom-call(f32[19,16,8,128]{3,2,1,0:T(8,128)S(1)} %get-tuple-element.58.adj, f32[18,24,128]{2,1,0:T(8,128)S(1)} %get-tuple-element.61.fluid_pad, f32[3,16,8,128]{3,2,1,0:T(8,128)S(1)} %get-tuple-element.62.grad, f32[3,16,8,128]{3,2,1,0:T(8,128)S(1)} %get-tuple-element.63.dgrad_in, ...), custom_call_target="tpu_custom_call" | custom-call | tf_op jit(solution)/shard_map/first_inner/pallas_call | solution.py:189
  28.0 1.2 %first_outer.1._ = f32[32,128]{1,0:T(8,128)S(1)} custom-call(f32[19,16,8,128]{3,2,1,0:T(8,128)S(1)} %get-tuple-element.58.adj, f32[18,24,128]{2,1,0:T(8,128)S(1)} %get-tuple-element.61.fluid_pad, f32[3,16,8,128]{3,2,1,0:T(8,128)S(1)} %get-tuple-element.62.grad, f32[3,16,8,128]{3,2,1,0:T(8,128)S(1)} %get-tuple-element.63.dgrad_in, ...), custom_call_target="tpu_custom_call" | custom-call | tf_op jit(solution)/shard_map/first_outer/pallas_call | solution.py:189
  29.2 2.2 %collective-permute-start.8 = (f32[32,128]{1,0:T(8,128)S(1)}, f32[32,128]{1,0:T(8,128)S(1)}, u32[]{:S(2)}, u32[]{:S(2)}) collective-permute-start(f32[32,128]{1,0:T(8,128)S(1)} %first_outer.1._), channel_id=1, source_target_pairs={{0,16},{1,17},{2,18},{3,19},{4,20},{5,21},{6,22},{7,23},{8,24},{9,... | collective-permute-start | bytes 49160 | tf_op jit(solution)/shard_map/ppermute | solution.py:836
  31.4 0.8 %collective-permute-done.8 = f32[32,128]{1,0:T(8,128)S(1)} collective-permute-done((f32[32,128]{1,0:T(8,128)S(1)}, f32[32,128]{1,0:T(8,128)S(1)}, u32[]{:S(2)}, u32[]{:S(2)}) %collective-permute-start.8) | collective-permute-done | bytes 16416 | tf_op jit(solution)/shard_map/ppermute | solution.py:836
  32.2 1.9 %collective-permute-start.11 = (f32[32,128]{1,0:T(8,128)S(1)}, f32[32,128]{1,0:T(8,128)S(1)}, u32[]{:S(2)}, u32[]{:S(2)}) collective-permute-start(f32[32,128]{1,0:T(8,128)S(1)} %add.30.refs_0_), channel_id=1, source_target_pairs={{0,80},{1,81},{2,82},{3,83},{4,84},{5,85},{6,86},{7,87},{8,88},{9,... | collective-permute-start | bytes 49160 | tf_op jit(solution)/shard_map/ppermute | solution.py:836
  34.1 0.8 %collective-permute-start.10 = (f32[32,128]{1,0:T(8,128)S(1)}, f32[32,128]{1,0:T(8,128)S(1)}, u32[]{:S(2)}, u32[]{:S(2)}) collective-permute-start(f32[32,128]{1,0:T(8,128)S(1)} %add.30.refs_0_), channel_id=1, source_target_pairs={{0,112},{1,113},{2,114},{3,115},{4,116},{5,117},{6,118},{7,119},{8... | collective-permute-start | bytes 49160 | tf_op jit(solution)/shard_map/ppermute | solution.py:836
  35.8 1.5 %first_adjoint.3.refs_1_ = f32[19,16,8,128]{3,2,1,0:T(8,128)} custom-call(f32[3,16,8,128]{3,2,1,0:T(8,128)S(1)} %first_speed.1.speed, f32[16,8,128]{2,1,0:T(8,128)S(1)} %copy-done.3, f32[19,16,8,128]{3,2,1,0:T(8,128)S(1)} %get-tuple-element.58.adj, f32[18,24,128]{2,1,0:T(8,128)S(1)} %get-tuple-element.61.fluid_pad, f32[80,128]{1,0:T(8,128)S(1)} %collective-permute-done.4.ya, ...), custom_call_target="tpu_custom_call" | custom-call | tf_op jit(solution)/shard_map/first_adjoint/pallas_call | solution.py:780
  37.4 1.1 %collective-permute-done.10 = f32[32,128]{1,0:T(8,128)S(1)} collective-permute-done((f32[32,128]{1,0:T(8,128)S(1)}, f32[32,128]{1,0:T(8,128)S(1)}, u32[]{:S(2)}, u32[]{:S(2)}) %collective-permute-start.10) | collective-permute-done | bytes 16416 | tf_op jit(solution)/shard_map/ppermute | solution.py:836
  38.5 0.9 %collective-permute-start.13 = (f32[32,128]{1,0:T(8,128)S(1)}, f32[32,128]{1,0:T(8,128)S(1)}, u32[]{:S(2)}, u32[]{:S(2)}) collective-permute-start(f32[32,128]{1,0:T(8,128)S(1)} %add_add_fusion.1.refs_0_), channel_id=1, source_target_pairs={{0,19},{1,18},{2,17},{3,16},{4,23},{5,22},{6,21},{7,20},{8,27},{9,... | collective-permute-start | bytes 49160 | tf_op jit(solution)/shard_map/ppermute | solution.py:836
  39.4 2.1 %collective-permute-start.12 = (f32[32,128]{1,0:T(8,128)S(1)}, f32[32,128]{1,0:T(8,128)S(1)}, u32[]{:S(2)}, u32[]{:S(2)}) collective-permute-start(f32[32,128]{1,0:T(8,128)S(1)} %add_add_fusion.1.refs_0_), channel_id=1, source_target_pairs={{0,17},{1,16},{2,19},{3,18},{4,21},{5,20},{6,23},{7,22},{8,25},{9,... | collective-permute-start | bytes 49160 | tf_op jit(solution)/shard_map/ppermute | solution.py:836
  41.5 1.4 %first_adjoint.4.refs_1_ = f32[19,16,8,128]{3,2,1,0:T(8,128)} custom-call(f32[3,16,8,128]{3,2,1,0:T(8,128)S(1)} %first_speed.1.speed, f32[16,8,128]{2,1,0:T(8,128)S(1)} %copy-done.3, f32[19,16,8,128]{3,2,1,0:T(8,128)S(1)} %get-tuple-element.58.adj, f32[18,24,128]{2,1,0:T(8,128)S(1)} %get-tuple-element.61.fluid_pad, ...), custom_call_target="tpu_custom_call", output_to_operand_aliasing={{}: (10, {})} | custom-call | tf_op jit(solution)/shard_map/first_adjoint/pallas_call | solution.py:780
  43.2 0.8 %collective-permute-start.17 = (f32[32,128]{1,0:T(8,128)S(1)}, f32[32,128]{1,0:T(8,128)S(1)}, u32[]{:S(2)}, u32[]{:S(2)}) collective-permute-start(f32[32,128]{1,0:T(8,128)S(1)} %add_add_fusion.refs_0_), channel_id=1, source_target_pairs={{0,24},{1,25},{2,26},{3,27},{4,28},{5,29},{6,30},{7,31},{8,16},{9,... | collective-permute-start | bytes 49160 | tf_op jit(solution)/shard_map/ppermute | solution.py:836
  44.0 1.6 %collective-permute-start.16 = (f32[32,128]{1,0:T(8,128)S(1)}, f32[32,128]{1,0:T(8,128)S(1)}, u32[]{:S(2)}, u32[]{:S(2)}) collective-permute-start(f32[32,128]{1,0:T(8,128)S(1)} %add_add_fusion.refs_0_), channel_id=1, source_target_pairs={{0,28},{1,29},{2,30},{3,31},{4,24},{5,25},{6,26},{7,27},{8,20},{9,... | collective-permute-start | bytes 49160 | tf_op jit(solution)/shard_map/ppermute | solution.py:836
  46.3 1.4 %first_adjoint.5 = f32[19,16,8,128]{3,2,1,0:T(8,128)} custom-call(f32[3,16,8,128]{3,2,1,0:T(8,128)S(1)} %first_speed.1.speed, f32[16,8,128]{2,1,0:T(8,128)S(1)} %copy-done.3, f32[19,16,8,128]{3,2,1,0:T(8,128)S(1)} %get-tuple-element.58.adj, f32[18,24,128]{2,1,0:T(8,128)S(1)} %get-tuple-element.61.fluid_pad, ...), custom_call_target="tpu_custom_call", output_to_operand_aliasing={{}: (10, {})} | custom-call | tf_op jit(solution)/shard_map/first_adjoint/pallas_call | solution.py:780
  (47 shorter events, 6.9 us)
Async XLA Ops:
  0.6 8.6 %copy-start.2 = (s32[16,8,128]{2,1,0:T(8,128)S(1)}, s32[16,8,128]{2,1,0:T(8,128)}, u32[]{:S(2)}) copy-start(s32[16,8,128]{2,1,0:T(8,128)} %fluid.5) | copy-start | bytes 196612
  0.6 8.6 %copy-start.3 = (f32[16,8,128]{2,1,0:T(8,128)S(1)}, f32[16,8,128]{2,1,0:T(8,128)}, u32[]{:S(2)}) copy-start(f32[16,8,128]{2,1,0:T(8,128)} %phase.9) | copy-start | bytes 196612
  0.7 8.6 %copy-start.5 = (f32[16,8,128]{2,1,0:T(8,128)S(1)}, f32[16,8,128]{2,1,0:T(8,128)}, u32[]{:S(2)}) copy-start(f32[16,8,128]{2,1,0:T(8,128)} %phase.6) | copy-start | bytes 196612
  0.7 8.6 %copy-start.7 = (s32[16,8,128]{2,1,0:T(8,128)S(1)}, s32[16,8,128]{2,1,0:T(8,128)}, u32[]{:S(2)}) copy-start(s32[16,8,128]{2,1,0:T(8,128)} %refs_4_.1) | copy-start | bytes 196612
  0.7 8.6 %copy-start.6 = (s32[16,8,128]{2,1,0:T(8,128)S(1)}, s32[16,8,128]{2,1,0:T(8,128)}, u32[]{:S(2)}) copy-start(s32[16,8,128]{2,1,0:T(8,128)} %refs_3_.1) | copy-start | bytes 196612
  2.4 14.6 %copy-start = (f32[19,16,8,128]{3,2,1,0:T(8,128)S(1)}, f32[19,16,8,128]{3,2,1,0:T(8,128)}, u32[]{:S(2)}) copy-start(f32[19,16,8,128]{3,2,1,0:T(8,128)} %adj.3) | copy-start | bytes 3735556
  2.4 9.9 %collective-permute-start = (f32[240,128]{1,0:T(8,128)S(1)}, f32[240,128]{1,0:T(8,128)S(1)}, u32[]{:S(2)}, u32[]{:S(2)}) collective-permute-start(f32[240,128]{1,0:T(8,128)S(1)} %get-tuple-element.48), channel_id=1, source_target_pairs={{0,15},{1,2},{2,1},{3,4},{4,3},{5,6},{6,5},{7,8},{8,7},{9,10},{10,... | collective-permute-start | bytes 368648 | tf_op jit(solution)/shard_map/ppermute | solution.py:799
  9.3 3.9 %collective-permute-start.1 = (f32[240,128]{1,0:T(8,128)S(1)}, f32[240,128]{1,0:T(8,128)S(1)}, u32[]{:S(2)}, u32[]{:S(2)}) collective-permute-start(f32[240,128]{1,0:T(8,128)S(1)} %get-tuple-element.49), channel_id=1, source_target_pairs={{0,1},{1,0},{2,3},{3,2},{4,5},{5,4},{6,7},{7,6},{8,9},{9,8},{10,11... | collective-permute-start | bytes 368648 | tf_op jit(solution)/shard_map/ppermute | solution.py:798
  13.2 4.5 %collective-permute-start.2 = (f32[22,8,128]{2,1,0:T(8,128)S(1)}, f32[22,8,128]{2,1,0:T(8,128)S(1)}, u32[]{:S(2)}, u32[]{:S(2)}) collective-permute-start(f32[22,8,128]{2,1,0:T(8,128)S(1)} %get-tuple-element.53), channel_id=1, source_target_pairs={{0,16},{16,0},{32,48},{48,32},{64,80},{80,64},{96,112},{112,96},{1... | collective-permute-start | bytes 270344 | tf_op jit(solution)/shard_map/ppermute | solution.py:798
  15.2 4.2 %collective-permute-start.3 = (f32[22,8,128]{2,1,0:T(8,128)S(1)}, f32[22,8,128]{2,1,0:T(8,128)S(1)}, u32[]{:S(2)}, u32[]{:S(2)}) collective-permute-start(f32[22,8,128]{2,1,0:T(8,128)S(1)} %get-tuple-element.54), channel_id=1, source_target_pairs={{0,112},{16,32},{32,16},{48,64},{64,48},{80,96},{96,80},{112,0},{1... | collective-permute-start | bytes 270344 | tf_op jit(solution)/shard_map/ppermute | solution.py:799
  19.8 5.6 %collective-permute-start.4 = (f32[80,128]{1,0:T(8,128)S(1)}, f32[80,128]{1,0:T(8,128)S(1)}, u32[]{:S(2)}, u32[]{:S(2)}) collective-permute-start(f32[80,128]{1,0:T(8,128)S(1)} %get-tuple-element.64), channel_id=1, source_target_pairs={{0,1},{1,0},{2,3},{3,2},{4,5},{5,4},{6,7},{7,6},{8,9},{9,8},{10,11... | collective-permute-start | bytes 122888 | tf_op jit(solution)/shard_map/ppermute | solution.py:798
  19.9 6.3 %collective-permute-start.5 = (f32[80,128]{1,0:T(8,128)S(1)}, f32[80,128]{1,0:T(8,128)S(1)}, u32[]{:S(2)}, u32[]{:S(2)}) collective-permute-start(f32[80,128]{1,0:T(8,128)S(1)} %get-tuple-element.65), channel_id=1, source_target_pairs={{0,15},{1,2},{2,1},{3,4},{4,3},{5,6},{6,5},{7,8},{8,7},{9,10},{10,... | collective-permute-start | bytes 122888 | tf_op jit(solution)/shard_map/ppermute | solution.py:799
  23.2 4.6 %collective-permute-start.6 = (f32[5,8,128]{2,1,0:T(8,128)S(1)}, f32[5,8,128]{2,1,0:T(8,128)S(1)}, u32[]{:S(2)}, u32[]{:S(2)}) collective-permute-start(f32[5,8,128]{2,1,0:T(8,128)S(1)} %get-tuple-element.66), channel_id=1, source_target_pairs={{0,16},{16,0},{32,48},{48,32},{64,80},{80,64},{96,112},{112,96},{1... | collective-permute-start | bytes 61448 | tf_op jit(solution)/shard_map/ppermute | solution.py:798
  24.5 3.5 %collective-permute-start.7 = (f32[5,8,128]{2,1,0:T(8,128)S(1)}, f32[5,8,128]{2,1,0:T(8,128)S(1)}, u32[]{:S(2)}, u32[]{:S(2)}) collective-permute-start(f32[5,8,128]{2,1,0:T(8,128)S(1)} %get-tuple-element.67), channel_id=1, source_target_pairs={{0,112},{16,32},{32,16},{48,64},{64,48},{80,96},{96,80},{112,0},{1... | collective-permute-start | bytes 61448 | tf_op jit(solution)/shard_map/ppermute | solution.py:799
  29.2 3.0 %collective-permute-start.8 = (f32[32,128]{1,0:T(8,128)S(1)}, f32[32,128]{1,0:T(8,128)S(1)}, u32[]{:S(2)}, u32[]{:S(2)}) collective-permute-start(f32[32,128]{1,0:T(8,128)S(1)} %first_outer.1._), channel_id=1, source_target_pairs={{0,16},{1,17},{2,18},{3,19},{4,20},{5,21},{6,22},{7,23},{8,24},{9,... | collective-permute-start | bytes 49160 | tf_op jit(solution)/shard_map/ppermute | solution.py:836
  32.2 5.2 %collective-permute-start.11 = (f32[32,128]{1,0:T(8,128)S(1)}, f32[32,128]{1,0:T(8,128)S(1)}, u32[]{:S(2)}, u32[]{:S(2)}) collective-permute-start(f32[32,128]{1,0:T(8,128)S(1)} %add.30.refs_0_), channel_id=1, source_target_pairs={{0,80},{1,81},{2,82},{3,83},{4,84},{5,85},{6,86},{7,87},{8,88},{9,... | collective-permute-start | bytes 49160 | tf_op jit(solution)/shard_map/ppermute | solution.py:836
  34.1 4.4 %collective-permute-start.10 = (f32[32,128]{1,0:T(8,128)S(1)}, f32[32,128]{1,0:T(8,128)S(1)}, u32[]{:S(2)}, u32[]{:S(2)}) collective-permute-start(f32[32,128]{1,0:T(8,128)S(1)} %add.30.refs_0_), channel_id=1, source_target_pairs={{0,112},{1,113},{2,114},{3,115},{4,116},{5,117},{6,118},{7,119},{8... | collective-permute-start | bytes 49160 | tf_op jit(solution)/shard_map/ppermute | solution.py:836
  34.9 3.6 %collective-permute-start.9 = (f32[32,128]{1,0:T(8,128)S(1)}, f32[32,128]{1,0:T(8,128)S(1)}, u32[]{:S(2)}, u32[]{:S(2)}) collective-permute-start(f32[32,128]{1,0:T(8,128)S(1)} %add.30.refs_0_), channel_id=1, source_target_pairs={{0,48},{1,49},{2,50},{3,51},{4,52},{5,53},{6,54},{7,55},{8,56},{9,... | collective-permute-start | bytes 49160 | tf_op jit(solution)/shard_map/ppermute | solution.py:836
  38.4 4.7 %collective-permute-start.14 = (f32[32,128]{1,0:T(8,128)S(1)}, f32[32,128]{1,0:T(8,128)S(1)}, u32[]{:S(2)}, u32[]{:S(2)}) collective-permute-start(f32[32,128]{1,0:T(8,128)S(1)} %add_add_fusion.1.refs_0_), channel_id=1, source_target_pairs={{0,18},{1,19},{2,16},{3,17},{4,22},{5,23},{6,20},{7,21},{8,26},{9,... | collective-permute-start | bytes 49160 | tf_op jit(solution)/shard_map/ppermute | solution.py:836
  38.5 4.7 %collective-permute-start.13 = (f32[32,128]{1,0:T(8,128)S(1)}, f32[32,128]{1,0:T(8,128)S(1)}, u32[]{:S(2)}, u32[]{:S(2)}) collective-permute-start(f32[32,128]{1,0:T(8,128)S(1)} %add_add_fusion.1.refs_0_), channel_id=1, source_target_pairs={{0,19},{1,18},{2,17},{3,16},{4,23},{5,22},{6,21},{7,20},{8,27},{9,... | collective-permute-start | bytes 49160 | tf_op jit(solution)/shard_map/ppermute | solution.py:836
  39.4 3.8 %collective-permute-start.12 = (f32[32,128]{1,0:T(8,128)S(1)}, f32[32,128]{1,0:T(8,128)S(1)}, u32[]{:S(2)}, u32[]{:S(2)}) collective-permute-start(f32[32,128]{1,0:T(8,128)S(1)} %add_add_fusion.1.refs_0_), channel_id=1, source_target_pairs={{0,17},{1,16},{2,19},{3,18},{4,21},{5,20},{6,23},{7,22},{8,25},{9,... | collective-permute-start | bytes 49160 | tf_op jit(solution)/shard_map/ppermute | solution.py:836
  43.2 4.8 %collective-permute-start.17 = (f32[32,128]{1,0:T(8,128)S(1)}, f32[32,128]{1,0:T(8,128)S(1)}, u32[]{:S(2)}, u32[]{:S(2)}) collective-permute-start(f32[32,128]{1,0:T(8,128)S(1)} %add_add_fusion.refs_0_), channel_id=1, source_target_pairs={{0,24},{1,25},{2,26},{3,27},{4,28},{5,29},{6,30},{7,31},{8,16},{9,... | collective-permute-start | bytes 49160 | tf_op jit(solution)/shard_map/ppermute | solution.py:836
  44.0 4.4 %collective-permute-start.16 = (f32[32,128]{1,0:T(8,128)S(1)}, f32[32,128]{1,0:T(8,128)S(1)}, u32[]{:S(2)}, u32[]{:S(2)}) collective-permute-start(f32[32,128]{1,0:T(8,128)S(1)} %add_add_fusion.refs_0_), channel_id=1, source_target_pairs={{0,28},{1,29},{2,30},{3,31},{4,24},{5,25},{6,26},{7,27},{8,20},{9,... | collective-permute-start | bytes 49160 | tf_op jit(solution)/shard_map/ppermute | solution.py:836
  45.6 3.2 %collective-permute-start.15 = (f32[32,128]{1,0:T(8,128)S(1)}, f32[32,128]{1,0:T(8,128)S(1)}, u32[]{:S(2)}, u32[]{:S(2)}) collective-permute-start(f32[32,128]{1,0:T(8,128)S(1)} %add_add_fusion.refs_0_), channel_id=1, source_target_pairs={{0,20},{1,21},{2,22},{3,23},{4,16},{5,17},{6,18},{7,19},{8,28},{9,... | collective-permute-start | bytes 49160 | tf_op jit(solution)/shard_map/ppermute | solution.py:836
  (3 other events, 24.6 us)
